TPU v7x, 128 devices: a whole 4x4x4 slice. The times are simulated.
128 devices in a mesh: gx: 16 (over x, y), gy: 8 (over z, core).
Axes of the slice: x: 4, y: 4, z: 4, core: 2. Of those that a mesh axis runs over, the one named last changes fastest.
Arguments:
- tokens: bfloat16 [64, 1024, 256], P('gx', 'gy'), may hold values from -6 to 6
- lengths: int32 [64], P('gx'), may hold values from 513 to 1024, as said below
- w_in: bfloat16 [256, 768], P(('gx', 'gy')), may hold values from -0.375 to 0.375
- b_q: bfloat16 [256], P(('gx', 'gy')), may hold values from -3 to 3
- b_v: bfloat16 [256], P(('gx', 'gy')), may hold values from -3 to 3
- w_out: bfloat16 [256, 256], P(('gx', 'gy')), may hold values from -3 to 3
- b_out: bfloat16 [256], P(('gx', 'gy')), may hold values from -3 to 3
- gain_first: bfloat16 [256], P(('gx', 'gy')), may hold values from 0.099609375 to 1.8984375
- shift_first: bfloat16 [256], P(('gx', 'gy')), may hold values from -3 to 3
- w_up: bfloat16 [256, 2048], P(('gx', 'gy')), may hold values from -0.375 to 0.375
- b_up: bfloat16 [2048], P(('gx', 'gy')), may hold values from -3 to 3
- w_down: bfloat16 [2048, 256], P(('gx', 'gy')), may hold values from -0.1875 to 0.1875
- b_down: bfloat16 [256], P(('gx', 'gy')), may hold values from -3 to 3
- gain_second: bfloat16 [256], P(('gx', 'gy')), may hold values from 0.099609375 to 1.8984375
- shift_second: bfloat16 [256], P(('gx', 'gy')), may hold values from -3 to 3
- cotangent: bfloat16 [64, 1024, 256], P('gx', 'gy'), may hold values from -6 to 6
Outputs:
- layer_out: bfloat16 [64, 1024, 256], P('gx', 'gy')
- grad_tokens: float32 [64, 1024, 256], P('gx', 'gy')
- grad_w_in: float32 [256, 768], P(('gx', 'gy'))
- grad_b_q: float32 [256], P(('gx', 'gy'))
- grad_b_v: float32 [256], P(('gx', 'gy'))
- grad_w_out: float32 [256, 256], P(('gx', 'gy'))
- grad_b_out: float32 [256], P(('gx', 'gy'))
- grad_gain_first: float32 [256], P(('gx', 'gy'))
- grad_shift_first: float32 [256], P(('gx', 'gy'))
- grad_w_up: float32 [256, 2048], P(('gx', 'gy'))
- grad_b_up: float32 [2048], P(('gx', 'gy'))
- grad_w_down: float32 [2048, 256], P(('gx', 'gy'))
- grad_b_down: float32 [256], P(('gx', 'gy'))
- grad_gain_second: float32 [256], P(('gx', 'gy'))
- grad_shift_second: float32 [256], P(('gx', 'gy'))
Inputs may be any that keep to these rules, and one draw needn't show every extreme that they name: `lengths`: each image's number of real tokens; among the 4 images of each index of gx one has more than 896; at least one image of all has 1024.
All inputs are finite; a program needn't handle non-finite values.
Results may differ from a plain program's by a relative error of at most 0.02.
Values may be sent and summed in bfloat16 or wider, within the bound.
A program may use at most 128 MiB of HBM per device.

v0:
```python
import math

import jax
import jax.numpy as jnp
from jax import lax
from jax.sharding import PartitionSpec as P

D = 256
H = 8
HD = 32


EPSILON = 1e-05
GELU_SCALE = math.sqrt(2.0 / math.pi)


def layer_norm(values, gain_vec, shift_vec):
    centre = jnp.mean(values, axis=-1, keepdims=True)
    shifted = values - centre
    spread = jnp.mean(shifted * shifted, axis=-1, keepdims=True)
    return shifted * lax.rsqrt(spread + EPSILON) * gain_vec + shift_vec


def gelu_tanh(values):
    return (
        0.5 * values * (1.0 + jnp.tanh(GELU_SCALE * (values + 0.044715 * values * values * values)))
    )


def sine_table(place, model_width):
    column = jnp.arange(model_width, dtype=jnp.int32)
    frequency = jnp.power(10000.0, -(2 * (column // 2)).astype(jnp.float32) / model_width)
    phase_angle = place.astype(jnp.float32)[:, None] * frequency[None, :]
    return jnp.where(column % 2 == 0, jnp.sin(phase_angle), jnp.cos(phase_angle))


def split_heads(array):
    return array.reshape(array.shape[0], array.shape[1], H, HD)


def projections(gathered, tokens, position):
    w_in, b_q, b_v = (gathered[0], gathered[1], gathered[2])
    shifted = (tokens.astype(jnp.float32) + position[None]).astype(jnp.bfloat16)
    query_rows = jnp.einsum("isd,de->ise", shifted, w_in[:, :D], preferred_element_type=jnp.float32)
    query_rows = (query_rows + b_q.astype(jnp.float32)).astype(jnp.bfloat16)
    key_rows = jnp.einsum(
        "isd,de->ise", shifted, w_in[:, D : 2 * D], preferred_element_type=jnp.float32
    ).astype(jnp.bfloat16)
    value_rows = jnp.einsum(
        "isd,de->ise", tokens, w_in[:, 2 * D :], preferred_element_type=jnp.float32
    )
    value_rows = (value_rows + b_v.astype(jnp.float32)).astype(jnp.bfloat16)
    return (shifted, query_rows, key_rows, value_rows)


def attention(query_rows, all_keys, all_values, lengths):
    score_scale = 1.0 / math.sqrt(HD)
    scores = (
        jnp.einsum(
            "iqhd,ikhd->ihqk",
            split_heads(query_rows),
            split_heads(all_keys),
            preferred_element_type=jnp.float32,
        )
        * score_scale
    )
    key_index = jnp.arange(all_keys.shape[1], dtype=jnp.int32)
    is_valid = (key_index[None, :] < lengths[:, None])[:, None, None, :]
    scores = jnp.where(is_valid, scores, -1e30)
    row_peak = jnp.max(scores, axis=-1, keepdims=True)
    exponent = jnp.exp(scores - row_peak)
    row_total = jnp.sum(exponent, axis=-1, keepdims=True)
    attn_probs = exponent / row_total
    probs_low = attn_probs.astype(jnp.bfloat16)
    attn_mixed = jnp.einsum(
        "ihqk,ikhd->iqhd", probs_low, split_heads(all_values), preferred_element_type=jnp.float32
    )
    attn_mixed = attn_mixed.reshape(query_rows.shape).astype(jnp.bfloat16)
    return (attn_probs, probs_low, row_peak, row_total, attn_mixed)


def remainder(gathered, tokens, attn_mixed):
    w_out, b_out, gain_first, shift_first, w_up, b_up, w_down, b_down, gain_second, shift_second = (
        gathered[3:]
    )
    branch = jnp.einsum("isd,de->ise", attn_mixed, w_out, preferred_element_type=jnp.float32)
    first_sum = tokens.astype(jnp.float32) + branch + b_out.astype(jnp.float32)
    hidden = layer_norm(first_sum, gain_first.astype(jnp.float32), shift_first.astype(jnp.float32))
    hidden_low = hidden.astype(jnp.bfloat16)
    up_proj = jnp.einsum("isd,df->isf", hidden_low, w_up, preferred_element_type=jnp.float32)
    up_proj = up_proj + b_up.astype(jnp.float32)
    active_low = gelu_tanh(up_proj).astype(jnp.bfloat16)
    second_sum = hidden + jnp.einsum(
        "isf,fd->isd", active_low, w_down, preferred_element_type=jnp.float32
    )
    second_sum = second_sum + b_down.astype(jnp.float32)
    output = layer_norm(
        second_sum, gain_second.astype(jnp.float32), shift_second.astype(jnp.float32)
    )
    return (first_sum, hidden_low, up_proj, active_low, second_sum, output)


def body(
    tokens,
    lengths,
    w_in,
    b_q,
    b_v,
    w_out,
    b_out,
    gain_first,
    shift_first,
    w_up,
    b_up,
    w_down,
    b_down,
    gain_second,
    shift_second,
    cotangent,
):
    pieces = (
        w_in,
        b_q,
        b_v,
        w_out,
        b_out,
        gain_first,
        shift_first,
        w_up,
        b_up,
        w_down,
        b_down,
        gain_second,
        shift_second,
    )
    gathered = (
        lax.all_gather(pieces[0], ("gx", "gy"), axis=0, tiled=True),
        lax.all_gather(pieces[1], ("gx", "gy"), axis=0, tiled=True),
        lax.all_gather(pieces[2], ("gx", "gy"), axis=0, tiled=True),
        lax.all_gather(pieces[3], ("gx", "gy"), axis=0, tiled=True),
        lax.all_gather(pieces[4], ("gx", "gy"), axis=0, tiled=True),
        lax.all_gather(pieces[5], ("gx", "gy"), axis=0, tiled=True),
        lax.all_gather(pieces[6], ("gx", "gy"), axis=0, tiled=True),
        lax.all_gather(pieces[7], ("gx", "gy"), axis=0, tiled=True),
        lax.all_gather(pieces[8], ("gx", "gy"), axis=0, tiled=True),
        lax.all_gather(pieces[9], ("gx", "gy"), axis=0, tiled=True),
        lax.all_gather(pieces[10], ("gx", "gy"), axis=0, tiled=True),
        lax.all_gather(pieces[11], ("gx", "gy"), axis=0, tiled=True),
        lax.all_gather(pieces[12], ("gx", "gy"), axis=0, tiled=True),
    )
    seg_rows = tokens.shape[1]
    key_place = lax.axis_index("gy") * seg_rows + jnp.arange(seg_rows, dtype=jnp.int32)
    position = sine_table(key_place, tokens.shape[2])
    shifted, query_rows, key_rows, value_rows = projections(gathered, tokens, position)
    all_keys, all_values = (
        lax.all_gather(key_rows, "gy", axis=1, tiled=True),
        lax.all_gather(value_rows, "gy", axis=1, tiled=True),
    )
    attn_mixed = attention(query_rows, all_keys, all_values, lengths)[4]
    layer_out = remainder(gathered, tokens, attn_mixed)[5].astype(jnp.bfloat16)
    regathered = (
        lax.all_gather(pieces[0], ("gx", "gy"), axis=0, tiled=True),
        lax.all_gather(pieces[1], ("gx", "gy"), axis=0, tiled=True),
        lax.all_gather(pieces[2], ("gx", "gy"), axis=0, tiled=True),
        lax.all_gather(pieces[3], ("gx", "gy"), axis=0, tiled=True),
        lax.all_gather(pieces[4], ("gx", "gy"), axis=0, tiled=True),
        lax.all_gather(pieces[5], ("gx", "gy"), axis=0, tiled=True),
        lax.all_gather(pieces[6], ("gx", "gy"), axis=0, tiled=True),
        lax.all_gather(pieces[7], ("gx", "gy"), axis=0, tiled=True),
        lax.all_gather(pieces[8], ("gx", "gy"), axis=0, tiled=True),
        lax.all_gather(pieces[9], ("gx", "gy"), axis=0, tiled=True),
        lax.all_gather(pieces[10], ("gx", "gy"), axis=0, tiled=True),
        lax.all_gather(pieces[11], ("gx", "gy"), axis=0, tiled=True),
        lax.all_gather(pieces[12], ("gx", "gy"), axis=0, tiled=True),
    )
    shifted, query_rows, key_rows, value_rows = projections(regathered, tokens, position)
    all_keys, all_values = (
        lax.all_gather(key_rows, "gy", axis=1, tiled=True),
        lax.all_gather(value_rows, "gy", axis=1, tiled=True),
    )
    attn_probs, probs_low, row_peak, row_total, attn_mixed = attention(
        query_rows, all_keys, all_values, lengths
    )
    first_sum, hidden_low, up_proj, active_low, second_sum, output = remainder(
        regathered, tokens, attn_mixed
    )
    (
        w_full,
        bq_full,
        bv_full,
        wout_full,
        bout_full,
        gain_one,
        shift_one,
        wup_full,
        bup_full,
        wdown_full,
        bdown_full,
        gain_two,
        shift_two,
    ) = regathered
    score_scale = 1.0 / math.sqrt(HD)
    _, pull_second = jax.vjp(
        layer_norm, second_sum, gain_two.astype(jnp.float32), shift_two.astype(jnp.float32)
    )
    d_second, g_gain_second, g_shift_second = pull_second(cotangent.astype(jnp.float32))
    d_ffn = d_second.astype(jnp.bfloat16)
    g_w_down = jnp.einsum("isf,isd->fd", active_low, d_ffn, preferred_element_type=jnp.float32)
    g_b_down = jnp.sum(d_ffn.astype(jnp.float32), axis=(0, 1))
    d_active = jnp.einsum("isd,fd->isf", d_ffn, wdown_full, preferred_element_type=jnp.float32)
    _, pull_gelu = jax.vjp(gelu_tanh, up_proj)
    d_up = pull_gelu(d_active)[0].astype(jnp.bfloat16)
    g_w_up = jnp.einsum("isd,isf->df", hidden_low, d_up, preferred_element_type=jnp.float32)
    g_b_up = jnp.sum(d_up.astype(jnp.float32), axis=(0, 1))
    d_hidden = (
        jnp.einsum("isf,df->isd", d_up, wup_full, preferred_element_type=jnp.float32) + d_second
    )
    _, pull_first = jax.vjp(
        layer_norm, first_sum, gain_one.astype(jnp.float32), shift_one.astype(jnp.float32)
    )
    d_first, g_gain_first, g_shift_first = pull_first(d_hidden)
    d_branch = d_first.astype(jnp.bfloat16)
    g_w_out = jnp.einsum("isd,ise->de", attn_mixed, d_branch, preferred_element_type=jnp.float32)
    g_b_out = jnp.sum(d_branch.astype(jnp.float32), axis=(0, 1))
    d_mixed = jnp.einsum("ise,de->isd", d_branch, wout_full, preferred_element_type=jnp.float32)
    d_mixed = d_mixed.astype(jnp.bfloat16)
    d_probs = jnp.einsum(
        "iqhd,ikhd->ihqk",
        split_heads(d_mixed),
        split_heads(all_values),
        preferred_element_type=jnp.float32,
    )
    inner_sum = jnp.sum(attn_probs * d_probs, axis=-1, keepdims=True)
    d_scores = (attn_probs * (d_probs - inner_sum)).astype(jnp.bfloat16)
    d_queries = (
        jnp.einsum(
            "ihqk,ikhd->iqhd", d_scores, split_heads(all_keys), preferred_element_type=jnp.float32
        )
        * score_scale
    )
    d_queries = d_queries.reshape(query_rows.shape).astype(jnp.bfloat16)
    key_terms = (
        jnp.einsum(
            "ihqk,iqhd->ikhd", d_scores, split_heads(query_rows), preferred_element_type=jnp.float32
        )
        * score_scale
    )
    value_terms = jnp.einsum(
        "ihqk,iqhd->ikhd", probs_low, split_heads(d_mixed), preferred_element_type=jnp.float32
    )
    d_keys, d_values = (
        lax.psum_scatter(
            key_terms.reshape(all_keys.shape).astype(jnp.bfloat16),
            "gy",
            scatter_dimension=1,
            tiled=True,
        ).astype(jnp.float32),
        lax.psum_scatter(
            value_terms.reshape(all_keys.shape).astype(jnp.bfloat16),
            "gy",
            scatter_dimension=1,
            tiled=True,
        ).astype(jnp.float32),
    )
    d_keys = d_keys.astype(jnp.bfloat16)
    d_values = d_values.astype(jnp.bfloat16)
    d_query_key = jnp.concatenate([d_queries, d_keys], axis=2)
    g_w_in = jnp.concatenate(
        [
            jnp.einsum("isd,ise->de", shifted, d_query_key, preferred_element_type=jnp.float32),
            jnp.einsum("isd,ise->de", tokens, d_values, preferred_element_type=jnp.float32),
        ],
        axis=1,
    )
    g_b_q = jnp.sum(d_queries.astype(jnp.float32), axis=(0, 1))
    g_b_v = jnp.sum(d_values.astype(jnp.float32), axis=(0, 1))
    d_all = jnp.concatenate([d_query_key, d_values], axis=2)
    grad_tokens = d_first + jnp.einsum(
        "ise,de->isd", d_all, w_full, preferred_element_type=jnp.float32
    )
    grad_terms = (
        g_w_in,
        g_b_q,
        g_b_v,
        g_w_out,
        g_b_out,
        g_gain_first,
        g_shift_first,
        g_w_up,
        g_b_up,
        g_w_down,
        g_b_down,
        g_gain_second,
        g_shift_second,
    )
    shards = (
        lax.psum_scatter(grad_terms[0], ("gx", "gy"), scatter_dimension=0, tiled=True),
        lax.psum_scatter(grad_terms[1], ("gx", "gy"), scatter_dimension=0, tiled=True),
        lax.psum_scatter(grad_terms[2], ("gx", "gy"), scatter_dimension=0, tiled=True),
        lax.psum_scatter(grad_terms[3], ("gx", "gy"), scatter_dimension=0, tiled=True),
        lax.psum_scatter(grad_terms[4], ("gx", "gy"), scatter_dimension=0, tiled=True),
        lax.psum_scatter(grad_terms[5], ("gx", "gy"), scatter_dimension=0, tiled=True),
        lax.psum_scatter(grad_terms[6], ("gx", "gy"), scatter_dimension=0, tiled=True),
        lax.psum_scatter(grad_terms[7], ("gx", "gy"), scatter_dimension=0, tiled=True),
        lax.psum_scatter(grad_terms[8], ("gx", "gy"), scatter_dimension=0, tiled=True),
        lax.psum_scatter(grad_terms[9], ("gx", "gy"), scatter_dimension=0, tiled=True),
        lax.psum_scatter(grad_terms[10], ("gx", "gy"), scatter_dimension=0, tiled=True),
        lax.psum_scatter(grad_terms[11], ("gx", "gy"), scatter_dimension=0, tiled=True),
        lax.psum_scatter(grad_terms[12], ("gx", "gy"), scatter_dimension=0, tiled=True),
    )
    return (
        layer_out,
        grad_tokens,
        shards[0],
        shards[1],
        shards[2],
        shards[3],
        shards[4],
        shards[5],
        shards[6],
        shards[7],
        shards[8],
        shards[9],
        shards[10],
        shards[11],
        shards[12],
    )


def solution(mesh):
    placed = (
        P("gx", "gy", None),
        P("gx"),
        P(("gx", "gy"), None),
        P(("gx", "gy")),
        P(("gx", "gy")),
        P(("gx", "gy"), None),
        P(("gx", "gy")),
        P(("gx", "gy")),
        P(("gx", "gy")),
        P(("gx", "gy"), None),
        P(("gx", "gy")),
        P(("gx", "gy"), None),
        P(("gx", "gy")),
        P(("gx", "gy")),
        P(("gx", "gy")),
        P("gx", "gy", None),
    )
    return jax.shard_map(
        body,
        mesh=mesh,
        in_specs=placed,
        out_specs=(
            P("gx", "gy", None),
            P("gx", "gy", None),
            P(("gx", "gy"), None),
            P(("gx", "gy")),
            P(("gx", "gy")),
            P(("gx", "gy"), None),
            P(("gx", "gy")),
            P(("gx", "gy")),
            P(("gx", "gy")),
            P(("gx", "gy"), None),
            P(("gx", "gy")),
            P(("gx", "gy"), None),
            P(("gx", "gy")),
            P(("gx", "gy")),
            P(("gx", "gy")),
        ),
        check_vma=False,
    )
```

profile of v0, /device:TPU:1, one launch (start us, length us, event | category | flops | bytes accessed | tf_op | source)
XLA Modules:
  0.0 1106.3 jit_solution(8154909090863409346)
XLA Ops:
  7.2 0.7 all-gather.14.cloned.1.call-update
  8.0 38.9 %all-gather = bf16[128,2,768]{2,1,0:T(2,128)(2,1)S(1)} all-gather(bf16[1,2,768]{2,1,0:T(2,128)(2,1)} %bitcast.93), channel_id=1, replica_groups=mesh['gx'=16,'gy'=8] {'gx','gy'}, dimensions={0}, use_global_device_ids=true | all-gather | bytes 396288 | tf_op jit(solution)/shard_map/all_gather | solution.py:137
  47.6 1.9 convolution_convert_fusion.1
  49.6 0.9 dynamic-update-slice.8
  50.5 0.8 dynamic-update-slice.6
  51.3 0.8 dynamic-update-slice.3
  52.2 0.8 dynamic-update-slice.4
  53.0 0.8 dynamic-update-slice.2
  53.9 0.8 dynamic-update-slice.1
  54.7 0.8 dynamic-update-slice
  55.5 0.8 dynamic-update-slice.7
  56.4 0.8 dynamic-update-slice.5
  57.2 64.4 %all-reduce.23 = (bf16[256]{0:T(256)(128)(2,1)S(1)}, bf16[256]{0:T(256)(128)(2,1)S(1)}, bf16[256]{0:T(256)(128)(2,1)S(1)}, bf16[256]{0:T(256)(128)(2,1)S(1)}, bf...) all-reduce(bf16[256]{0:T(256)(128)(2,1)S(1)} %dynamic-update-slice,, ...), channel_id=1, replica_groups=mesh['gx'=16,'gy'=8] {'gx','gy'}, use_global_device_ids=true, to_apply=%add | all-reduce | flops 4096 | bytes 16384
  121.6 1.9 fusion.26
  124.1 0.7 iota_compare_fusion
  126.0 0.6 convert_element_type.186
  126.6 33.6 %all-gather.1 = bf16[128,2,256]{2,1,0:T(2,128)(2,1)S(1)} all-gather(bf16[1,2,256]{2,1,0:T(2,128)(2,1)} %bitcast.94), channel_id=1, replica_groups=mesh['gx'=16,'gy'=8] {'gx','gy'}, dimensions={0}, use_global_device_ids=true | all-gather | bytes 132096 | tf_op jit(solution)/shard_map/all_gather | solution.py:140
  160.3 1.2 fusion.27
  161.7 2.4 reshape.246
  164.2 3.0 copy.65
  167.2 9.3 fusion.66
  176.4 4.0 copy.63
  180.4 9.5 fusion.23
  190.7 3.7 multiply_convert_fusion.2
  194.5 18.0 %all-gather.12.cloned.1.call-done = bf16[2048,256]{1,0:T(8,128)(2,1)} async-done(((bf16[16,256]{1,0:T(8,128)(2,1)}), bf16[2048,256]{1,0:T(8,128)(2,1)}) %all-gather.12.cloned.1.call-update) | async-done | bytes 1048592 | tf_op jit(solution)/shard_map/all_gather | solution.py:146
  212.5 2.9 fusion.68
  215.4 0.9 fusion.37
  216.3 0.9 fusion.39
  217.2 1.6 convert_reduce_fusion.2
  218.8 4.7 convert_reduce_fusion
  223.5 1.5 multiply_reduce_fusion.1
  225.4 0.7 convert_reduce_fusion.3
  226.2 1.0 convolution_convert_fusion
  227.2 1.8 copy.67
  229.0 8.4 fusion.15
  237.4 3.9 copy.69
  241.4 15.2 %multiply_reduce_fusion = (f32[4,8,128]{2,1,0:T(8,128)S(1)}, f32[4,8,128,1024]{3,2,1,0:T(8,128)}) fusion(f32[4,8,128,1024]{3,2,1,0:T(8,128)} %get-tuple-element.54, f32[4,8,128]{2,1,0:T(8,128)} %copy-done.18, bf16[4,128,8,32]{1,3,2,0:T(8,128)(2,1)} %bitcast.91, bf16[4,1024,8,32]{1,3,2,0:T(8,128)(2,1)} %bitcast.83), kind=kOutput, calls=%fused_computation.2 | convolution fusion | flops 281014272 | bytes 35946496 | tf_op jit(solution)/shard_map/iqhd,ikhd->ihqk/dot_general | solution.py:227
  256.6 11.9 %multiply_convert_fusion = bf16[4,8,128,1024]{3,2,1,0:T(8,128)(2,1)S(1)} fusion(f32[4,8,128,1024]{3,2,1,0:T(8,128)} %get-tuple-element.63, f32[4,8,128]{2,1,0:T(8,128)S(1)} %get-tuple-element.62, f32[4,8,128,1024]{3,2,1,0:T(8,128)} %get-tuple-element.54, f32[4,8,128]{2,1,0:T(8,128)S(1)} %copy-done.19), kind=kLoop, calls=%fused_computation.1 | loop fusion | flops 16777216 | bytes 41975808 | tf_op jit(solution)/shard_map/convert_element_type | solution.py:234
  268.5 3.0 multiply_convert_fusion.1
  271.6 0.9 copy-done
  272.4 3.9 copy.68
  276.4 7.0 convert_reduce_fusion.5
  283.5 1.1 copy.70
  284.6 1.9 convolution_bitcast_fusion.3
  286.5 3.8 convolution_bitcast_fusion.1
  290.3 1.3 convolution_bitcast_fusion.4
  291.5 12.8 %reduce-scatter.4.cloned.1.call-done = bf16[4,128,256]{2,1,0:T(8,128)(2,1)} async-done(((bf16[4,1024,256]{2,1,0:T(8,128)(2,1)}), bf16[4,128,256]{2,1,0:T(8,128)(2,1)}) %reduce-scatter.4.cloned.1.call-update) | async-done | bytes 262160 | tf_op jit(solution)/shard_map/reduce_scatter | solution.py:252
  304.4 1.3 convolution_bitcast_fusion.2
  305.7 0.9 pad_maximum_fusion
  307.1 3.7 convolution_bitcast_fusion
  311.2 68.3 %all-reduce.21 = (f32[256]{0:T(256)S(1)}, f32[256]{0:T(256)S(1)}, f32[256]{0:T(256)S(1)}, f32[256]{0:T(256)S(1)}, f32[256]{0:T(256)S(1)}, /*index=5*/f32[2048]{0...) all-reduce(f32[256]{0:T(256)S(1)} %reduce_sum.189, ...), channel_id=5, replica_groups=mesh['gx'=16,'gy'=8] {'gx','gy'}, use_global_device_ids=true, to_apply=%region_15.16.clone | all-reduce | flops 4096 | bytes 32768
  379.5 0.6 dynamic-slice.1
  380.0 0.6 dynamic-slice.2
  380.6 0.6 dynamic-slice.4
  381.2 0.6 dynamic-slice.5
  381.8 0.6 dynamic-slice.6
  382.9 0.6 dynamic-slice.10
  384.1 0.6 dynamic-slice.8
  384.7 1.2 convolution_add_fusion
  385.9 79.0 %all-reduce.26.cloned.1.call-done = (f32[256,768]{1,0:T(8,128)}, f32[256,256]{1,0:T(8,128)}, f32[256,2048]{1,0:T(8,128)}) async-done(((f32[256,768]{1,0:T(8,128)}, f32[256,256]{1,0:T(8,128)}, f32[256,2048]{1,0:T(8,128)}), (f32[256,768]{1,0:T(8,128)}, f32[256,256]{1,0:T(8,128)}, f32[256,2048]{1,0:T(8,128)})) %all-reduce.26.cloned.1.call-update) | async-done | bytes 3145744
  464.9 1.3 constant_dynamic-slice_fusion.1
  466.2 1.3 constant_dynamic-slice_fusion.2
  467.6 1.5 constant_dynamic-slice_fusion
  469.0 630.5 %reduce-scatter.8.cloned.1.call-done = f32[16,256]{1,0:T(8,128)} async-done(((f32[2048,256]{1,0:T(8,128)}), f32[16,256]{1,0:T(8,128)}) %reduce-scatter.8.cloned.1.call-update) | async-done | bytes 16400 | tf_op jit(solution)/shard_map/reduce_scatter | solution.py:306
  (131 shorter events, 6.1 us)
Async XLA Ops:
  7.2 154.5 %all-gather.14.cloned.1.call-start = ((), (), s32[]{:S(2)}) async-start(), calls=%async_computation.9 | async-start | bytes 1056768 | tf_op jit(solution)/shard_map/all_gather | solution.py:144
  7.9 156.2 %all-gather.10.cloned.1.call-start = ((), (), s32[]{:S(2)}) async-start(), calls=%async_computation.4 | async-start | bytes 2359296 | tf_op jit(solution)/shard_map/all_gather | solution.py:156
  47.6 116.6 %copy-start.6 = (f32[128,256]{1,0:T(8,128)}, f32[128,256]{1,0:T(8,128)S(1)}, u32[]{:S(2)}) copy-start(f32[128,256]{1,0:T(8,128)S(1)} %fusion.44) | copy-start | bytes 393220
  49.5 126.9 %all-gather.8.cloned.1.call-start = ((), (), s32[]{:S(2)}) async-start(), calls=%async_computation.3 | async-start | bytes 2359296 | tf_op jit(solution)/shard_map/all_gather | solution.py:157
  123.5 89.0 %all-gather.12.cloned.1.call-start = ((), (), s32[]{:S(2)}) async-start(), calls=%async_computation.5 | async-start | bytes 1056768 | tf_op jit(solution)/shard_map/all_gather | solution.py:146
  124.1 166.2 %reduce-scatter.6.cloned.1.call-start = ((), (), s32[]{:S(2)}) async-start(), calls=%async_computation.7 | async-start | bytes 2359296 | tf_op jit(solution)/shard_map/reduce_scatter | solution.py:258
  125.4 65.3 %copy-start.26 = (f32[256]{0:T(256)}, f32[256]{0:T(256)S(1)}, u32[]{:S(2)}) copy-start(f32[256]{0:T(256)S(1)} %convert_element_type.180) | copy-start | bytes 3076
  126.6 64.1 %copy-start.23 = (f32[2048]{0:T(1024)}, f32[2048]{0:T(1024)S(1)}, u32[]{:S(2)}) copy-start(f32[2048]{0:T(1024)S(1)} %convert_element_type.182) | copy-start | bytes 24580
  160.3 29.8 %copy-start.8 = (bf16[256,256,1]{1,0,2:T(8,128)(2,1)}, bf16[256,256,1]{1,0,2:T(8,128)(2,1)S(1)}, u32[]{:S(2)}) copy-start(bf16[256,256,1]{1,0,2:T(8,128)(2,1)S(1)} %reshape.245) | copy-start | bytes 393220
  161.7 14.8 %copy-start.14 = (bf16[4,128,256]{1,2,0:T(8,128)(2,1)}, bf16[4,128,256]{1,2,0:T(8,128)(2,1)S(1)}, u32[]{:S(2)}) copy-start(bf16[4,128,256]{1,2,0:T(8,128)(2,1)S(1)} %copy.64) | copy-start | bytes 786436
  176.4 13.6 %copy-start.18 = (f32[4,8,128]{2,1,0:T(8,128)}, f32[4,8,128]{2,1,0:T(8,128)S(1)}, u32[]{:S(2)}) copy-start(f32[4,8,128]{2,1,0:T(8,128)S(1)} %get-tuple-element.53) | copy-start | bytes 49156
  180.4 9.6 copy-start.1
  180.4 10.3 copy-start.11
  190.0 0.7 copy-start.13
  194.5 20.9 %copy-start.2 = (bf16[4,128,256]{2,1,0:T(8,128)(2,1)S(1)}, bf16[4,128,256]{2,1,0:T(8,128)(2,1)}, u32[]{:S(2)}) copy-start(bf16[4,128,256]{2,1,0:T(8,128)(2,1)} %param.31) | copy-start | bytes 786436
  212.5 2.9 copy-start.20
  212.5 4.7 copy-start.33
  212.5 6.3 copy-start.24
  212.5 6.3 copy-start.34
  212.5 6.3 copy-start.36
  218.8 4.7 copy-start.16
  218.8 4.7 copy-start.12
  223.5 2.7 copy-start.3
  223.5 2.7 copy-start.9
  225.4 0.8 copy-start.4
  225.4 11.9 %copy-start.21 = (f32[4,128]{1,0:T(4,128)}, f32[4,128]{1,0:T(4,128)S(1)}, u32[]{:S(2)}) copy-start(f32[4,128]{1,0:T(4,128)S(1)} %negate_multiply_fusion) | copy-start | bytes 6148
  241.3 63.1 %reduce-scatter.4.cloned.1.call-start = ((), (), s32[]{:S(2)}) async-start(), calls=%async_computation.6 | async-start | bytes 2359296 | tf_op jit(solution)/shard_map/reduce_scatter | solution.py:252
  241.4 15.3 %copy-start.19 = (f32[4,8,128]{2,1,0:T(8,128)S(1)}, f32[4,8,128]{2,1,0:T(8,128)}, u32[]{:S(2)}) copy-start(f32[4,8,128]{2,1,0:T(8,128)} %copy-done.18) | copy-start | bytes 49156
  256.6 11.9 %copy-start.15 = (bf16[4,128,256]{1,2,0:T(8,128)(2,1)S(1)}, bf16[4,128,256]{1,2,0:T(8,128)(2,1)}, u32[]{:S(2)}) copy-start(bf16[4,128,256]{1,2,0:T(8,128)(2,1)} %copy-done.14) | copy-start | bytes 786436
  268.5 3.9 copy-start
  276.4 188.6 %all-reduce.26.cloned.1.call-start = ((), (), s32[]{:S(2)}) async-start(), calls=%async_computation.10 | async-start | bytes 6291456
  283.5 20.9 %copy-start.7 = (f32[128,256]{1,0:T(8,128)S(1)}, f32[128,256]{1,0:T(8,128)}, u32[]{:S(2)}) copy-start(f32[128,256]{1,0:T(8,128)} %copy-done.6) | copy-start | bytes 393220
  290.3 16.8 %copy-start.17 = (bf16[4,128,256]{2,1,0:T(8,128)(2,1)S(1)}, bf16[4,128,256]{2,1,0:T(8,128)(2,1)}, u32[]{:S(2)}) copy-start(bf16[4,128,256]{2,1,0:T(8,128)(2,1)} %copy-done.16) | copy-start | bytes 786436
  306.6 4.4 copy-start.10
  306.6 4.5 copy-start.25
  306.6 4.5 copy-start.27
  306.7 4.5 copy-start.28
  306.7 4.5 copy-start.29
  306.7 4.5 copy-start.30
  306.7 4.5 copy-start.31
  306.7 4.5 copy-start.32
  306.7 78.0 %copy-start.5 = (f32[4,128,256]{2,1,0:T(8,128)S(1)}, f32[4,128,256]{2,1,0:T(8,128)}, u32[]{:S(2)}) copy-start(f32[4,128,256]{2,1,0:T(8,128)} %copy-done.4) | copy-start | bytes 1572868
  306.7 78.0 %copy-start.22 = (f32[4,128]{1,0:T(4,128)S(1)}, f32[4,128]{1,0:T(4,128)}, u32[]{:S(2)}) copy-start(f32[4,128]{1,0:T(4,128)} %copy-done.21) | copy-start | bytes 6148
  306.7 78.0 %copy-start.35 = (bf16[4,128,256]{2,1,0:T(8,128)(2,1)S(1)}, bf16[4,128,256]{2,1,0:T(8,128)(2,1)}, u32[]{:S(2)}) copy-start(bf16[4,128,256]{2,1,0:T(8,128)(2,1)} %reduce-scatter.4.cloned.1.call-done) | copy-start | bytes 786436
  306.7 792.7 %reduce-scatter.8.cloned.1.call-start = ((), (), s32[]{:S(2)}) async-start(), calls=%async_computation.8 | async-start | bytes 2113536 | tf_op jit(solution)/shard_map/reduce_scatter | solution.py:306
Sparse Core Ops, SparseCore 0:
  10.8 67.2 all-gather.13
  80.4 23.0 all-gather.9
  123.6 22.1 all-gather.7
  148.5 63.9 all-gather.11
  241.4 27.7 reduce-scatter.5
  276.5 27.8 reduce-scatter.3
  309.5 155.3 all-reduce.25
  468.0 631.4 reduce-scatter.7
where the time goes:
time: 1110 us
  waiting for transfers between devices  742 us (67%)
  blocking collectives  205 us (18%)
  matrix products  84.8 us (8%)
  local copies, waits for them, and re-layouts  38.8 us (3%)
  other arithmetic  20.7 us (2%)
  between operations  14.7 us (1%)
    reduce_scatter x1, waiting for transfers between devices, body(): lax.psum_scatter(grad_terms[9], ('gx', 'gy'), scatter_dimension=0, tiled=...  630 us
    unnamed x2, blocking collectives  133 us
    unnamed x9, waiting for transfers between devices  80.3 us
    all_gather x1, blocking collectives, body(): lax.all_gather(pieces[0], ('gx', 'gy'), axis=0, tiled=True)  38.9 us
    all_gather x1, blocking collectives, body(): lax.all_gather(pieces[3], ('gx', 'gy'), axis=0, tiled=True)  33.6 us
  transfers between devices with their start and end apart: 8, of which 4 were waited for; matrix products, arithmetic and copies ran while one was open for 10% of the time, Pallas kernels for 0%

commit v1 on v0

v1 whole, which is shorter than its diff:
```python
import math

import jax
import jax.numpy as jnp
import numpy as np
from jax import lax
from jax.experimental import pallas as pl
from jax.experimental.pallas import tpu as pltpu
from jax.sharding import PartitionSpec as P

MESH = pl.DeviceIdType.MESH
F32 = jnp.float32
BF16 = jnp.bfloat16

D = 256
HD = 32
EPSILON = 1e-05
GELU_SCALE = math.sqrt(2.0 / math.pi)
SCORE_SCALE = 1.0 / math.sqrt(HD)
EXP2_SCALE = SCORE_SCALE * math.log2(math.e)


def dot(left, right):
    return jnp.dot(left, right, preferred_element_type=F32)


def dot_nt(left, right):
    return lax.dot_general(left, right, (((1,), (1,)), ((), ())), preferred_element_type=F32)


def dot_tn(left, right):
    return lax.dot_general(left, right, (((0,), (0,)), ((), ())), preferred_element_type=F32)


def iota(shape, dim):
    return lax.broadcasted_iota(jnp.int32, shape, dim)


def column_sum(values):
    return jnp.sum(values, axis=0, keepdims=True)


def norm_forward(values, gain, shift):
    centre = jnp.mean(values, axis=-1, keepdims=True)
    moved = values - centre
    spread = jnp.mean(moved * moved, axis=-1, keepdims=True)
    inverse = lax.rsqrt(spread + EPSILON)
    unit = moved * inverse
    return unit * gain + shift, unit, inverse


def norm_backward(d_out, unit, inverse, gain):
    d_unit = d_out * gain
    mean_d = jnp.mean(d_unit, axis=-1, keepdims=True)
    mean_du = jnp.mean(d_unit * unit, axis=-1, keepdims=True)
    return inverse * (d_unit - mean_d - unit * mean_du)


SCRATCH = dict(
    pf=((48, 128), F32),
    s1=((8, 112, 128), BF16),
    asmf=((384, 128), F32),
    img=((4, 2, 128, 256), BF16),
    cotb=((4, 128, 256), BF16),
    wio=((16, 112, 128), BF16),
    ff=((2, 16, 128, 256), BF16),
    vecs=((16, 256), F32),
    sh=((1024, 256), BF16),
    sht=((256, 1024), BF16),
    imgt=((256, 1024), BF16),
    kk=((1024, 128), BF16),
    vv=((1024, 128), BF16),
    qq=((1024, 128), BF16),
    kt=((128, 1024), BF16),
    vt=((128, 1024), BF16),
    qt=((256, 1024), BF16),
    ee=((4, 1024, 1024), BF16),
    ot=((128, 1024), F32),
    ri=((8, 1024), F32),
    mx=((4, 2, 128, 128), BF16),
    mr=((4, 128, 128), BF16),
    hid=((512, 256), F32),
    hlow=((512, 256), BF16),
    hlt=((256, 512), BF16),
    unit1=((512, 256), F32),
    inv1=((512, 1), F32),
    act=((8, 512, 256), BF16),
    dgl=((8, 512, 256), BF16),
    acc=((512, 256), F32),
    lob=((4, 128, 256), BF16),
    lor=((4, 128, 256), BF16),
    dffn=((512, 256), BF16),
    gp=((2, 16, 128, 256), BF16),
    gs=((16, 128, 256), BF16),
    rs=((16, 128, 256), BF16),
    r1=((3, 4, 128, 256), BF16),
    s2=((4, 128, 256), BF16),
    r2=((3, 128, 256), BF16),
    fin=((2, 128, 128), F32),
    gv=((16, 256), F32),
    dfirst=((512, 256), F32),
    dms=((4, 128, 128), BF16),
    dmx=((4, 2, 128, 128), BF16),
    dot_=((256, 1024), BF16),
    doo=((1024, 128), BF16),
    ds=((1024, 1024), BF16),
    dqt=((128, 1024), F32),
    dk=((1024, 128), F32),
    dv=((1024, 128), F32),
    gio=((16, 80, 128), BF16),
    q1=((3, 4, 80, 128), BF16),
    qs2=((4, 80, 128), BF16),
    q2=((3, 80, 128), BF16),
    fio=((80, 128), F32),
    v0=((16, 256), F32),
    vr1=((3, 16, 256), F32),
    v1=((16, 256), F32),
    vr2=((3, 16, 256), F32),
    v2=((16, 256), F32),
    vr3=((8, 16, 256), F32),
    gt=((4, 2, 128, 256), BF16),
    gtr=((4, 128, 256), BF16),
    gob=((4, 128, 256), BF16),
    gor=((4, 128, 256), BF16),
    p3f=((8, 48, 128), F32),
    p3=((8, 48, 128), BF16),
    r3=((8, 48, 128), BF16),
)

SEMS = dict(
    s1_s=7, s1_r=8, tk_s=3, tk_r=4, tf_s=4, tf_r=4, ct_s=3, ct_r=4,
    wi_sa=3, wi_sb=12, wi_r=16, wo_sa=3, wo_sb=12, wo_r=16,
    ff_sa=3, ff_sb=12, ff_r=16, fw_s=16, fw_r=16,
    mx_s=1, mx_r=1, dm_s=1, dm_r=1, lo_s=3, lo_r=4, gs_s=1, gs_r=1,
    r1_s=3, r1_r=3, r2_s=3, r2_r=3, q1_s=3, q1_r=3, q2_s=3, q2_r=3,
    v1_s=3, v1_r=3, v2_s=3, v2_r=3, v3_s=7, v3_r=8,
    gt_s=1, gt_r=1, go_s=3, go_r=4, p3_s=7, p3_r=8,
)

INPUTS = (
    "tok", "cot", "lens", "freq", "w_in", "w_out", "w_up", "w_down",
    "b_q", "b_v", "b_out", "gain1", "shift1", "b_down", "gain2", "shift2", "b_up",
)
OUTPUTS = (
    "layer_out", "grad_tokens", "g_w_in", "g_b_q", "g_b_v", "g_w_out", "g_b_out",
    "g_gain1", "g_shift1", "g_w_up", "g_b_up", "g_w_down", "g_b_down", "g_gain2", "g_shift2",
)
SMALL = ("b_q", "b_v", "b_out", "gain1", "shift1", "b_down", "gain2", "shift2")
G_SMALL = tuple("g_" + name for name in SMALL)
ROW = {name: row for row, name in enumerate(SMALL)}


class Refs:
    pass


def kernel(*refs):
    r = Refs()
    names = INPUTS + OUTPUTS + tuple(SCRATCH) + tuple(SEMS)
    for name, ref in zip(names, refs):
        setattr(r, name, ref)

    gx, gy = lax.axis_index("gx"), lax.axis_index("gy")
    x, y = lax.div(gx, 4), lax.rem(gx, 4)
    z, c = lax.div(gy, 2), lax.rem(gy, 2)
    a = x * (1 - c) + y * c
    b = y * (1 - c) + x * c

    def group(a_at, b_at):
        return a_at * (4 - 3 * c) + b_at * (1 + 3 * c)

    def ring(at, step, size=4):
        return lax.rem(at + (step % size), size)

    def a_peer(step):
        return (group(ring(a, step), b), gy)

    def b_peer(step):
        return (group(a, ring(b, step)), gy)

    def z_peer(step):
        return (gx, 2 * ring(z, step) + c)

    def gy_peer(step):
        return (gx, ring(gy, step, 8))

    sibling = (gx, 2 * z + 1 - c)
    here = group(a, b)

    def remote(src, dst, send, recv, device):
        return pltpu.make_async_remote_copy(
            src_ref=src, dst_ref=dst, send_sem=send, recv_sem=recv,
            device_id=device, device_id_type=MESH,
        )

    sent = []

    def send(make):
        make().start()
        sent.append(make)

    def await_recv(ref, sem):
        remote(ref, ref, sem, sem, sibling).wait_recv()

    barrier = pltpu.get_barrier_semaphore()
    peers = [a_peer(k) for k in (1, 2, 3)] + [b_peer(k) for k in (1, 2, 3)]
    peers += [gy_peer(k) for k in range(1, 8)]
    for peer in peers:
        pl.semaphore_signal(barrier, inc=1, device_id=peer, device_id_type=MESH)

    column = 0
    for ref, chunks in ((r.w_in, 6), (r.w_out, 2), (r.w_up, 16)):
        rows = ref[...].astype(F32)
        for k in range(chunks):
            for row in range(2):
                at = row * 24 + column
                r.pf[at : at + 1, :] = rows[row : row + 1, k * 128 : (k + 1) * 128]
            column += 1
    lane = iota((1, 256), 1)
    place = 2 * (8 * gx + gy)
    small_rows = []
    for name in SMALL:
        pair = getattr(r, name)[...].astype(F32).reshape(1, 2)
        row = jnp.where(lane == place, pair[:, 0:1], 0.0)
        small_rows.append(jnp.where(lane == place + 1, pair[:, 1:2], row))
    up_bias = r.b_up[...].astype(F32).reshape(1, 16)
    up_place = 128 * lax.rem(gx, 2) + 16 * gy
    up_row = jnp.zeros((1, 256), F32)
    for k in range(16):
        up_row = jnp.where(lane == up_place + k, up_bias[:, k : k + 1], up_row)
    up_rows = jnp.where(iota((8, 256), 0) == lax.div(gx, 2), up_row, 0.0)
    vec_low = jnp.concatenate(small_rows + [up_rows], axis=0).astype(BF16)
    r.s1[gy, 0:48, :] = r.pf[...].astype(BF16)
    r.s1[gy, 48:64, :] = r.w_down[:, 0:128]
    r.s1[gy, 64:80, :] = r.w_down[:, 128:256]
    r.s1[gy, 80:96, :] = vec_low[:, 0:128]
    r.s1[gy, 96:112, :] = vec_low[:, 128:256]

    pl.semaphore_wait(barrier, 13)

    for k in range(1, 8):
        send(lambda k=k: remote(
            r.s1.at[gy], r.s1.at[gy], r.s1_s.at[k - 1], r.s1_r.at[gy], gy_peer(k)))
    for k in (1, 2, 3):
        send(lambda k=k: remote(
            r.tok.at[ring(z, k)], r.img.at[z, c], r.tk_s.at[k - 1], r.tk_r.at[z], z_peer(k)))
    r.img[z, c] = r.tok[z]
    send(lambda: remote(r.img.at[z, c], r.img.at[z, c], r.tf_s.at[0], r.tf_r.at[z], sibling))
    r.cotb[z] = r.cot[z]

    freq = r.freq[...]
    even = lax.rem(iota((1, 256), 1), 2) == 0
    fine = iota((32, 256), 0).astype(F32) * freq
    coarse = iota((32, 256), 0).astype(F32) * 32.0 * freq
    sin_f, cos_f = jnp.sin(fine), jnp.cos(fine)
    sin_c, cos_c = jnp.sin(coarse), jnp.cos(coarse)
    first_c = jnp.where(even, sin_c, cos_c)
    second_c = jnp.where(even, cos_c, -sin_c)

    for k in range(1, 8):
        at = ring(gy, -k, 8)
        await_recv(r.s1.at[at], r.s1_r.at[at])
    vec_sum = jnp.zeros((32, 128), F32)
    for i in range(8):
        piece = r.s1[i, 0:48, :].astype(F32)
        for row in range(2):
            r.asmf[pl.ds(2 * i + row, 24, stride=16), :] = piece[row * 24 : row * 24 + 24]
        vec_sum = vec_sum + r.s1[i, 80:112, :].astype(F32)
    for k in range(3):
        rows = r.asmf[pl.ds(pl.multiple_of(32 * k + 16 * c, 16), 16), :]
        r.wio[here, 16 * k : 16 * k + 16, :] = rows.astype(BF16)
    r.wio[here, 48:80, :] = vec_sum.astype(BF16)
    r.wio[here, 80:112, :] = r.asmf[96:128, :].astype(BF16)

    def block(ref, at, part):
        return ref.at[at, pl.ds(part[0], part[1])]

    def gather_start(view, sem_a, sem_b, recv):
        for k in (1, 2, 3):
            send(lambda k=k: remote(
                view(here), view(here), sem_a.at[k - 1], recv.at[here], a_peer(k)))
        for k in (1, 2, 3):
            send(lambda k=k: remote(
                view(here), view(here), sem_b.at[k - 1], recv.at[here], b_peer(k)))

    def gather_relay(view, sem_b, recv):
        for i in (1, 2, 3):
            at = group(ring(a, -i), b)
            await_recv(view(at), recv.at[at])
            for k in (1, 2, 3):
                send(lambda k=k, i=i, at=at: remote(
                    view(at), view(at), sem_b.at[3 * i + k - 1], recv.at[at], b_peer(k)))

    def gather_wait(view, recv):
        for k in (1, 2, 3):
            for i in range(4):
                at = group(ring(a, -i), ring(b, -k))
                await_recv(view(at), recv.at[at])

    def wi_view(at):
        return r.wio.at[at, pl.ds(0, 80)]

    def wo_view(at):
        return r.wio.at[at, pl.ds(80, 32)]

    def ff_view(at):
        return r.ff.at[c, at]

    gather_start(wi_view, r.wi_sa, r.wi_sb, r.wi_r)

    @pl.when(c == 0)
    def _():
        for j in range(8):
            for half in range(2):
                at = 16 * (8 + 2 * j + half)
                r.ff[0, here, 16 * j : 16 * j + 16, 128 * half : 128 * half + 128] = (
                    r.asmf[at : at + 16, :].astype(BF16))

    @pl.when(c == 1)
    def _():
        for i in range(8):
            for half in range(2):
                r.ff[1, here, 16 * i : 16 * i + 16, 128 * half : 128 * half + 128] = (
                    r.s1[i, 48 + 16 * half : 64 + 16 * half, :])

    gather_start(ff_view, r.ff_sa, r.ff_sb, r.ff_r)
    gather_start(wo_view, r.wo_sa, r.wo_sb, r.wo_r)

    for k in (1, 2, 3):
        at = ring(z, -k)
        await_recv(r.img.at[at, c], r.tk_r.at[at])
        send(lambda k=k, at=at: remote(
            r.img.at[at, c], r.img.at[at, c], r.tf_s.at[k], r.tf_r.at[at], sibling))
    for k in (1, 2, 3):
        send(lambda k=k: remote(
            r.cot.at[ring(z, k)], r.cotb.at[z], r.ct_s.at[k - 1], r.ct_r.at[z], z_peer(k)))

    gather_relay(wi_view, r.wi_sb, r.wi_r)

    for k in range(4):
        at = ring(z, -k)
        await_recv(r.img.at[at, 1 - c], r.tf_r.at[at])

    for i in range(8):
        rows = r.img[i // 2, i % 2].astype(F32)
        for k in range(4):
            at = 4 * i + k
            pos = first_c[at : at + 1] * cos_f + second_c[at : at + 1] * sin_f
            r.sh[32 * at : 32 * at + 32, :] = (rows[32 * k : 32 * k + 32] + pos).astype(BF16)
    image = r.img[...].reshape(1024, 256)

    gather_relay(ff_view, r.ff_sb, r.ff_r)
    gather_relay(wo_view, r.wo_sb, r.wo_r)

    r.sht[...] = r.sh[...].T
    r.imgt[...] = image.T

    gather_wait(wi_view, r.wi_r)
    vec_sum = jnp.zeros((32, 128), F32)
    for i in range(16):
        vec_sum = vec_sum + r.wio[i, 48:80, :].astype(F32)
    r.vecs[:, 0:128] = vec_sum[0:16]
    r.vecs[:, 128:256] = vec_sum[16:32]

    def own_half(row):
        both = r.vecs[row : row + 1, :]
        return both[:, 0:128] * (1 - c).astype(F32) + both[:, 128:256] * c.astype(F32)

    def w_part(k):
        return r.wio[:, 16 * k : 16 * k + 16, :].reshape(256, 128)

    queries = (dot(r.sh[...], w_part(0)) + own_half(ROW["b_q"])).astype(BF16)
    keys = dot(r.sh[...], w_part(1)).astype(BF16)
    values = (dot(image, w_part(2)) + own_half(ROW["b_v"])).astype(BF16)
    r.qq[...] = queries
    r.kk[...] = keys
    r.vv[...] = values
    r.kt[...] = keys.T
    r.vt[...] = values.T
    r.qt[0:128, :] = queries.T
    ones_row = iota((128, 1024), 0) == 0
    r.qt[128:256, :] = jnp.where(ones_row, 1.0, 0.0).astype(BF16)

    length = r.lens[z]

    def head_lanes(head):
        return lax.div(iota((1024, 128), 1), HD) == head

    def forward_head(head, carry):
        masked = jnp.where(head_lanes(head), r.kk[...], jnp.zeros((), BF16))
        hidden_key = (iota((1024, 128), 0) >= length) & (iota((1024, 128), 1) == 0)
        bias = jnp.where(hidden_key, -1e30, 0.0).astype(BF16)
        scores = dot(jnp.concatenate([masked, bias], axis=1), r.qt[...])
        peak = jnp.max(scores, axis=0, keepdims=True)
        weights = jnp.exp2(scores * EXP2_SCALE - peak * EXP2_SCALE).astype(BF16)
        r.ee[head] = weights
        rows = r.vt[pl.ds(pl.multiple_of(head * HD, HD), HD), :]
        left = jnp.concatenate([rows, jnp.ones((16, 1024), BF16)], axis=0)
        mixed = dot(left, weights)
        inverse = 1.0 / mixed[HD : HD + 1]
        r.ot[pl.ds(pl.multiple_of(head * HD, HD), HD), :] = mixed[0:HD] * inverse
        r.ri[pl.ds(head, 1), :] = inverse

        @pl.when(head == 2)
        def _():
            gather_wait(ff_view, r.ff_r)
            for i in range(16):
                remote(ff_view(i), ff_view(i), r.fw_s.at[i], r.fw_r.at[i], sibling).start()

        return carry

    lax.fori_loop(0, 4, forward_head, 0)
    for i in range(16):
        sent.append(lambda i=i: remote(
            ff_view(i), ff_view(i), r.fw_s.at[i], r.fw_r.at[i], sibling))

    r.mx[...] = r.ot[...].T.astype(BF16).reshape(4, 2, 128, 128)
    send(lambda: remote(r.mx.at[:, 1 - c], r.mr, r.mx_s.at[0], r.mx_r.at[0], sibling))

    gather_wait(wo_view, r.wo_r)

    def w_out_rows(half):
        low = r.wio[pl.ds(8 * half, 8), 80:96, :].reshape(128, 128)
        high = r.wio[pl.ds(8 * half, 8), 96:112, :].reshape(128, 128)
        return jnp.concatenate([low, high], axis=1)

    def vec(name):
        return r.vecs[ROW[name] : ROW[name] + 1, :]

    mixed_own = r.mx[:, c].reshape(512, 128)
    branch = dot(mixed_own, w_out_rows(c))
    await_recv(r.mr, r.mx_r.at[0])
    mixed_other = r.mr[...].reshape(512, 128)
    branch = branch + dot(mixed_other, w_out_rows(1 - c))
    first_sum = r.img[:, c].reshape(512, 256).astype(F32) + branch + vec("b_out")
    hidden, unit, inverse = norm_forward(first_sum, vec("gain1"), vec("shift1"))
    r.unit1[...] = unit
    r.inv1[...] = inverse
    r.hid[...] = hidden
    hidden_low = hidden.astype(BF16)
    r.hlow[...] = hidden_low
    r.hlt[...] = hidden_low.T

    for i in range(16):
        await_recv(r.ff.at[1 - c, i], r.fw_r.at[i])

    def up_block(j):
        return r.ff[0, :, pl.ds(pl.multiple_of(16 * j, 16), 16), :].reshape(256, 256)

    def down_block(j):
        return r.ff[1, pl.ds(2 * j, 2), :, :].reshape(256, 256)

    def forward_ffn(j, carry):
        up = dot(r.hlow[...], up_block(j)) + r.vecs[pl.ds(8 + j, 1), :]
        square = up * up
        wave = jnp.tanh(GELU_SCALE * (up + 0.044715 * up * square))
        active = (0.5 * up * (1.0 + wave)).astype(BF16)
        slope = GELU_SCALE * (1.0 + 3 * 0.044715 * square)
        grad = 0.5 * (1.0 + wave) + 0.5 * up * (1.0 - wave * wave) * slope
        r.act[j] = active
        r.dgl[j] = grad.astype(BF16)
        r.acc[...] += dot(active, down_block(j))
        return carry

    r.acc[...] = r.hid[...] + vec("b_down")
    lax.fori_loop(0, 8, forward_ffn, 0)

    out, unit, inverse = norm_forward(r.acc[...], vec("gain2"), vec("shift2"))
    r.lob[...] = out.astype(BF16).reshape(4, 128, 256)
    for k in (1, 2, 3):
        send(lambda k=k: remote(
            r.lob.at[ring(z, k)], r.lor.at[z], r.lo_s.at[k - 1], r.lo_r.at[z], z_peer(k)))
    r.lor[z] = r.lob[z]

    for k in (1, 2, 3):
        at = ring(z, -k)
        await_recv(r.cotb.at[at], r.ct_r.at[at])
    d_out = r.cotb[...].reshape(512, 256).astype(F32)
    r.gv[ROW["gain2"] : ROW["gain2"] + 1, :] = column_sum(d_out * unit)
    r.gv[ROW["shift2"] : ROW["shift2"] + 1, :] = column_sum(d_out)
    d_second = norm_backward(d_out, unit, inverse, vec("gain2"))
    d_ffn = d_second.astype(BF16)
    r.dffn[...] = d_ffn
    r.gv[ROW["b_down"] : ROW["b_down"] + 1, :] = column_sum(d_ffn.astype(F32))
    r.acc[...] = d_second

    def backward_ffn(j, carry):
        d_active = dot_nt(r.dffn[...], down_block(j))
        d_up = (d_active * r.dgl[j].astype(F32)).astype(BF16)
        g_down = dot_tn(r.act[j], r.dffn[...])
        r.gp[1, pl.ds(2 * j, 2)] = g_down.astype(BF16).reshape(2, 128, 256)
        g_up = dot(r.hlt[...], d_up)
        r.gp[0, :, pl.ds(pl.multiple_of(16 * j, 16), 16), :] = (
            g_up.astype(BF16).reshape(16, 16, 256))
        r.gv[pl.ds(8 + j, 1), :] = column_sum(d_up.astype(F32))
        r.acc[...] += dot_nt(d_up, up_block(j))
        return carry

    lax.fori_loop(0, 8, backward_ffn, 0)
    send(lambda: remote(r.gp.at[1 - c], r.gs, r.gs_s.at[0], r.gs_r.at[0], sibling))

    d_hidden = r.acc[...]
    unit = r.unit1[...]
    r.gv[ROW["gain1"] : ROW["gain1"] + 1, :] = column_sum(d_hidden * unit)
    r.gv[ROW["shift1"] : ROW["shift1"] + 1, :] = column_sum(d_hidden)
    d_first = norm_backward(d_hidden, unit, r.inv1[...], vec("gain1"))
    r.dfirst[...] = d_first
    d_branch = d_first.astype(BF16)
    r.gv[ROW["b_out"] : ROW["b_out"] + 1, :] = column_sum(d_branch.astype(F32))
    r.dms[...] = dot_nt(d_branch, w_out_rows(1 - c)).astype(BF16).reshape(4, 128, 128)
    send(lambda: remote(r.dms, r.dmx.at[:, c], r.dm_s.at[0], r.dm_r.at[0], sibling))
    r.dmx[:, c] = dot_nt(d_branch, w_out_rows(c)).astype(BF16).reshape(4, 128, 128)

    def spot(g):
        return g * (1 - c) + (4 * lax.rem(g, 4) + lax.div(g, 4)) * c

    for half, mixed in ((c, r.mx[:, c].reshape(512, 128)), (1 - c, r.mr[...].reshape(512, 128))):
        g_out = dot_tn(mixed, d_branch).astype(BF16)
        for i in range(8):
            at = spot(8 * half + i)
            r.gio[at, 48:64, :] = g_out[16 * i : 16 * i + 16, 0:128]
            r.gio[at, 64:80, :] = g_out[16 * i : 16 * i + 16, 128:256]

    await_recv(r.dmx.at[:, 1 - c], r.dm_r.at[0])
    d_mixed_t = r.dmx[...].reshape(1024, 128).astype(F32).T
    extra = []
    for head in range(4):
        rows = slice(32 * head, 32 * head + 32)
        scaled = d_mixed_t[rows] * r.ri[head : head + 1, :]
        r.dot_[rows, :] = scaled.astype(BF16)
        inner = -column_sum(scaled * r.ot[rows, :])
        high = inner.astype(BF16).astype(F32)
        extra += [high, inner - high]
    extra.append(jnp.zeros((8, 1024), F32))
    r.dot_[128:144, :] = jnp.concatenate(extra, axis=0).astype(BF16)
    r.dot_[144:256, :] = jnp.zeros((112, 1024), BF16)
    r.doo[...] = r.dot_[0:128, :].T
    r.dk[...] = jnp.zeros((1024, 128), F32)
    r.dv[...] = jnp.zeros((1024, 128), F32)

    def add_siblings():
        await_recv(r.gs, r.gs_r.at[0])

        def add(i, carry):
            at = group(lax.div(i, 4), lax.rem(i, 4))
            r.rs[i] = (r.gp[c, at].astype(F32) + r.gs[at].astype(F32)).astype(BF16)
            return carry

        lax.fori_loop(0, 16, add, 0)
        for k in (1, 2, 3):
            ff_first(k).start()

    def ff_first(k):
        return remote(
            r.rs.at[pl.ds(4 * ring(a, k), 4)], r.r1.at[k - 1], r.r1_s.at[k - 1],
            r.r1_r.at[k - 1], a_peer(k))

    def ff_second(k):
        return remote(
            r.s2.at[ring(b, k)], r.r2.at[k - 1], r.r2_s.at[k - 1], r.r2_r.at[k - 1], b_peer(k))

    def add_first():
        for k in range(3):
            await_recv(r.r1.at[k], r.r1_r.at[k])

        def add(i, carry):
            total = r.rs[4 * a + i].astype(F32)
            for k in range(3):
                total = total + r.r1[k, i].astype(F32)
            r.s2[i] = total.astype(BF16)
            return carry

        lax.fori_loop(0, 4, add, 0)
        for k in (1, 2, 3):
            ff_second(k).start()

    def backward_head(head, carry):
        lanes = head_lanes(head)
        zero = jnp.zeros((), BF16)
        masked = jnp.where(lanes, r.vv[...], zero)
        ones = jnp.where(lax.div(iota((1024, 128), 1), 2) == head, 1.0, 0.0).astype(BF16)
        d_probs = dot(jnp.concatenate([masked, ones], axis=1), r.dot_[...])
        d_scores = r.ee[head] * d_probs.astype(BF16)
        r.ds[...] = d_scores
        at = pl.ds(pl.multiple_of(head * HD, HD), HD)
        r.dqt[at, :] = dot(r.kt[at, :], d_scores)
        q_masked = jnp.where(lanes, r.qq[...], zero)
        do_masked = jnp.where(lanes, r.doo[...], zero)
        for k in range(0, 1024, 256):
            r.dk[k : k + 256, :] += dot(r.ds[k : k + 256, :], q_masked)
            r.dv[k : k + 256, :] += dot(r.ee[head, k : k + 256, :], do_masked)

        @pl.when(head == 0)
        def _():
            add_siblings()

        @pl.when(head == 3)
        def _():
            add_first()

        return carry

    lax.fori_loop(0, 4, backward_head, 0)
    for k in (1, 2, 3):
        sent.append(lambda k=k: ff_first(k))
        sent.append(lambda k=k: ff_second(k))

    d_queries = (r.dqt[...] * SCORE_SCALE).T.astype(BF16)
    d_keys = (r.dk[...] * SCORE_SCALE).astype(BF16)
    d_values = r.dv[...].astype(BF16)
    for k, (left, right) in enumerate(((r.sht, d_queries), (r.sht, d_keys), (r.imgt, d_values))):
        g_part = dot(left[...], right).astype(BF16)
        for i in range(16):
            r.gio[spot(i), 16 * k : 16 * k + 16, :] = g_part[16 * i : 16 * i + 16, :]

    def io_first(k):
        return remote(
            r.gio.at[pl.ds(4 * ring(a, k), 4)], r.q1.at[k - 1], r.q1_s.at[k - 1],
            r.q1_r.at[k - 1], a_peer(k))

    for k in (1, 2, 3):
        send(lambda k=k: io_first(k))
    low_half, high_half = (1 - c).astype(F32), c.astype(F32)
    for name, d_rows in (("b_q", d_queries), ("b_v", d_values)):
        sums = column_sum(d_rows.astype(F32))
        r.gv[ROW[name] : ROW[name] + 1, :] = jnp.concatenate(
            [sums * low_half, sums * high_half], axis=1)
    r.v0[...] = r.gv[...]
    for k in (1, 2, 3):
        send(lambda k=k: remote(
            r.v0, r.vr1.at[k - 1], r.v1_s.at[k - 1], r.v1_r.at[k - 1], a_peer(k)))

    d_tokens = (
        dot_nt(d_queries, w_part(0)) + dot_nt(d_keys, w_part(1)) + dot_nt(d_values, w_part(2)))
    r.gt[...] = d_tokens.astype(BF16).reshape(4, 2, 128, 256)
    send(lambda: remote(r.gt.at[:, 1 - c], r.gtr, r.gt_s.at[0], r.gt_r.at[0], sibling))

    for k in range(3):
        await_recv(r.q1.at[k], r.q1_r.at[k])
    for i in range(4):
        total = r.gio[4 * a + i].astype(F32)
        for k in range(3):
            total = total + r.q1[k, i].astype(F32)
        r.qs2[i] = total.astype(BF16)
    for k in (1, 2, 3):
        send(lambda k=k: remote(
            r.qs2.at[ring(b, k)], r.q2.at[k - 1], r.q2_s.at[k - 1], r.q2_r.at[k - 1], b_peer(k)))
    total = r.v0[...]
    for k in range(3):
        await_recv(r.vr1.at[k], r.v1_r.at[k])
        total = total + r.vr1[k]
    r.v1[...] = total
    for k in (1, 2, 3):
        send(lambda k=k: remote(
            r.v1, r.vr2.at[k - 1], r.v2_s.at[k - 1], r.v2_r.at[k - 1], b_peer(k)))

    await_recv(r.gtr, r.gt_r.at[0])
    full = (
        r.dfirst[...]
        + r.gt[:, c].reshape(512, 256).astype(F32)
        + r.gtr[...].reshape(512, 256).astype(F32))
    r.gob[...] = full.astype(BF16).reshape(4, 128, 256)
    for k in (1, 2, 3):
        send(lambda k=k: remote(
            r.gob.at[ring(z, k)], r.gor.at[z], r.go_s.at[k - 1], r.go_r.at[z], z_peer(k)))
    r.gor[z] = r.gob[z]

    for k in range(3):
        await_recv(r.r2.at[k], r.r2_r.at[k])
    total = r.s2[b].astype(F32)
    for k in range(3):
        total = total + r.r2[k].astype(F32)
    r.fin[0] = total[:, 0:128]
    r.fin[1] = total[:, 128:256]
    for k in range(3):
        await_recv(r.q2.at[k], r.q2_r.at[k])
    total = r.qs2[b].astype(F32)
    for k in range(3):
        total = total + r.q2[k].astype(F32)
    r.fio[...] = total

    r.p3f[...] = jnp.zeros((8, 48, 128), F32)

    @pl.when(c == 0)
    def _():
        for i in range(8):
            for half in range(2):
                for row in range(2):
                    at = 16 * half + 8 * row
                    r.p3f[i, at : at + 8, :] = r.fin.at[half][
                        pl.ds(2 * i + row, 8, stride=16), :]

    @pl.when(c == 1)
    def _():
        for i in range(8):
            for half in range(2):
                r.p3f[i, 16 * half : 16 * half + 16, :] = r.fin[half, 16 * i : 16 * i + 16, :]

    for i in range(8):
        for row in range(2):
            at = 32 + 8 * row
            r.p3f[i, at : at + 5, :] = r.fio[pl.ds(2 * i + row, 5, stride=16), :]
    r.p3[...] = r.p3f[...].astype(BF16)
    for k in range(1, 8):
        send(lambda k=k: remote(
            r.p3.at[ring(gy, k, 8)], r.r3.at[gy], r.p3_s.at[k - 1], r.p3_r.at[gy], gy_peer(k)))
    r.r3[gy] = r.p3[gy]

    total = r.v1[...]
    for k in range(3):
        await_recv(r.vr2.at[k], r.v2_r.at[k])
        total = total + r.vr2[k]
    r.v2[...] = total
    for k in range(1, 8):
        send(lambda k=k: remote(
            r.v2, r.vr3.at[gy], r.v3_s.at[k - 1], r.v3_r.at[gy], gy_peer(k)))
    r.vr3[gy] = r.v2[...]

    for k in (1, 2, 3):
        at = ring(z, -k)
        await_recv(r.lor.at[at], r.lo_r.at[at])
    r.layer_out[...] = r.lor[...]
    for k in (1, 2, 3):
        at = ring(z, -k)
        await_recv(r.gor.at[at], r.go_r.at[at])
    r.grad_tokens[...] = r.gor[...].astype(F32)

    for k in range(1, 8):
        at = ring(gy, -k, 8)
        await_recv(r.r3.at[at], r.p3_r.at[at])
    core0 = jnp.zeros((48, 128), F32)
    core1 = jnp.zeros((48, 128), F32)
    for i in range(4):
        core0 = core0 + r.r3[2 * i].astype(F32)
        core1 = core1 + r.r3[2 * i + 1].astype(F32)
    r.g_w_down[:, 0:128] = core1[0:16]
    r.g_w_down[:, 128:256] = core1[16:32]
    for row in range(2):
        out_row = slice(row, row + 1)
        for j in range(8):
            for half in range(2):
                at = 16 * half + 8 * row + j
                lanes = 256 * j + 128 * half
                r.g_w_up[out_row, lanes : lanes + 128] = core0[at : at + 1]
        base = 32 + 8 * row
        for k in range(3):
            at = base + k
            r.g_w_in[out_row, 256 * k : 256 * k + 128] = core0[at : at + 1]
            r.g_w_in[out_row, 256 * k + 128 : 256 * k + 256] = core1[at : at + 1]
        both = core0 + core1
        r.g_w_out[out_row, 0:128] = both[base + 3 : base + 4]
        r.g_w_out[out_row, 128:256] = both[base + 4 : base + 5]

    for k in range(1, 8):
        at = ring(gy, -k, 8)
        await_recv(r.vr3.at[at], r.v3_r.at[at])
    total = jnp.zeros((16, 256), F32)
    for i in range(8):
        total = total + r.vr3[i]
    moved = pltpu.roll(total, lax.rem(256 - place, 256), axis=1)
    for name in SMALL:
        row = ROW[name]
        getattr(r, "g_" + name)[...] = moved[row : row + 1, 0:2].reshape(2)
    up_total = column_sum(jnp.where(iota((8, 256), 0) == lax.div(gx, 2), total[8:16], 0.0))
    up_total = jnp.broadcast_to(up_total, (8, 256))
    up_total = pltpu.roll(up_total, lax.rem(256 - up_place, 256), axis=1)
    r.g_b_up[...] = up_total[0:1, 0:16].reshape(16)

    for make in sent:
        make().wait_send()


def body(
    tokens, lengths, w_in, b_q, b_v, w_out, b_out, gain_first, shift_first, w_up, b_up,
    w_down, b_down, gain_second, shift_second, cotangent,
):
    column = np.arange(D)
    freq = np.power(10000.0, -(2.0 * (column // 2)) / D).astype(np.float32)[None, :]
    args = (
        tokens, cotangent, lengths, jnp.asarray(freq), w_in, w_out, w_up, w_down,
        b_q, b_v, b_out, gain_first, shift_first, b_down, gain_second, shift_second, b_up,
    )
    vmem = pl.BlockSpec(memory_space=pltpu.VMEM)
    in_specs = [vmem] * len(args)
    in_specs[2] = pl.BlockSpec(memory_space=pltpu.SMEM)
    shape = jax.ShapeDtypeStruct
    vector = shape((2,), F32)
    out_shape = (
        shape((4, 128, 256), BF16), shape((4, 128, 256), F32), shape((2, 768), F32),
        vector, vector, shape((2, 256), F32), vector, vector, vector,
        shape((2, 2048), F32), shape((16,), F32), shape((16, 256), F32),
        vector, vector, vector,
    )
    scratch = [pltpu.VMEM(dims, kind) for dims, kind in SCRATCH.values()]
    scratch += [pltpu.SemaphoreType.DMA((count,)) for count in SEMS.values()]
    return pl.pallas_call(
        kernel,
        out_shape=out_shape,
        in_specs=in_specs,
        out_specs=tuple([vmem] * len(out_shape)),
        scratch_shapes=scratch,
        compiler_params=pltpu.CompilerParams(
            collective_id=0, has_side_effects=True, vmem_limit_bytes=62 * 2**20),
        name="encoder_layer",
    )(*args)


def solution(mesh):
    both = ("gx", "gy")
    rows, vector, whole = P(both, None), P(both), P("gx", "gy", None)
    return jax.shard_map(
        body,
        mesh=mesh,
        in_specs=(
            whole, P("gx"), rows, vector, vector, rows, vector, vector, vector, rows, vector,
            rows, vector, vector, vector, whole,
        ),
        out_specs=(
            whole, whole, rows, vector, vector, rows, vector, vector, vector, rows, vector,
            rows, vector, vector, vector,
        ),
        check_vma=False,
    )
```

time: 1110 us -> 86.8 us (0.08)
  waiting for transfers between devices: 742 us -> 0 us
  blocking collectives: 205 us -> 0 us
  matrix products: 84.8 us -> 0 us
  Pallas kernels: 0 us -> 75.7 us
  local copies, waits for them, and re-layouts: 38.8 us -> 10.2 us
  other arithmetic: 20.7 us -> 0 us
  between operations: 14.7 us -> 0.7 us
    reduce_scatter x3 -> x0, waiting for transfers between devices: 643 us -> none  [the longest x1 630 us: body(): lax.psum_scatter(grad_terms[9], ('gx', 'gy'), scatter_dimension=0, tiled=...]
    unnamed x2 -> x0, blocking collectives: 133 us -> none
    unnamed x9 -> x0, waiting for transfers between devices: 80.3 us -> none
    pallas_call x0 -> x1, Pallas kernels: none -> 75.7 us  [body(): pl.pallas_call(kernel, out_shape=out_shape, in_specs=in_specs, out_specs=...]
    dot_general x20 -> x0, matrix products: 75.5 us -> none  [the longest x1 15.2 us: body(): jnp.einsum('iqhd,ikhd->ihqk', split_heads(d_mixed), split_heads(all_value...]
    all_gather x2 -> x0, blocking collectives: 72.4 us -> none  [the longest x1 38.9 us: body(): lax.all_gather(pieces[0], ('gx', 'gy'), axis=0, tiled=True)]
    all_gather x4 -> x0, waiting for transfers between devices: 18.1 us -> none  [the longest x1 18 us: body(): lax.all_gather(pieces[9], ('gx', 'gy'), axis=0, tiled=True)]
    convert_element_type x11 -> x0, other arithmetic: 13.6 us -> none  [the longest x1 11.9 us: body(): d_scores = (attn_probs * (d_probs - inner_sum)).astype(jnp.bfloat16)]
  transfers between devices with their start and end apart: 8 -> 0, of which waited for: 4 -> 0; matrix products, arithmetic and copies ran while one was open for 10% -> 0% of each run, Pallas kernels for 0% -> 0%
where the time goes in v1:
time: 86.8 us; the launch traced here: 86.6 us
  Pallas kernels  75.7 us (87%)
  local copies, waits for them, and re-layouts  10.2 us (12%)
    pallas_call x1, Pallas kernels, body(): pl.pallas_call(kernel, out_shape=out_shape, in_specs=in_specs, out_specs=...  75.7 us
    unnamed x43, local copies, waits for them, and re-layouts  10.2 us

profile of v1, /device:TPU:1, one launch (start us, length us, event | category | flops | bytes accessed | tf_op | source)
XLA Modules:
  0.0 86.6 jit_solution(15508783673978467296)
XLA Ops:
  0.7 75.7 %encoder_layer.1 = (bf16[4,128,256]{2,1,0:T(8,128)(2,1)}, f32[4,128,256]{2,1,0:T(8,128)}, f32[2,768]{1,0:T(2,128)}, f32[2]{0:T(128)}, f32[2]{0:T(128)}, /*index=...) custom-call(bf16[4,128,256]{2,1,0:T(8,128)(2,1)} %refs_0_.1, ...), custom_call_target="tpu_custom_call" | custom-call | tf_op jit(solution)/shard_map/encoder_layer/pallas_call | solution.py:796
  76.4 0.0 copy-start
  76.4 1.7 %copy.47 = bf16[4,128,256]{2,1,0:T(8,128)(2,1)} copy(bf16[4,128,256]{2,1,0:T(8,128)(2,1)} %get-tuple-element.30) | data formatting | bytes 524288
  78.1 0.0 copy-done
  78.1 0.0 copy-start.3
  78.1 0.0 copy-start.13
  78.1 0.0 copy-start.12
  78.1 0.0 copy-start.4
  78.1 0.8 copy.48
  78.9 0.0 copy-done.3
  78.9 0.0 copy-start.2
  78.9 0.6 copy.49
  79.5 0.0 copy-done.13
  79.5 0.5 copy.50
  80.0 0.0 copy-done.12
  80.0 0.5 copy.51
  80.5 0.0 copy-done.4
  80.5 0.0 copy-start.11
  80.5 0.6 copy.52
  81.1 0.1 copy-done.11
  81.2 0.0 copy-start.10
  81.2 0.5 copy.53
  81.7 0.2 copy-done.10
  81.9 0.0 copy-start.9
  81.9 0.5 copy.54
  82.4 0.1 copy-done.9
  82.5 0.5 copy.55
  83.0 0.0 copy-done.2
  83.0 0.0 copy-start.8
  83.0 0.0 copy-start.1
  83.0 0.6 copy.56
  83.6 0.1 copy-done.8
  83.7 0.5 copy.57
  84.2 0.0 copy-done.1
  84.2 0.0 copy-start.7
  84.2 0.6 copy.58
  84.8 0.0 copy-done.7
  84.8 0.0 copy-start.6
  84.8 0.5 copy.59
  85.3 0.1 copy-done.6
  85.4 0.0 copy-start.5
  85.4 0.5 copy.60
  85.9 0.1 copy-done.5
  86.1 0.5 copy.61
Async XLA Ops:
  76.4 1.7 %copy-start = (f32[4,128,256]{2,1,0:T(8,128)S(1)}, f32[4,128,256]{2,1,0:T(8,128)}, u32[]{:S(2)}) copy-start(f32[4,128,256]{2,1,0:T(8,128)} %get-tuple-element.31) | copy-start | bytes 1572868
  78.1 0.8 copy-start.3
  78.1 1.4 %copy-start.13 = (f32[2]{0:T(128)S(1)}, f32[2]{0:T(128)}, u32[]{:S(2)}) copy-start(f32[2]{0:T(128)} %get-tuple-element.33) | copy-start | bytes 28
  78.1 1.9 %copy-start.12 = (f32[2]{0:T(128)S(1)}, f32[2]{0:T(128)}, u32[]{:S(2)}) copy-start(f32[2]{0:T(128)} %get-tuple-element.34) | copy-start | bytes 28
  78.1 2.4 %copy-start.4 = (f32[2,256]{1,0:T(2,128)S(1)}, f32[2,256]{1,0:T(2,128)}, u32[]{:S(2)}) copy-start(f32[2,256]{1,0:T(2,128)} %get-tuple-element.35) | copy-start | bytes 6148
  78.9 4.1 %copy-start.2 = (f32[2,2048]{1,0:T(2,128)S(1)}, f32[2,2048]{1,0:T(2,128)}, u32[]{:S(2)}) copy-start(f32[2,2048]{1,0:T(2,128)} %get-tuple-element.39) | copy-start | bytes 49156
  80.5 0.7 copy-start.11
  81.2 0.7 copy-start.10
  81.9 0.6 copy-start.9
  83.0 0.7 copy-start.8
  83.0 1.2 %copy-start.1 = (f32[16,256]{1,0:T(8,128)S(1)}, f32[16,256]{1,0:T(8,128)}, u32[]{:S(2)}) copy-start(f32[16,256]{1,0:T(8,128)} %get-tuple-element.41) | copy-start | bytes 49156
  84.2 0.6 copy-start.7
  84.8 0.6 copy-start.6
  85.4 0.6 copy-start.5

commit v2 on v1

--- a/solution.py
+++ b/solution.py
@@ -14,6 +14,7 @@
 
 D = 256
 HD = 32
+VMEM_LIMIT = 56 * 2**20
 EPSILON = 1e-05
 GELU_SCALE = math.sqrt(2.0 / math.pi)
 SCORE_SCALE = 1.0 / math.sqrt(HD)
@@ -57,12 +58,12 @@
 
 
 SCRATCH = dict(
-    pf=((48, 128), F32),
-    s1=((8, 112, 128), BF16),
+    pf=((64, 128), F32),
+    s1=((8, 128, 128), BF16),
     asmf=((384, 128), F32),
     img=((4, 2, 128, 256), BF16),
     cotb=((4, 128, 256), BF16),
-    wio=((16, 112, 128), BF16),
+    wio=((16, 128, 128), BF16),
     ff=((2, 16, 128, 256), BF16),
     vecs=((16, 256), F32),
     sh=((1024, 256), BF16),
@@ -88,7 +89,6 @@
     dgl=((8, 512, 256), BF16),
     acc=((512, 256), F32),
     lob=((4, 128, 256), BF16),
-    lor=((4, 128, 256), BF16),
     dffn=((512, 256), BF16),
     gp=((2, 16, 128, 256), BF16),
     gs=((16, 128, 256), BF16),
@@ -107,34 +107,37 @@
     dqt=((128, 1024), F32),
     dk=((1024, 128), F32),
     dv=((1024, 128), F32),
-    gio=((16, 80, 128), BF16),
-    q1=((3, 4, 80, 128), BF16),
-    qs2=((4, 80, 128), BF16),
-    q2=((3, 80, 128), BF16),
-    fio=((80, 128), F32),
+    gwo=((16, 32, 128), BF16),
+    wo1=((3, 4, 32, 128), BF16),
+    wos=((4, 32, 128), BF16),
+    wo2=((3, 32, 128), BF16),
+    fwo=((32, 128), F32),
+    gio=((16, 64, 128), BF16),
+    q1=((16, 64, 128), BF16),
+    fio=((64, 128), F32),
     v0=((16, 256), F32),
     vr1=((3, 16, 256), F32),
     v1=((16, 256), F32),
     vr2=((3, 16, 256), F32),
     v2=((16, 256), F32),
-    vr3=((8, 16, 256), F32),
     gt=((4, 2, 128, 256), BF16),
     gtr=((4, 128, 256), BF16),
     gob=((4, 128, 256), BF16),
-    gor=((4, 128, 256), BF16),
     p3f=((8, 48, 128), F32),
     p3=((8, 48, 128), BF16),
-    r3=((8, 48, 128), BF16),
+    p4f=((8, 16, 128), F32),
+    p4=((8, 16, 128), BF16),
 )
 
 SEMS = dict(
-    s1_s=7, s1_r=8, tk_s=3, tk_r=4, tf_s=4, tf_r=4, ct_s=3, ct_r=4,
-    wi_sa=3, wi_sb=12, wi_r=16, wo_sa=3, wo_sb=12, wo_r=16,
+    in_s=17, s1_s=7, s1_r=8, s2_s=7, s2_r=8, tk_s=3, tk_r=4, tf_s=4, tf_r=4, ct_s=3, ct_r=4,
+    wi_s=15, wi_r=16, wo_sa=3, wo_sb=12, wo_r=16,
     ff_sa=3, ff_sb=12, ff_r=16, fw_s=16, fw_r=16,
-    mx_s=1, mx_r=1, dm_s=1, dm_r=1, lo_s=3, lo_r=4, gs_s=1, gs_r=1,
-    r1_s=3, r1_r=3, r2_s=3, r2_r=3, q1_s=3, q1_r=3, q2_s=3, q2_r=3,
+    mx_s=1, mx_r=1, dm_s=1, dm_r=1, lo_s=3, lo_r=4, gs_s=8, gs_r=8,
+    r1_s=3, r1_r=3, r2_s=3, r2_r=3, q1_s=15, q1_r=16,
+    g1_s=3, g1_r=3, g2_s=3, g2_r=3,
     v1_s=3, v1_r=3, v2_s=3, v2_r=3, v3_s=7, v3_r=8,
-    gt_s=1, gt_r=1, go_s=3, go_r=4, p3_s=7, p3_r=8,
+    gt_s=1, gt_r=1, go_s=3, go_r=4, p3_s=7, p3_r=8, p4_s=7, p4_r=8, own_s=5,
 )
 
 INPUTS = (
@@ -145,8 +148,15 @@
     "layer_out", "grad_tokens", "g_w_in", "g_b_q", "g_b_v", "g_w_out", "g_b_out",
     "g_gain1", "g_shift1", "g_w_up", "g_b_up", "g_w_down", "g_b_down", "g_gain2", "g_shift2",
 )
+PACKED = dict(
+    lor=((4, 128, 256), BF16),
+    gor=((4, 128, 256), BF16),
+    r3=((8, 48, 128), BF16),
+    r4=((8, 16, 128), BF16),
+    vr3=((8, 16, 256), F32),
+)
+LOADED = INPUTS[3:]
 SMALL = ("b_q", "b_v", "b_out", "gain1", "shift1", "b_down", "gain2", "shift2")
-G_SMALL = tuple("g_" + name for name in SMALL)
 ROW = {name: row for row, name in enumerate(SMALL)}
 
 
@@ -156,7 +166,8 @@
 
 def kernel(*refs):
     r = Refs()
-    names = INPUTS + OUTPUTS + tuple(SCRATCH) + tuple(SEMS)
+    held = tuple("v_" + name for name in LOADED)
+    names = INPUTS + tuple(PACKED) + held + tuple(SCRATCH) + tuple(SEMS)
     for name, ref in zip(names, refs):
         setattr(r, name, ref)
 
@@ -178,6 +189,9 @@
     def b_peer(step):
         return (group(a, ring(b, step)), gy)
 
+    def gx_peer(step):
+        return (ring(gx, step, 16), gy)
+
     def z_peer(step):
         return (gx, 2 * ring(z, step) + c)
 
@@ -202,53 +216,79 @@
     def await_recv(ref, sem):
         remote(ref, ref, sem, sem, sibling).wait_recv()
 
+    loads = [
+        pltpu.make_async_copy(getattr(r, name), getattr(r, "v_" + name), r.in_s.at[i])
+        for i, name in enumerate(LOADED)
+    ]
+    loads.append(pltpu.make_async_copy(r.tok.at[z], r.img.at[z, c], r.in_s.at[15]))
+    loads.append(pltpu.make_async_copy(r.cot.at[z], r.cotb.at[z], r.in_s.at[16]))
+
     barrier = pltpu.get_barrier_semaphore()
-    peers = [a_peer(k) for k in (1, 2, 3)] + [b_peer(k) for k in (1, 2, 3)]
-    peers += [gy_peer(k) for k in range(1, 8)]
+    peers = [gx_peer(k) for k in range(1, 16)] + [gy_peer(k) for k in range(1, 8)]
     for peer in peers:
         pl.semaphore_signal(barrier, inc=1, device_id=peer, device_id_type=MESH)
-
+    for load in loads:
+        load.start()
+    for load in loads:
+        load.wait()
+
+    rows = r.v_w_in[...].astype(F32)
+    for row in range(2):
+        for k in range(6):
+            at = 6 * row + k
+            r.pf[at : at + 1, :] = rows[row : row + 1, k * 128 : (k + 1) * 128]
     column = 0
-    for ref, chunks in ((r.w_in, 6), (r.w_out, 2), (r.w_up, 16)):
+    for ref, chunks in ((r.v_w_out, 2), (r.v_w_up, 16)):
         rows = ref[...].astype(F32)
         for k in range(chunks):
             for row in range(2):
-                at = row * 24 + column
+                at = 16 + row * 18 + column
                 r.pf[at : at + 1, :] = rows[row : row + 1, k * 128 : (k + 1) * 128]
             column += 1
     lane = iota((1, 256), 1)
     place = 2 * (8 * gx + gy)
     small_rows = []
     for name in SMALL:
-        pair = getattr(r, name)[...].astype(F32).reshape(1, 2)
+        pair = getattr(r, "v_" + name)[...].astype(F32).reshape(1, 2)
         row = jnp.where(lane == place, pair[:, 0:1], 0.0)
         small_rows.append(jnp.where(lane == place + 1, pair[:, 1:2], row))
-    up_bias = r.b_up[...].astype(F32).reshape(1, 16)
+    up_bias = r.v_b_up[...].astype(F32).reshape(1, 16)
     up_place = 128 * lax.rem(gx, 2) + 16 * gy
     up_row = jnp.zeros((1, 256), F32)
     for k in range(16):
         up_row = jnp.where(lane == up_place + k, up_bias[:, k : k + 1], up_row)
     up_rows = jnp.where(iota((8, 256), 0) == lax.div(gx, 2), up_row, 0.0)
     vec_low = jnp.concatenate(small_rows + [up_rows], axis=0).astype(BF16)
-    r.s1[gy, 0:48, :] = r.pf[...].astype(BF16)
-    r.s1[gy, 48:64, :] = r.w_down[:, 0:128]
-    r.s1[gy, 64:80, :] = r.w_down[:, 128:256]
-    r.s1[gy, 80:96, :] = vec_low[:, 0:128]
-    r.s1[gy, 96:112, :] = vec_low[:, 128:256]
-
-    pl.semaphore_wait(barrier, 13)
+    for row in range(2):
+        r.pf[12 + 2 * row : 13 + 2 * row, :] = small_rows[row][:, 0:128]
+        r.pf[13 + 2 * row : 14 + 2 * row, :] = small_rows[row][:, 128:256]
+    r.pf[52:64, :] = jnp.zeros((12, 128), F32)
+    r.s1[gy, 0:64, :] = r.pf[...].astype(BF16)
+    r.s1[gy, 64:80, :] = r.v_w_down[:, 0:128]
+    r.s1[gy, 80:96, :] = r.v_w_down[:, 128:256]
+    r.s1[gy, 96:112, :] = vec_low[:, 0:128]
+    r.s1[gy, 112:128, :] = vec_low[:, 128:256]
+
+    pl.semaphore_wait(barrier, 22)
+
+    def first_part(at):
+        return r.s1.at[at, pl.ds(0, 16)]
+
+    def second_part(at):
+        return r.s1.at[at, pl.ds(16, 112)]
 
     for k in range(1, 8):
         send(lambda k=k: remote(
-            r.s1.at[gy], r.s1.at[gy], r.s1_s.at[k - 1], r.s1_r.at[gy], gy_peer(k)))
+            first_part(gy), first_part(gy), r.s1_s.at[k - 1], r.s1_r.at[gy], gy_peer(k)))
     for k in (1, 2, 3):
         send(lambda k=k: remote(
             r.tok.at[ring(z, k)], r.img.at[z, c], r.tk_s.at[k - 1], r.tk_r.at[z], z_peer(k)))
-    r.img[z, c] = r.tok[z]
+    for k in range(1, 8):
+        send(lambda k=k: remote(
+            second_part(gy), second_part(gy), r.s2_s.at[k - 1], r.s2_r.at[gy], gy_peer(k)))
     send(lambda: remote(r.img.at[z, c], r.img.at[z, c], r.tf_s.at[0], r.tf_r.at[z], sibling))
-    r.cotb[z] = r.cot[z]
-
-    freq = r.freq[...]
+
+    freq = r.v_freq[...]
     even = lax.rem(iota((1, 256), 1), 2) == 0
     fine = iota((32, 256), 0).astype(F32) * freq
     coarse = iota((32, 256), 0).astype(F32) * 32.0 * freq
@@ -259,21 +299,39 @@
 
     for k in range(1, 8):
         at = ring(gy, -k, 8)
-        await_recv(r.s1.at[at], r.s1_r.at[at])
-    vec_sum = jnp.zeros((32, 128), F32)
+        await_recv(first_part(at), r.s1_r.at[at])
+    bias_low, bias_high = jnp.zeros((1, 128), F32), jnp.zeros((1, 128), F32)
+    share0, share1 = (1 - c).astype(F32), c.astype(F32)
     for i in range(8):
-        piece = r.s1[i, 0:48, :].astype(F32)
+        piece = r.s1[i, 0:16, :].astype(F32)
         for row in range(2):
-            r.asmf[pl.ds(2 * i + row, 24, stride=16), :] = piece[row * 24 : row * 24 + 24]
-        vec_sum = vec_sum + r.s1[i, 80:112, :].astype(F32)
+            r.asmf[pl.ds(2 * i + row, 6, stride=16), :] = piece[row * 6 : row * 6 + 6]
+        bias_low = bias_low + piece[12:13] * share0 + piece[13:14] * share1
+        bias_high = bias_high + piece[14:15] * share0 + piece[15:16] * share1
     for k in range(3):
         rows = r.asmf[pl.ds(pl.multiple_of(32 * k + 16 * c, 16), 16), :]
         r.wio[here, 16 * k : 16 * k + 16, :] = rows.astype(BF16)
-    r.wio[here, 48:80, :] = vec_sum.astype(BF16)
-    r.wio[here, 80:112, :] = r.asmf[96:128, :].astype(BF16)
-
-    def block(ref, at, part):
-        return ref.at[at, pl.ds(part[0], part[1])]
+    r.wio[here, 48:64, :] = jnp.concatenate(
+        [bias_low, bias_high, jnp.zeros((14, 128), F32)], axis=0).astype(BF16)
+
+    def wi_view(at):
+        return r.wio.at[at, pl.ds(0, 64)]
+
+    for k in range(1, 16):
+        send(lambda k=k: remote(
+            wi_view(gx), wi_view(gx), r.wi_s.at[k - 1], r.wi_r.at[gx], gx_peer(k)))
+
+    for k in range(1, 8):
+        at = ring(gy, -k, 8)
+        await_recv(second_part(at), r.s2_r.at[at])
+    vec_sum = jnp.zeros((32, 128), F32)
+    for i in range(8):
+        piece = r.s1[i, 16:64, :].astype(F32)
+        for row in range(2):
+            r.asmf[pl.ds(96 + 2 * i + row, 18, stride=16), :] = piece[row * 18 : row * 18 + 18]
+        vec_sum = vec_sum + r.s1[i, 96:128, :].astype(F32)
+    r.wio[here, 64:96, :] = r.asmf[96:128, :].astype(BF16)
+    r.wio[here, 96:128, :] = vec_sum.astype(BF16)
 
     def gather_start(view, sem_a, sem_b, recv):
         for k in (1, 2, 3):
@@ -297,16 +355,11 @@
                 at = group(ring(a, -i), ring(b, -k))
                 await_recv(view(at), recv.at[at])
 
-    def wi_view(at):
-        return r.wio.at[at, pl.ds(0, 80)]
-
     def wo_view(at):
-        return r.wio.at[at, pl.ds(80, 32)]
+        return r.wio.at[at, pl.ds(64, 64)]
 
     def ff_view(at):
         return r.ff.at[c, at]
-
-    gather_start(wi_view, r.wi_sa, r.wi_sb, r.wi_r)
 
     @pl.when(c == 0)
     def _():
@@ -321,7 +374,7 @@
         for i in range(8):
             for half in range(2):
                 r.ff[1, here, 16 * i : 16 * i + 16, 128 * half : 128 * half + 128] = (
-                    r.s1[i, 48 + 16 * half : 64 + 16 * half, :])
+                    r.s1[i, 64 + 16 * half : 80 + 16 * half, :])
 
     gather_start(ff_view, r.ff_sa, r.ff_sb, r.ff_r)
     gather_start(wo_view, r.wo_sa, r.wo_sb, r.wo_r)
@@ -334,8 +387,6 @@
     for k in (1, 2, 3):
         send(lambda k=k: remote(
             r.cot.at[ring(z, k)], r.cotb.at[z], r.ct_s.at[k - 1], r.ct_r.at[z], z_peer(k)))
-
-    gather_relay(wi_view, r.wi_sb, r.wi_r)
 
     for k in range(4):
         at = ring(z, -k)
@@ -355,23 +406,19 @@
     r.sht[...] = r.sh[...].T
     r.imgt[...] = image.T
 
-    gather_wait(wi_view, r.wi_r)
-    vec_sum = jnp.zeros((32, 128), F32)
+    for k in range(1, 16):
+        at = ring(gx, -k, 16)
+        await_recv(wi_view(at), r.wi_r.at[at])
+    biases = jnp.zeros((16, 128), F32)
     for i in range(16):
-        vec_sum = vec_sum + r.wio[i, 48:80, :].astype(F32)
-    r.vecs[:, 0:128] = vec_sum[0:16]
-    r.vecs[:, 128:256] = vec_sum[16:32]
-
-    def own_half(row):
-        both = r.vecs[row : row + 1, :]
-        return both[:, 0:128] * (1 - c).astype(F32) + both[:, 128:256] * c.astype(F32)
+        biases = biases + r.wio[i, 48:64, :].astype(F32)
 
     def w_part(k):
         return r.wio[:, 16 * k : 16 * k + 16, :].reshape(256, 128)
 
-    queries = (dot(r.sh[...], w_part(0)) + own_half(ROW["b_q"])).astype(BF16)
+    queries = (dot(r.sh[...], w_part(0)) + biases[0:1]).astype(BF16)
     keys = dot(r.sh[...], w_part(1)).astype(BF16)
-    values = (dot(image, w_part(2)) + own_half(ROW["b_v"])).astype(BF16)
+    values = (dot(image, w_part(2)) + biases[1:2]).astype(BF16)
     r.qq[...] = queries
     r.kk[...] = keys
     r.vv[...] = values
@@ -418,10 +465,15 @@
     send(lambda: remote(r.mx.at[:, 1 - c], r.mr, r.mx_s.at[0], r.mx_r.at[0], sibling))
 
     gather_wait(wo_view, r.wo_r)
+    vec_sum = jnp.zeros((32, 128), F32)
+    for i in range(16):
+        vec_sum = vec_sum + r.wio[i, 96:128, :].astype(F32)
+    r.vecs[:, 0:128] = vec_sum[0:16]
+    r.vecs[:, 128:256] = vec_sum[16:32]
 
     def w_out_rows(half):
-        low = r.wio[pl.ds(8 * half, 8), 80:96, :].reshape(128, 128)
-        high = r.wio[pl.ds(8 * half, 8), 96:112, :].reshape(128, 128)
+        low = r.wio[pl.ds(8 * half, 8), 64:80, :].reshape(128, 128)
+        high = r.wio[pl.ds(8 * half, 8), 80:96, :].reshape(128, 128)
         return jnp.concatenate([low, high], axis=1)
 
     def vec(name):
@@ -470,7 +522,8 @@
     for k in (1, 2, 3):
         send(lambda k=k: remote(
             r.lob.at[ring(z, k)], r.lor.at[z], r.lo_s.at[k - 1], r.lo_r.at[z], z_peer(k)))
-    r.lor[z] = r.lob[z]
+    own_copies = [pltpu.make_async_copy(r.lob.at[z], r.lor.at[z], r.own_s.at[0])]
+    own_copies[0].start()
 
     for k in (1, 2, 3):
         at = ring(z, -k)
@@ -484,6 +537,14 @@
     r.gv[ROW["b_down"] : ROW["b_down"] + 1, :] = column_sum(d_ffn.astype(F32))
     r.acc[...] = d_second
 
+    def down_send(j):
+        part = pl.ds(2 * j, 2)
+        return remote(r.gp.at[1, part], r.gs.at[part], r.gs_s.at[j], r.gs_r.at[j], sibling)
+
+    def up_send(j):
+        part = pl.ds(pl.multiple_of(16 * j, 16), 16)
+        return remote(r.gp.at[0, :, part], r.gs.at[:, part], r.gs_s.at[j], r.gs_r.at[j], sibling)
+
     def backward_ffn(j, carry):
         d_active = dot_nt(r.dffn[...], down_block(j))
         d_up = (d_active * r.dgl[j].astype(F32)).astype(BF16)
@@ -494,10 +555,18 @@
             g_up.astype(BF16).reshape(16, 16, 256))
         r.gv[pl.ds(8 + j, 1), :] = column_sum(d_up.astype(F32))
         r.acc[...] += dot_nt(d_up, up_block(j))
+
+        @pl.when(c == 0)
+        def _():
+            down_send(j).start()
+
+        @pl.when(c == 1)
+        def _():
+            up_send(j).start()
+
         return carry
 
     lax.fori_loop(0, 8, backward_ffn, 0)
-    send(lambda: remote(r.gp.at[1 - c], r.gs, r.gs_s.at[0], r.gs_r.at[0], sibling))
 
     d_hidden = r.acc[...]
     unit = r.unit1[...]
@@ -518,8 +587,51 @@
         g_out = dot_tn(mixed, d_branch).astype(BF16)
         for i in range(8):
             at = spot(8 * half + i)
-            r.gio[at, 48:64, :] = g_out[16 * i : 16 * i + 16, 0:128]
-            r.gio[at, 64:80, :] = g_out[16 * i : 16 * i + 16, 128:256]
+            r.gwo[at, 0:16, :] = g_out[16 * i : 16 * i + 16, 0:128]
+            r.gwo[at, 16:32, :] = g_out[16 * i : 16 * i + 16, 128:256]
+    r.gv[0:2, :] = jnp.zeros((2, 256), F32)
+    r.v0[...] = r.gv[...]
+
+    @pl.when(c == 0)
+    def _():
+        for j in range(8):
+            part = pl.ds(16 * j, 16)
+            await_recv(r.gs.at[:, part], r.gs_r.at[j])
+            down_send(j).wait_send()
+
+    @pl.when(c == 1)
+    def _():
+        for j in range(8):
+            part = pl.ds(2 * j, 2)
+            await_recv(r.gs.at[part], r.gs_r.at[j])
+            up_send(j).wait_send()
+
+    def add_cores(i, carry):
+        at = group(lax.div(i, 4), lax.rem(i, 4))
+        r.rs[i] = (r.gp[c, at].astype(F32) + r.gs[at].astype(F32)).astype(BF16)
+        return carry
+
+    lax.fori_loop(0, 16, add_cores, 0)
+
+    def first_sum_send(k, i):
+        part, to = pl.ds(4 * ring(a, k), 4), a_peer(k)
+        if i == 0:
+            return remote(r.rs.at[part], r.r1.at[k - 1], r.r1_s.at[k - 1], r.r1_r.at[k - 1], to)
+        if i == 1:
+            return remote(r.gwo.at[part], r.wo1.at[k - 1], r.g1_s.at[k - 1], r.g1_r.at[k - 1], to)
+        return remote(r.v0, r.vr1.at[k - 1], r.v1_s.at[k - 1], r.v1_r.at[k - 1], to)
+
+    def second_sum_send(k, i):
+        part, to = ring(b, k), b_peer(k)
+        if i == 0:
+            return remote(r.s2.at[part], r.r2.at[k - 1], r.r2_s.at[k - 1], r.r2_r.at[k - 1], to)
+        if i == 1:
+            return remote(r.wos.at[part], r.wo2.at[k - 1], r.g2_s.at[k - 1], r.g2_r.at[k - 1], to)
+        return remote(r.v1, r.vr2.at[k - 1], r.v2_s.at[k - 1], r.v2_r.at[k - 1], to)
+
+    for k in (1, 2, 3):
+        for i in range(3):
+            send(lambda k=k, i=i: first_sum_send(k, i))
 
     await_recv(r.dmx.at[:, 1 - c], r.dm_r.at[0])
     d_mixed_t = r.dmx[...].reshape(1024, 128).astype(F32).T
@@ -538,41 +650,27 @@
     r.dk[...] = jnp.zeros((1024, 128), F32)
     r.dv[...] = jnp.zeros((1024, 128), F32)
 
-    def add_siblings():
-        await_recv(r.gs, r.gs_r.at[0])
-
-        def add(i, carry):
-            at = group(lax.div(i, 4), lax.rem(i, 4))
-            r.rs[i] = (r.gp[c, at].astype(F32) + r.gs[at].astype(F32)).astype(BF16)
-            return carry
-
-        lax.fori_loop(0, 16, add, 0)
-        for k in (1, 2, 3):
-            ff_first(k).start()
-
-    def ff_first(k):
-        return remote(
-            r.rs.at[pl.ds(4 * ring(a, k), 4)], r.r1.at[k - 1], r.r1_s.at[k - 1],
-            r.r1_r.at[k - 1], a_peer(k))
-
-    def ff_second(k):
-        return remote(
-            r.s2.at[ring(b, k)], r.r2.at[k - 1], r.r2_s.at[k - 1], r.r2_r.at[k - 1], b_peer(k))
-
     def add_first():
         for k in range(3):
             await_recv(r.r1.at[k], r.r1_r.at[k])
+            await_recv(r.wo1.at[k], r.g1_r.at[k])
+            await_recv(r.vr1.at[k], r.v1_r.at[k])
 
         def add(i, carry):
             total = r.rs[4 * a + i].astype(F32)
+            small = r.gwo[4 * a + i].astype(F32)
             for k in range(3):
                 total = total + r.r1[k, i].astype(F32)
+                small = small + r.wo1[k, i].astype(F32)
             r.s2[i] = total.astype(BF16)
+            r.wos[i] = small.astype(BF16)
             return carry
 
         lax.fori_loop(0, 4, add, 0)
+        r.v1[...] = r.v0[...] + r.vr1[0] + r.vr1[1] + r.vr1[2]
         for k in (1, 2, 3):
-            ff_second(k).start()
+            for i in range(3):
+                second_sum_send(k, i).start()
 
     def backward_head(head, carry):
         lanes = head_lanes(head)
@@ -590,10 +688,6 @@
             r.dk[k : k + 256, :] += dot(r.ds[k : k + 256, :], q_masked)
             r.dv[k : k + 256, :] += dot(r.ee[head, k : k + 256, :], do_masked)
 
-        @pl.when(head == 0)
-        def _():
-            add_siblings()
-
         @pl.when(head == 3)
         def _():
             add_first()
@@ -602,8 +696,8 @@
 
     lax.fori_loop(0, 4, backward_head, 0)
     for k in (1, 2, 3):
-        sent.append(lambda k=k: ff_first(k))
-        sent.append(lambda k=k: ff_second(k))
+        for i in range(3):
+            sent.append(lambda k=k, i=i: second_sum_send(k, i))
 
     d_queries = (r.dqt[...] * SCORE_SCALE).T.astype(BF16)
     d_keys = (r.dk[...] * SCORE_SCALE).astype(BF16)
@@ -611,24 +705,16 @@
     for k, (left, right) in enumerate(((r.sht, d_queries), (r.sht, d_keys), (r.imgt, d_values))):
         g_part = dot(left[...], right).astype(BF16)
         for i in range(16):
-            r.gio[spot(i), 16 * k : 16 * k + 16, :] = g_part[16 * i : 16 * i + 16, :]
-
-    def io_first(k):
-        return remote(
-            r.gio.at[pl.ds(4 * ring(a, k), 4)], r.q1.at[k - 1], r.q1_s.at[k - 1],
-            r.q1_r.at[k - 1], a_peer(k))
-
-    for k in (1, 2, 3):
-        send(lambda k=k: io_first(k))
-    low_half, high_half = (1 - c).astype(F32), c.astype(F32)
-    for name, d_rows in (("b_q", d_queries), ("b_v", d_values)):
-        sums = column_sum(d_rows.astype(F32))
-        r.gv[ROW[name] : ROW[name] + 1, :] = jnp.concatenate(
-            [sums * low_half, sums * high_half], axis=1)
-    r.v0[...] = r.gv[...]
-    for k in (1, 2, 3):
-        send(lambda k=k: remote(
-            r.v0, r.vr1.at[k - 1], r.v1_s.at[k - 1], r.v1_r.at[k - 1], a_peer(k)))
+            r.gio[i, 16 * k : 16 * k + 16, :] = g_part[16 * i : 16 * i + 16, :]
+    ones = jnp.ones((1024, 128), BF16)
+    sums = jnp.where(
+        iota((128, 128), 1) < 64, dot_tn(d_queries, ones), dot_tn(d_values, ones)).astype(BF16)
+    for i in range(8):
+        r.gio[8 * c + i, 48:64, :] = sums[16 * i : 16 * i + 16, :]
+        r.gio[8 * (1 - c) + i, 48:64, :] = jnp.zeros((16, 128), BF16)
+    for k in range(1, 16):
+        send(lambda k=k: remote(
+            r.gio.at[ring(gx, k, 16)], r.q1.at[gx], r.q1_s.at[k - 1], r.q1_r.at[gx], gx_peer(k)))
 
     d_tokens = (
         dot_nt(d_queries, w_part(0)) + dot_nt(d_keys, w_part(1)) + dot_nt(d_values, w_part(2)))
@@ -636,49 +722,18 @@
     send(lambda: remote(r.gt.at[:, 1 - c], r.gtr, r.gt_s.at[0], r.gt_r.at[0], sibling))
 
     for k in range(3):
-        await_recv(r.q1.at[k], r.q1_r.at[k])
-    for i in range(4):
-        total = r.gio[4 * a + i].astype(F32)
-        for k in range(3):
-            total = total + r.q1[k, i].astype(F32)
-        r.qs2[i] = total.astype(BF16)
-    for k in (1, 2, 3):
-        send(lambda k=k: remote(
-            r.qs2.at[ring(b, k)], r.q2.at[k - 1], r.q2_s.at[k - 1], r.q2_r.at[k - 1], b_peer(k)))
-    total = r.v0[...]
-    for k in range(3):
-        await_recv(r.vr1.at[k], r.v1_r.at[k])
-        total = total + r.vr1[k]
-    r.v1[...] = total
-    for k in (1, 2, 3):
-        send(lambda k=k: remote(
-            r.v1, r.vr2.at[k - 1], r.v2_s.at[k - 1], r.v2_r.at[k - 1], b_peer(k)))
-
-    await_recv(r.gtr, r.gt_r.at[0])
-    full = (
-        r.dfirst[...]
-        + r.gt[:, c].reshape(512, 256).astype(F32)
-        + r.gtr[...].reshape(512, 256).astype(F32))
-    r.gob[...] = full.astype(BF16).reshape(4, 128, 256)
-    for k in (1, 2, 3):
-        send(lambda k=k: remote(
-            r.gob.at[ring(z, k)], r.gor.at[z], r.go_s.at[k - 1], r.go_r.at[z], z_peer(k)))
-    r.gor[z] = r.gob[z]
-
-    for k in range(3):
         await_recv(r.r2.at[k], r.r2_r.at[k])
+        await_recv(r.wo2.at[k], r.g2_r.at[k])
+        await_recv(r.vr2.at[k], r.v2_r.at[k])
     total = r.s2[b].astype(F32)
+    small = r.wos[b].astype(F32)
     for k in range(3):
         total = total + r.r2[k].astype(F32)
+        small = small + r.wo2[k].astype(F32)
     r.fin[0] = total[:, 0:128]
     r.fin[1] = total[:, 128:256]
-    for k in range(3):
-        await_recv(r.q2.at[k], r.q2_r.at[k])
-    total = r.qs2[b].astype(F32)
-    for k in range(3):
-        total = total + r.q2[k].astype(F32)
-    r.fio[...] = total
-
+    r.fwo[...] = small
+    r.v2[...] = r.v1[...] + r.vr2[0] + r.vr2[1] + r.vr2[2]
     r.p3f[...] = jnp.zeros((8, 48, 128), F32)
 
     @pl.when(c == 0)
@@ -699,42 +754,86 @@
     for i in range(8):
         for row in range(2):
             at = 32 + 8 * row
-            r.p3f[i, at : at + 5, :] = r.fio[pl.ds(2 * i + row, 5, stride=16), :]
+            r.p3f[i, at : at + 2, :] = r.fwo[pl.ds(2 * i + row, 2, stride=16), :]
     r.p3[...] = r.p3f[...].astype(BF16)
     for k in range(1, 8):
         send(lambda k=k: remote(
             r.p3.at[ring(gy, k, 8)], r.r3.at[gy], r.p3_s.at[k - 1], r.p3_r.at[gy], gy_peer(k)))
-    r.r3[gy] = r.p3[gy]
-
-    total = r.v1[...]
-    for k in range(3):
-        await_recv(r.vr2.at[k], r.v2_r.at[k])
-        total = total + r.vr2[k]
-    r.v2[...] = total
+        send(lambda k=k: remote(
+            r.v2, r.vr3.at[gy], r.v3_s.at[k - 1], r.v3_r.at[gy], gy_peer(k)))
+
+    await_recv(r.gtr, r.gt_r.at[0])
+    full = (
+        r.dfirst[...]
+        + r.gt[:, c].reshape(512, 256).astype(F32)
+        + r.gtr[...].reshape(512, 256).astype(F32))
+    r.gob[...] = full.astype(BF16).reshape(4, 128, 256)
+    for k in (1, 2, 3):
+        send(lambda k=k: remote(
+            r.gob.at[ring(z, k)], r.gor.at[z], r.go_s.at[k - 1], r.go_r.at[z], z_peer(k)))
+
+    total = r.gio[gx].astype(F32)
+    for k in range(1, 16):
+        at = ring(gx, -k, 16)
+        await_recv(r.q1.at[at], r.q1_r.at[at])
+        total = total + r.q1[at].astype(F32)
+    r.fio[...] = total
+    r.p4f[...] = jnp.zeros((8, 16, 128), F32)
+    for i in range(8):
+        for row in range(2):
+            at = 8 * row
+            r.p4f[i, at : at + 4, :] = r.fio[pl.ds(2 * i + row, 4, stride=16), :]
+    r.p4[...] = r.p4f[...].astype(BF16)
     for k in range(1, 8):
         send(lambda k=k: remote(
-            r.v2, r.vr3.at[gy], r.v3_s.at[k - 1], r.v3_r.at[gy], gy_peer(k)))
-    r.vr3[gy] = r.v2[...]
-
+            r.p4.at[ring(gy, k, 8)], r.r4.at[gy], r.p4_s.at[k - 1], r.p4_r.at[gy], gy_peer(k)))
+
+    own_copies += [
+        pltpu.make_async_copy(r.gob.at[z], r.gor.at[z], r.own_s.at[1]),
+        pltpu.make_async_copy(r.p3.at[gy], r.r3.at[gy], r.own_s.at[2]),
+        pltpu.make_async_copy(r.p4.at[gy], r.r4.at[gy], r.own_s.at[3]),
+        pltpu.make_async_copy(r.v2, r.vr3.at[gy], r.own_s.at[4]),
+    ]
+    for copy in own_copies[1:]:
+        copy.start()
     for k in (1, 2, 3):
         at = ring(z, -k)
         await_recv(r.lor.at[at], r.lo_r.at[at])
-    r.layer_out[...] = r.lor[...]
-    for k in (1, 2, 3):
-        at = ring(z, -k)
         await_recv(r.gor.at[at], r.go_r.at[at])
-    r.grad_tokens[...] = r.gor[...].astype(F32)
-
     for k in range(1, 8):
         at = ring(gy, -k, 8)
         await_recv(r.r3.at[at], r.p3_r.at[at])
+        await_recv(r.vr3.at[at], r.v3_r.at[at])
+        await_recv(r.r4.at[at], r.p4_r.at[at])
+    for copy in own_copies:
+        copy.wait()
+    for make in sent:
+        make().wait_send()
+
+
+def unpack(*refs):
+    r = Refs()
+    for name, ref in zip(tuple(PACKED) + OUTPUTS, refs):
+        setattr(r, name, ref)
+    gx, gy = lax.axis_index("gx"), lax.axis_index("gy")
+    place = 2 * (8 * gx + gy)
+    up_place = 128 * lax.rem(gx, 2) + 16 * gy
+    r.layer_out[...] = r.lor[...]
+    r.grad_tokens[...] = r.gor[...].astype(F32)
     core0 = jnp.zeros((48, 128), F32)
     core1 = jnp.zeros((48, 128), F32)
+    into0 = jnp.zeros((16, 128), F32)
+    into1 = jnp.zeros((16, 128), F32)
+    total = jnp.zeros((16, 256), F32)
     for i in range(4):
         core0 = core0 + r.r3[2 * i].astype(F32)
         core1 = core1 + r.r3[2 * i + 1].astype(F32)
+        into0 = into0 + r.r4[2 * i].astype(F32)
+        into1 = into1 + r.r4[2 * i + 1].astype(F32)
+        total = total + r.vr3[2 * i] + r.vr3[2 * i + 1]
     r.g_w_down[:, 0:128] = core1[0:16]
     r.g_w_down[:, 128:256] = core1[16:32]
+    w_out = core0 + core1
     for row in range(2):
         out_row = slice(row, row + 1)
         for j in range(8):
@@ -742,32 +841,26 @@
                 at = 16 * half + 8 * row + j
                 lanes = 256 * j + 128 * half
                 r.g_w_up[out_row, lanes : lanes + 128] = core0[at : at + 1]
-        base = 32 + 8 * row
         for k in range(3):
-            at = base + k
-            r.g_w_in[out_row, 256 * k : 256 * k + 128] = core0[at : at + 1]
-            r.g_w_in[out_row, 256 * k + 128 : 256 * k + 256] = core1[at : at + 1]
-        both = core0 + core1
-        r.g_w_out[out_row, 0:128] = both[base + 3 : base + 4]
-        r.g_w_out[out_row, 128:256] = both[base + 4 : base + 5]
-
-    for k in range(1, 8):
-        at = ring(gy, -k, 8)
-        await_recv(r.vr3.at[at], r.v3_r.at[at])
-    total = jnp.zeros((16, 256), F32)
-    for i in range(8):
-        total = total + r.vr3[i]
+            at = 8 * row + k
+            r.g_w_in[out_row, 256 * k : 256 * k + 128] = into0[at : at + 1]
+            r.g_w_in[out_row, 256 * k + 128 : 256 * k + 256] = into1[at : at + 1]
+        at = 32 + 8 * row
+        r.g_w_out[out_row, 0:128] = w_out[at : at + 1]
+        r.g_w_out[out_row, 128:256] = w_out[at + 1 : at + 2]
+    biases = into0 + into1
+    for name, lane in (("b_q", 0), ("b_v", 64)):
+        pair = jnp.concatenate(
+            [biases[3:4, lane : lane + 1], biases[11:12, lane : lane + 1]], axis=1)
+        getattr(r, "g_" + name)[...] = pair.reshape(2)
     moved = pltpu.roll(total, lax.rem(256 - place, 256), axis=1)
-    for name in SMALL:
+    for name in SMALL[2:]:
         row = ROW[name]
         getattr(r, "g_" + name)[...] = moved[row : row + 1, 0:2].reshape(2)
     up_total = column_sum(jnp.where(iota((8, 256), 0) == lax.div(gx, 2), total[8:16], 0.0))
     up_total = jnp.broadcast_to(up_total, (8, 256))
     up_total = pltpu.roll(up_total, lax.rem(256 - up_place, 256), axis=1)
     r.g_b_up[...] = up_total[0:1, 0:16].reshape(16)
-
-    for make in sent:
-        make().wait_send()
 
 
 def body(
@@ -781,28 +874,38 @@
         b_q, b_v, b_out, gain_first, shift_first, b_down, gain_second, shift_second, b_up,
     )
     vmem = pl.BlockSpec(memory_space=pltpu.VMEM)
-    in_specs = [vmem] * len(args)
+    anywhere = pl.BlockSpec(memory_space=pl.ANY)
+    in_specs = [anywhere] * len(args)
     in_specs[2] = pl.BlockSpec(memory_space=pltpu.SMEM)
     shape = jax.ShapeDtypeStruct
     vector = shape((2,), F32)
+    scratch = [pltpu.VMEM(args[INPUTS.index(name)].shape, args[INPUTS.index(name)].dtype)
+               for name in LOADED]
+    scratch += [pltpu.VMEM(dims, kind) for dims, kind in SCRATCH.values()]
+    scratch += [pltpu.SemaphoreType.DMA((count,)) for count in SEMS.values()]
+    packed = pl.pallas_call(
+        kernel,
+        out_shape=tuple(shape(dims, kind) for dims, kind in PACKED.values()),
+        in_specs=in_specs,
+        out_specs=tuple([anywhere] * len(PACKED)),
+        scratch_shapes=scratch,
+        compiler_params=pltpu.CompilerParams(
+            collective_id=0, has_side_effects=True, vmem_limit_bytes=VMEM_LIMIT),
+        name="encoder_layer",
+    )(*args)
     out_shape = (
         shape((4, 128, 256), BF16), shape((4, 128, 256), F32), shape((2, 768), F32),
         vector, vector, shape((2, 256), F32), vector, vector, vector,
         shape((2, 2048), F32), shape((16,), F32), shape((16, 256), F32),
         vector, vector, vector,
     )
-    scratch = [pltpu.VMEM(dims, kind) for dims, kind in SCRATCH.values()]
-    scratch += [pltpu.SemaphoreType.DMA((count,)) for count in SEMS.values()]
     return pl.pallas_call(
-        kernel,
+        unpack,
         out_shape=out_shape,
-        in_specs=in_specs,
+        in_specs=[vmem] * len(packed),
         out_specs=tuple([vmem] * len(out_shape)),
-        scratch_shapes=scratch,
-        compiler_params=pltpu.CompilerParams(
-            collective_id=0, has_side_effects=True, vmem_limit_bytes=62 * 2**20),
-        name="encoder_layer",
-    )(*args)
+        name="unpack_results",
+    )(*packed)
 
 
 def solution(mesh):

time: 86.8 us -> 76.6 us (0.88)
  local copies, waits for them, and re-layouts: 10.2 us -> 0 us
    unnamed x43 -> x0, local copies, waits for them, and re-layouts: 10.2 us -> none
    pallas_call x1 -> x2, Pallas kernels: 75.7 us -> 75.7 us  [the longest x1 73.6 us: body(): pl.pallas_call(kernel, out_shape=tuple((shape(dims, kind) for dims, kind...]
where the time goes in v2:
time: 76.6 us; the launch traced here: 76.4 us
  Pallas kernels  75.7 us (99%)
    pallas_call x1, Pallas kernels, body(): pl.pallas_call(kernel, out_shape=tuple((shape(dims, kind) for dims, kind...  73.6 us
    pallas_call x1, Pallas kernels, body(): pl.pallas_call(unpack, out_shape=out_shape, in_specs=[vmem] * len(packed)...  2.15 us

profile of v2, /device:TPU:1, one launch (start us, length us, event | category | flops | bytes accessed | tf_op | source)
XLA Modules:
  0.0 76.4 jit_solution(6412165206698689148)
XLA Ops:
  0.7 73.6 %encoder_layer.1 = (bf16[4,128,256]{2,1,0:T(8,128)(2,1)}, bf16[4,128,256]{2,1,0:T(8,128)(2,1)}, bf16[8,48,128]{2,1,0:T(8,128)(2,1)}, bf16[8,16,128]{2,1,0:T(8,128)(2,1)}, f32[8,16,256]{2,1,0:T(8,128)}) custom-call(bf16[4,128,256]{2,1,0:T(8,128)(2,1)} %refs_0_.1, bf16[4,128,256]{2,1,0:T(8,128)(2,1)} %refs_1_.1, s32[4]{0:T(128)} %refs_2_.1, ...), custom_call_target="tpu_custom_call" | custom-call | tf_op jit(solution)/shard_map/encoder_layer/pallas_call | solution.py:886
  74.2 2.2 %unpack_results.1 = (bf16[4,128,256]{2,1,0:T(8,128)(2,1)}, f32[4,128,256]{2,1,0:T(8,128)}, f32[2,768]{1,0:T(2,128)}, f32[2]{0:T(128)}, f32[2]{0:T(128)}, /*index...) custom-call(bf16[4,128,256]{2,1,0:T(8,128)(2,1)} %get-tuple-element., ...), custom_call_target="tpu_custom_call" | custom-call | tf_op jit(solution)/shard_map/unpack_results/pallas_call | solution.py:902

commit v3 on v2

v3 whole, which is shorter than its diff:
```python
import math

import jax
import jax.numpy as jnp
import numpy as np
from jax import lax
from jax.experimental import pallas as pl
from jax.experimental.pallas import tpu as pltpu
from jax.sharding import PartitionSpec as P

MESH = pl.DeviceIdType.MESH
F32 = jnp.float32
BF16 = jnp.bfloat16

D = 256
HD = 32
VMEM_LIMIT = 56 * 2**20
EPSILON = 1e-05
GELU_SCALE = math.sqrt(2.0 / math.pi)
SCORE_SCALE = 1.0 / math.sqrt(HD)
EXP2_SCALE = SCORE_SCALE * math.log2(math.e)


def dot(left, right):
    return jnp.dot(left, right, preferred_element_type=F32)


def dot_nt(left, right):
    return lax.dot_general(left, right, (((1,), (1,)), ((), ())), preferred_element_type=F32)


def dot_tn(left, right):
    return lax.dot_general(left, right, (((0,), (0,)), ((), ())), preferred_element_type=F32)


def iota(shape, dim):
    return lax.broadcasted_iota(jnp.int32, shape, dim)


def column_sum(values):
    return jnp.sum(values, axis=0, keepdims=True)


def norm_forward(values, gain, shift):
    centre = jnp.mean(values, axis=-1, keepdims=True)
    moved = values - centre
    spread = jnp.mean(moved * moved, axis=-1, keepdims=True)
    inverse = lax.rsqrt(spread + EPSILON)
    unit = moved * inverse
    return unit * gain + shift, unit, inverse


def norm_backward(d_out, unit, inverse, gain):
    d_unit = d_out * gain
    mean_d = jnp.mean(d_unit, axis=-1, keepdims=True)
    mean_du = jnp.mean(d_unit * unit, axis=-1, keepdims=True)
    return inverse * (d_unit - mean_d - unit * mean_du)


SCRATCH = dict(
    pf=((112, 128), F32),
    s1=((8, 112, 128), BF16),
    asmf=((384, 128), F32),
    img=((4, 2, 128, 256), BF16),
    cotb=((4, 128, 256), BF16),
    wio=((16, 112, 128), BF16),
    ff=((2, 16, 128, 256), BF16),
    vecs=((16, 256), F32),
    sh=((1024, 256), BF16),
    sht=((256, 1024), BF16),
    imgt=((256, 1024), BF16),
    kx=((4, 1024, 256), BF16),
    vx=((4, 1024, 256), BF16),
    qm=((4, 1024, 128), BF16),
    vv=((1024, 128), BF16),
    qq=((1024, 128), BF16),
    kt=((128, 1024), BF16),
    vt=((128, 1024), BF16),
    qt=((256, 1024), BF16),
    ee=((4, 1024, 1024), BF16),
    ot=((128, 1024), F32),
    ri=((8, 1024), F32),
    mx=((4, 2, 128, 128), BF16),
    mr=((4, 128, 128), BF16),
    hid=((512, 256), F32),
    hlow=((512, 256), BF16),
    hlt=((256, 512), BF16),
    unit1=((512, 256), F32),
    inv1=((512, 1), F32),
    act=((4, 512, 512), BF16),
    dgl=((4, 512, 512), BF16),
    acc=((512, 256), F32),
    lob=((4, 128, 256), BF16),
    dffn=((512, 256), BF16),
    gp=((2, 16, 128, 256), BF16),
    gs=((16, 128, 256), BF16),
    rs=((16, 128, 256), BF16),
    r1=((3, 4, 128, 256), BF16),
    s2=((4, 128, 256), BF16),
    r2=((3, 128, 256), BF16),
    fin=((2, 128, 128), F32),
    gv=((16, 256), F32),
    dfirst=((512, 256), F32),
    dms=((4, 128, 128), BF16),
    dmx=((4, 2, 128, 128), BF16),
    dot_=((256, 1024), BF16),
    doo=((1024, 128), BF16),
    ds=((2, 1024, 1024), BF16),
    dqt=((128, 1024), F32),
    dk=((1024, 128), F32),
    dv=((1024, 128), F32),
    gwo=((16, 32, 128), BF16),
    wo1=((3, 4, 32, 128), BF16),
    wos=((4, 32, 128), BF16),
    wo2=((3, 32, 128), BF16),
    fwo=((32, 128), F32),
    gio=((16, 64, 128), BF16),
    q1=((16, 64, 128), BF16),
    fio=((64, 128), F32),
    v0=((16, 256), F32),
    vr1=((3, 16, 256), F32),
    v1=((16, 256), F32),
    vr2=((3, 16, 256), F32),
    v2=((16, 256), F32),
    gt=((4, 2, 128, 256), BF16),
    gtr=((4, 128, 256), BF16),
    gob=((4, 128, 256), BF16),
    p3f=((8, 48, 128), F32),
    p3=((8, 48, 128), BF16),
    p4f=((8, 16, 128), F32),
    p4=((8, 16, 128), BF16),
)

GROUPS = (
    "s1", "s2", "tk", "tf", "ct", "wi", "wa", "wb", "fa", "fb", "fc", "fw", "mx", "dm", "lo",
    "gs", "r1", "r2", "g1", "g2", "v1", "v2", "v3", "q1", "gt", "go", "p3", "p4",
)
SEMS = dict(in_s=16, own_s=5, tk_r=3)
for group_name in GROUPS:
    SEMS.setdefault(group_name + "_s", 1)
    SEMS.setdefault(group_name + "_r", 1)

INPUTS = (
    "tok", "cot", "lens", "freq", "w_in", "w_out", "w_up", "w_down",
    "b_q", "b_v", "b_out", "gain1", "shift1", "b_down", "gain2", "shift2", "b_up",
)
OUTPUTS = (
    "layer_out", "grad_tokens", "g_w_in", "g_b_q", "g_b_v", "g_w_out", "g_b_out",
    "g_gain1", "g_shift1", "g_w_up", "g_b_up", "g_w_down", "g_b_down", "g_gain2", "g_shift2",
)
PACKED = dict(
    lor=((4, 128, 256), BF16),
    gor=((4, 128, 256), BF16),
    r3=((8, 48, 128), BF16),
    r4=((8, 16, 128), BF16),
    vr3=((8, 16, 256), F32),
)
LOADED = INPUTS[3:]
SMALL = ("b_q", "b_v", "b_out", "gain1", "shift1", "b_down", "gain2", "shift2")
ROW = {name: row for row, name in enumerate(SMALL)}


class Refs:
    pass


def kernel(*refs):
    r = Refs()
    held = tuple("v_" + name for name in LOADED)
    names = INPUTS + tuple(PACKED) + held + tuple(SCRATCH) + tuple(SEMS)
    for name, ref in zip(names, refs):
        setattr(r, name, ref)

    gx, gy = lax.axis_index("gx"), lax.axis_index("gy")
    x, y = lax.div(gx, 4), lax.rem(gx, 4)
    z, c = lax.div(gy, 2), lax.rem(gy, 2)
    a = x * (1 - c) + y * c
    b = y * (1 - c) + x * c

    def group(a_at, b_at):
        return a_at * (4 - 3 * c) + b_at * (1 + 3 * c)

    def ring(at, step, size=4):
        return lax.rem(at + (step % size), size)

    def a_peer(step):
        return (group(ring(a, step), b), gy)

    def b_peer(step):
        return (group(a, ring(b, step)), gy)

    def gx_peer(step):
        return (ring(gx, step, 16), gy)

    def z_peer(step):
        return (gx, 2 * ring(z, step) + c)

    def gy_peer(step):
        return (gx, ring(gy, step, 8))

    sibling = (gx, 2 * z + 1 - c)
    here = group(a, b)

    def remote(src, dst, send, recv, device):
        return pltpu.make_async_remote_copy(
            src_ref=src, dst_ref=dst, send_sem=send, recv_sem=recv,
            device_id=device, device_id_type=MESH,
        )

    closing = []

    def sem(name):
        return getattr(r, name).at[0]

    def copy_to(name, src, dst, device, recv=None):
        return remote(src, dst, sem(name + "_s"), recv or sem(name + "_r"), device)

    def sends_end(name, ref):
        closing.append(lambda: remote(ref, ref, sem(name + "_s"), sem(name + "_s"), sibling))

    def await_recv(name, ref, at=0):
        done = getattr(r, name + "_r").at[at]
        remote(ref, ref, done, done, sibling).wait_recv()

    loads = [
        pltpu.make_async_copy(getattr(r, name), getattr(r, "v_" + name), r.in_s.at[i])
        for i, name in enumerate(LOADED)
    ]
    loads.append(pltpu.make_async_copy(r.tok.at[z], r.img.at[z, c], r.in_s.at[14]))
    loads.append(pltpu.make_async_copy(r.cot.at[z], r.cotb.at[z], r.in_s.at[15]))

    barrier = pltpu.get_barrier_semaphore()
    peers = [gx_peer(k) for k in range(1, 16)] + [gy_peer(k) for k in range(1, 8)]
    for peer in peers:
        pl.semaphore_signal(barrier, inc=1, device_id=peer, device_id_type=MESH)
    for load in loads:
        load.start()
    for load in loads:
        load.wait()

    rows = r.v_w_in[...].astype(F32)
    for row in range(2):
        for k in range(6):
            at = 6 * row + k
            r.pf[at : at + 1, :] = rows[row : row + 1, k * 128 : (k + 1) * 128]
    lane = iota((1, 256), 1)
    place = 2 * (8 * gx + gy)
    for i, name in enumerate(("b_q", "b_v")):
        pair = getattr(r, "v_" + name)[...].astype(F32).reshape(1, 2)
        row = jnp.where(lane == place, pair[:, 0:1], 0.0)
        row = jnp.where(lane == place + 1, pair[:, 1:2], row)
        r.pf[12 + 2 * i : 13 + 2 * i, :] = row[:, 0:128]
        r.pf[13 + 2 * i : 14 + 2 * i, :] = row[:, 128:256]
    r.s1[gy, 0:16, :] = r.pf[0:16, :].astype(BF16)

    rows = r.v_w_out[...].astype(F32)
    r.pf[16:32, :] = jnp.zeros((16, 128), F32)
    for row in range(2):
        for k in range(2):
            at = 16 + 2 * row + k
            r.pf[at : at + 1, :] = rows[row : row + 1, k * 128 : (k + 1) * 128]
    thin = iota((1, 128), 1)
    packed = jnp.zeros((1, 128), F32)
    for i, name in enumerate(SMALL):
        pair = getattr(r, "v_" + name)[...].astype(F32).reshape(1, 2)
        packed = jnp.where(thin == 2 * i, pair[:, 0:1], packed)
        packed = jnp.where(thin == 2 * i + 1, pair[:, 1:2], packed)
    up_bias = r.v_b_up[...].astype(F32).reshape(1, 16)
    for k in range(16):
        packed = jnp.where(thin == 16 + k, up_bias[:, k : k + 1], packed)
    r.pf[20:21, :] = packed
    rows = r.v_w_up[...].astype(F32)
    for row in range(2):
        for k in range(16):
            at = 32 + 16 * row + k
            r.pf[at : at + 1, :] = rows[row : row + 1, k * 128 : (k + 1) * 128]
    r.s1[gy, 16:64, :] = r.pf[16:64, :].astype(BF16)
    r.s1[gy, 64:80, :] = r.v_w_down[:, 0:128]
    r.s1[gy, 80:96, :] = r.v_w_down[:, 128:256]
    r.s1[gy, 96:112, :] = r.pf[16:32, :].astype(BF16)

    pl.semaphore_wait(barrier, 22)

    def first_part(at):
        return r.s1.at[at, pl.ds(0, 16)]

    def second_part(at, core):
        return r.s1.at[at, pl.ds(pl.multiple_of(16 + 48 * core, 16), 48)]

    for k in range(1, 8):
        copy_to("s1", first_part(gy), first_part(gy), gy_peer(k)).start()
    sends_end("s1", r.s1.at[pl.ds(0, 7), pl.ds(0, 16)])
    for k in (1, 2, 3):
        copy_to("tk", r.tok.at[ring(z, k)], r.img.at[z, c], z_peer(k), r.tk_r.at[k - 1]).start()
    sends_end("tk", r.cotb.at[pl.ds(0, 3)])
    for k in range(1, 8):
        part = second_part(gy, lax.rem(gy + k, 2))
        copy_to("s2", part, part, gy_peer(k)).start()
    sends_end("s2", r.s1.at[pl.ds(0, 7), pl.ds(0, 48)])
    copy_to("tf", r.img.at[z, c], r.img.at[z, c], sibling).start()

    freq = r.v_freq[...]
    even = lax.rem(iota((1, 256), 1), 2) == 0
    fine = iota((32, 256), 0).astype(F32) * freq
    coarse = iota((32, 256), 0).astype(F32) * 32.0 * freq
    sin_f, cos_f = jnp.sin(fine), jnp.cos(fine)
    sin_c, cos_c = jnp.sin(coarse), jnp.cos(coarse)
    first_c = jnp.where(even, sin_c, cos_c)
    second_c = jnp.where(even, cos_c, -sin_c)

    await_recv("s1", r.s1.at[pl.ds(0, 7), pl.ds(0, 16)])
    bias_low, bias_high = jnp.zeros((1, 128), F32), jnp.zeros((1, 128), F32)
    share0, share1 = (1 - c).astype(F32), c.astype(F32)
    for i in range(8):
        piece = r.s1[i, 0:16, :].astype(F32)
        for row in range(2):
            r.asmf[pl.ds(2 * i + row, 6, stride=16), :] = piece[row * 6 : row * 6 + 6]
        bias_low = bias_low + piece[12:13] * share0 + piece[13:14] * share1
        bias_high = bias_high + piece[14:15] * share0 + piece[15:16] * share1
    for k in range(3):
        rows = r.asmf[pl.ds(pl.multiple_of(32 * k + 16 * c, 16), 16), :]
        r.wio[here, 16 * k : 16 * k + 16, :] = rows.astype(BF16)
    r.wio[here, 48:64, :] = jnp.concatenate(
        [bias_low, bias_high, jnp.zeros((14, 128), F32)], axis=0).astype(BF16)

    def wi_view(at):
        return r.wio.at[at, pl.ds(0, 64)]

    for k in range(1, 16):
        copy_to("wi", wi_view(gx), wi_view(gx), gx_peer(k)).start()
    sends_end("wi", r.wio.at[pl.ds(0, 15), pl.ds(0, 64)])

    await_recv("s2", r.s1.at[pl.ds(0, 7), pl.ds(0, 48)])

    def wo_view(at):
        return r.wio.at[at, pl.ds(64, 48)]

    def ff_view(at):
        return r.ff.at[c, at]

    @pl.when(c == 0)
    def _():
        for i in range(8):
            piece = r.s1[i, 32:64, :].astype(F32)
            for row in range(2):
                r.asmf[pl.ds(128 + 2 * i + row, 16, stride=16), :] = (
                    piece[16 * row : 16 * row + 16])
        for j in range(8):
            for half in range(2):
                at = 128 + 16 * (2 * j + half)
                r.ff[0, here, 16 * j : 16 * j + 16, 128 * half : 128 * half + 128] = (
                    r.asmf[at : at + 16, :].astype(BF16))

    @pl.when(c == 1)
    def _():
        for i in range(8):
            for half in range(2):
                r.ff[1, here, 16 * i : 16 * i + 16, 128 * half : 128 * half + 128] = (
                    r.s1[i, 64 + 16 * half : 80 + 16 * half, :])

    for k in (1, 2, 3):
        copy_to("fa", ff_view(here), ff_view(here), a_peer(k)).start()
    for k in (1, 2, 3):
        copy_to("fb", ff_view(here), ff_view(here), b_peer(k)).start()

    r.asmf[96:112, :] = jnp.zeros((16, 128), F32)
    shared_at = pl.multiple_of(16 + 80 * c, 16)
    for i in range(8):
        piece = r.s1[i, pl.ds(shared_at, 16), :].astype(F32)
        for row in range(2):
            r.asmf[pl.ds(64 + 2 * i + row, 2, stride=16), :] = piece[2 * row : 2 * row + 2]
        r.asmf[96 + i : 97 + i, :] = piece[4:5]
    r.wio[here, 64:112, :] = r.asmf[64:112, :].astype(BF16)
    for k in (1, 2, 3):
        copy_to("wa", wo_view(here), wo_view(here), a_peer(k)).start()
    for k in (1, 2, 3):
        copy_to("wb", wo_view(here), wo_view(here), b_peer(k)).start()

    for k in (1, 2, 3):
        at = ring(z, -k)
        await_recv("tk", r.img.at[at, c], k - 1)
        copy_to("tf", r.img.at[at, c], r.img.at[at, c], sibling).start()
    sends_end("tf", r.img.at[:, 0])
    for k in (1, 2, 3):
        copy_to("ct", r.cot.at[ring(z, k)], r.cotb.at[z], z_peer(k)).start()
    sends_end("ct", r.cotb.at[pl.ds(0, 3)])
    await_recv("tf", r.img.at[:, 1 - c])

    for i in range(8):
        rows = r.img[i // 2, i % 2].astype(F32)
        for k in range(4):
            at = 4 * i + k
            pos = first_c[at : at + 1] * cos_f + second_c[at : at + 1] * sin_f
            r.sh[32 * at : 32 * at + 32, :] = (rows[32 * k : 32 * k + 32] + pos).astype(BF16)
    image = r.img[...].reshape(1024, 256)

    await_recv("fa", r.ff.at[c, pl.ds(0, 3)])
    for i in (1, 2, 3):
        at = group(ring(a, -i), b)
        for k in (1, 2, 3):
            copy_to("fc", ff_view(at), ff_view(at), b_peer(k)).start()
    for i in range(4):
        at = group(ring(a, -i), b)
        copy_to("fw", ff_view(at), ff_view(at), sibling).start()
    await_recv("wa", r.wio.at[pl.ds(0, 3), pl.ds(64, 48)])
    for i in (1, 2, 3):
        at = group(ring(a, -i), b)
        for k in (1, 2, 3):
            copy_to("wb", wo_view(at), wo_view(at), b_peer(k)).start()
    sends_end("fa", r.ff.at[c, pl.ds(0, 3)])
    sends_end("fb", r.ff.at[c, pl.ds(0, 3)])
    sends_end("fc", r.ff.at[c, pl.ds(0, 9)])
    sends_end("fw", r.ff.at[c])
    sends_end("wa", r.wio.at[pl.ds(0, 3), pl.ds(64, 48)])
    sends_end("wb", r.wio.at[pl.ds(0, 12), pl.ds(64, 48)])

    r.sht[...] = r.sh[...].T
    r.imgt[...] = image.T

    await_recv("wi", r.wio.at[pl.ds(0, 15), pl.ds(0, 64)])
    biases = jnp.zeros((16, 128), F32)
    for i in range(16):
        biases = biases + r.wio[i, 48:64, :].astype(F32)

    def w_part(k):
        return r.wio[:, 16 * k : 16 * k + 16, :].reshape(256, 128)

    queries = (dot(r.sh[...], w_part(0)) + biases[0:1]).astype(BF16)
    keys = dot(r.sh[...], w_part(1)).astype(BF16)
    values = (dot(image, w_part(2)) + biases[1:2]).astype(BF16)
    r.qq[...] = queries
    r.vv[...] = values
    r.kt[...] = keys.T
    r.vt[...] = values.T
    r.qt[0:128, :] = queries.T
    ones_row = iota((128, 1024), 0) == 0
    r.qt[128:256, :] = jnp.where(ones_row, 1.0, 0.0).astype(BF16)

    length = r.lens[z]

    zero = jnp.zeros((), BF16)
    head_of_lane = lax.div(iota((1024, 128), 1), HD)
    hidden_key = (iota((1024, 128), 0) >= length) & (iota((1024, 128), 1) == 0)
    bias = jnp.where(hidden_key, -1e30, 0.0).astype(BF16)
    for head in range(4):
        r.kx[head, :, 0:128] = jnp.where(head_of_lane == head, keys, zero)
        r.kx[head, :, 128:256] = bias

    for head in range(4):
        peak = None
        for k in range(0, 1024, 512):
            part = jnp.max(dot(r.kx[head, k : k + 512, :], r.qt[...]), axis=0, keepdims=True)
            peak = part if peak is None else jnp.maximum(peak, part)
        scores = dot(r.kx[head], r.qt[...])
        weights = jnp.exp2(scores * EXP2_SCALE - peak * EXP2_SCALE).astype(BF16)
        r.ee[head] = weights
        rows = slice(head * HD, head * HD + HD)
        left = jnp.concatenate([r.vt[rows, :], jnp.ones((16, 1024), BF16)], axis=0)
        mixed = dot(left, weights)
        inverse = 1.0 / mixed[HD : HD + 1]
        r.ot[rows, :] = mixed[0:HD] * inverse
        r.ri[head : head + 1, :] = inverse
        if head == 2:
            await_recv("fb", r.ff.at[c, pl.ds(0, 3)])
            for k in (1, 2, 3):
                at = group(a, ring(b, -k))
                copy_to("fw", ff_view(at), ff_view(at), sibling).start()

    r.mx[...] = r.ot[...].T.astype(BF16).reshape(4, 2, 128, 128)
    copy_to("mx", r.mx.at[:, 1 - c], r.mr, sibling).start()
    sends_end("mx", r.mr)

    await_recv("fc", r.ff.at[c, pl.ds(0, 9)])
    for i in (1, 2, 3):
        for k in (1, 2, 3):
            at = group(ring(a, -i), ring(b, -k))
            copy_to("fw", ff_view(at), ff_view(at), sibling).start()

    await_recv("wb", r.wio.at[pl.ds(0, 12), pl.ds(64, 48)])
    rows = r.wio[:, 96:112, :].reshape(256, 128)
    spot_row, spot_lane = iota((256, 256), 0), iota((256, 256), 1)
    pick = spot_row == 16 * lax.div(spot_lane, 16) + lax.div(lax.rem(spot_lane, 16), 2)
    spread = dot_tn(rows, jnp.where(pick, 1.0, 0.0).astype(BF16))
    even_lane = lax.rem(iota((1, 256), 1), 2) == 0
    for i in range(8):
        r.vecs[i : i + 1, :] = jnp.where(
            even_lane, spread[2 * i : 2 * i + 1], spread[2 * i + 1 : 2 * i + 2])
    tile = iota((128, 256), 0) == 16 + lax.rem(iota((128, 256), 1), 16)
    wide = dot(rows, jnp.where(tile, 1.0, 0.0).astype(BF16))
    keep = lax.rem(spot_row, 32) == (
        16 * lax.div(spot_lane, 128) + lax.rem(lax.div(spot_lane, 16), 8))
    wide = jnp.where(keep, wide, 0.0).reshape(8, 32, 256)
    r.vecs[8:16, :] = jnp.sum(wide, axis=1)

    for head in range(4):
        r.vx[head, :, 0:128] = jnp.where(head_of_lane == head, r.vv[...], zero)
        r.vx[head, :, 128:256] = jnp.where(
            lax.div(iota((1024, 128), 1), 2) == head, 1.0, 0.0).astype(BF16)
        r.qm[head] = jnp.where(head_of_lane == head, r.qq[...], zero)

    def w_out_rows(half):
        low = r.wio[pl.ds(8 * half, 8), 64:80, :].reshape(128, 128)
        high = r.wio[pl.ds(8 * half, 8), 80:96, :].reshape(128, 128)
        return jnp.concatenate([low, high], axis=1)

    def vec(name):
        return r.vecs[ROW[name] : ROW[name] + 1, :]

    mixed_own = r.mx[:, c].reshape(512, 128)
    branch = dot(mixed_own, w_out_rows(c))
    await_recv("mx", r.mr)
    mixed_other = r.mr[...].reshape(512, 128)
    branch = branch + dot(mixed_other, w_out_rows(1 - c))
    first_sum = r.img[:, c].reshape(512, 256).astype(F32) + branch + vec("b_out")
    hidden, unit, inverse = norm_forward(first_sum, vec("gain1"), vec("shift1"))
    r.unit1[...] = unit
    r.inv1[...] = inverse
    r.hid[...] = hidden
    hidden_low = hidden.astype(BF16)
    r.hlow[...] = hidden_low
    r.hlt[...] = hidden_low.T

    await_recv("fw", r.ff.at[1 - c])

    def up_block(j):
        parts = [r.ff[0, :, 16 * k : 16 * k + 16, :].reshape(256, 256) for k in (2 * j, 2 * j + 1)]
        return jnp.concatenate(parts, axis=1)

    def down_block(j):
        return r.ff[1, 4 * j : 4 * j + 4, :, :].reshape(512, 256)

    r.acc[...] = r.hid[...] + vec("b_down")
    for j in range(4):
        up_shift = jnp.concatenate(
            [r.vecs[8 + 2 * j : 9 + 2 * j, :], r.vecs[9 + 2 * j : 10 + 2 * j, :]], axis=1)
        up = dot(r.hlow[...], up_block(j)) + up_shift
        square = up * up
        gate = 0.5 + 0.5 * jnp.tanh(up * (GELU_SCALE + GELU_SCALE * 0.044715 * square))
        active = up * gate
        slope = 2 * GELU_SCALE + 6 * 0.044715 * GELU_SCALE * square
        r.dgl[j] = (gate + active * (1.0 - gate) * slope).astype(BF16)
        active = active.astype(BF16)
        r.act[j] = active
        r.acc[...] += dot(active, down_block(j))

    out, unit, inverse = norm_forward(r.acc[...], vec("gain2"), vec("shift2"))
    r.lob[...] = out.astype(BF16).reshape(4, 128, 256)
    for k in (1, 2, 3):
        copy_to("lo", r.lob.at[ring(z, k)], r.lor.at[z], z_peer(k)).start()
    sends_end("lo", r.lob.at[pl.ds(0, 3)])
    own_copies = [pltpu.make_async_copy(r.lob.at[z], r.lor.at[z], r.own_s.at[0])]
    own_copies[0].start()

    await_recv("ct", r.cotb.at[pl.ds(0, 3)])
    d_out = r.cotb[...].reshape(512, 256).astype(F32)
    r.gv[ROW["gain2"] : ROW["gain2"] + 1, :] = column_sum(d_out * unit)
    r.gv[ROW["shift2"] : ROW["shift2"] + 1, :] = column_sum(d_out)
    d_second = norm_backward(d_out, unit, inverse, vec("gain2"))
    d_ffn = d_second.astype(BF16)
    r.dffn[...] = d_ffn
    r.gv[ROW["b_down"] : ROW["b_down"] + 1, :] = column_sum(d_ffn.astype(F32))
    r.acc[...] = d_second

    for j in range(4):
        d_active = dot_nt(r.dffn[...], down_block(j))
        d_up = (d_active * r.dgl[j].astype(F32)).astype(BF16)
        g_down = dot_tn(r.act[j], r.dffn[...])
        r.gp[1, 4 * j : 4 * j + 4] = g_down.astype(BF16).reshape(4, 128, 256)
        g_up = dot(r.hlt[...], d_up).astype(BF16)
        sums = column_sum(d_up.astype(F32))
        for k in range(2):
            at, lanes = 2 * j + k, slice(256 * k, 256 * k + 256)
            r.gp[0, :, 16 * at : 16 * at + 16, :] = g_up[:, lanes].reshape(16, 16, 256)
            r.gv[8 + at : 9 + at, :] = sums[:, lanes]
        r.acc[...] += dot_nt(d_up, up_block(j))

        @pl.when(c == 0)
        def _():
            part = pl.ds(4 * j, 4)
            copy_to("gs", r.gp.at[1, part], r.gs.at[part], sibling).start()

        @pl.when(c == 1)
        def _():
            part = pl.ds(32 * j, 32)
            copy_to("gs", r.gp.at[0, :, part], r.gs.at[:, part], sibling).start()

    sends_end("gs", r.gs)

    d_hidden = r.acc[...]
    unit = r.unit1[...]
    r.gv[ROW["gain1"] : ROW["gain1"] + 1, :] = column_sum(d_hidden * unit)
    r.gv[ROW["shift1"] : ROW["shift1"] + 1, :] = column_sum(d_hidden)
    d_first = norm_backward(d_hidden, unit, r.inv1[...], vec("gain1"))
    r.dfirst[...] = d_first
    d_branch = d_first.astype(BF16)
    r.gv[ROW["b_out"] : ROW["b_out"] + 1, :] = column_sum(d_branch.astype(F32))
    r.dms[...] = dot_nt(d_branch, w_out_rows(1 - c)).astype(BF16).reshape(4, 128, 128)
    copy_to("dm", r.dms, r.dmx.at[:, c], sibling).start()
    sends_end("dm", r.dms)
    r.dmx[:, c] = dot_nt(d_branch, w_out_rows(c)).astype(BF16).reshape(4, 128, 128)

    def spot(g):
        return g * (1 - c) + (4 * lax.rem(g, 4) + lax.div(g, 4)) * c

    for half, mixed in ((c, r.mx[:, c].reshape(512, 128)), (1 - c, r.mr[...].reshape(512, 128))):
        g_out = dot_tn(mixed, d_branch).astype(BF16)
        for i in range(8):
            at = spot(8 * half + i)
            r.gwo[at, 0:16, :] = g_out[16 * i : 16 * i + 16, 0:128]
            r.gwo[at, 16:32, :] = g_out[16 * i : 16 * i + 16, 128:256]
    r.gv[0:2, :] = jnp.zeros((2, 256), F32)
    r.v0[...] = r.gv[...]

    await_recv("gs", r.gs)

    def add_cores(i, carry):
        at = group(lax.div(i, 4), lax.rem(i, 4))
        r.rs[i] = (r.gp[c, at].astype(F32) + r.gs[at].astype(F32)).astype(BF16)
        return carry

    lax.fori_loop(0, 16, add_cores, 0)

    for k in (1, 2, 3):
        part, to = pl.ds(4 * ring(a, k), 4), a_peer(k)
        copy_to("r1", r.rs.at[part], r.r1.at[k - 1], to).start()
        copy_to("g1", r.gwo.at[part], r.wo1.at[k - 1], to).start()
        copy_to("v1", r.v0, r.vr1.at[k - 1], to).start()
    sends_end("r1", r.r1)
    sends_end("g1", r.wo1)
    sends_end("v1", r.vr1)

    await_recv("dm", r.dmx.at[:, 1 - c])
    d_mixed_t = r.dmx[...].reshape(1024, 128).astype(F32).T
    extra = []
    for head in range(4):
        rows = slice(32 * head, 32 * head + 32)
        scaled = d_mixed_t[rows] * r.ri[head : head + 1, :]
        r.dot_[rows, :] = scaled.astype(BF16)
        inner = -column_sum(scaled * r.ot[rows, :])
        high = inner.astype(BF16).astype(F32)
        extra += [high, inner - high]
    extra.append(jnp.zeros((8, 1024), F32))
    r.dot_[128:144, :] = jnp.concatenate(extra, axis=0).astype(BF16)
    r.dot_[144:256, :] = jnp.zeros((112, 1024), BF16)
    r.doo[...] = r.dot_[0:128, :].T

    for head in range(4):
        d_probs = dot(r.vx[head], r.dot_[...])
        d_scores = r.ee[head] * d_probs.astype(BF16)
        r.ds[head % 2] = d_scores
        rows = slice(head * HD, head * HD + HD)
        r.dqt[rows, :] = dot(r.kt[rows, :], d_scores)
        do_masked = jnp.where(head_of_lane == head, r.doo[...], zero)
        for k in range(0, 1024, 256):
            d_key = dot(r.ds[head % 2, k : k + 256, :], r.qm[head])
            d_value = dot(r.ee[head, k : k + 256, :], do_masked)
            if head == 0:
                r.dk[k : k + 256, :] = d_key
                r.dv[k : k + 256, :] = d_value
            else:
                r.dk[k : k + 256, :] += d_key
                r.dv[k : k + 256, :] += d_value

    d_queries = (r.dqt[...] * SCORE_SCALE).T.astype(BF16)
    d_keys = (r.dk[...] * SCORE_SCALE).astype(BF16)
    d_values = r.dv[...].astype(BF16)
    for k, (left, right) in enumerate(((r.sht, d_queries), (r.sht, d_keys), (r.imgt, d_values))):
        g_part = dot(left[...], right).astype(BF16)
        for i in range(16):
            r.gio[i, 16 * k : 16 * k + 16, :] = g_part[16 * i : 16 * i + 16, :]
    ones = jnp.ones((1024, 128), BF16)
    sums = jnp.where(
        iota((128, 128), 1) < 64, dot_tn(d_queries, ones), dot_tn(d_values, ones)).astype(BF16)
    for i in range(8):
        r.gio[8 * c + i, 48:64, :] = sums[16 * i : 16 * i + 16, :]
        r.gio[8 * (1 - c) + i, 48:64, :] = jnp.zeros((16, 128), BF16)
    for k in range(1, 16):
        copy_to("q1", r.gio.at[ring(gx, k, 16)], r.q1.at[gx], gx_peer(k)).start()
    sends_end("q1", r.q1.at[pl.ds(0, 15)])

    d_tokens = (
        dot_nt(d_queries, w_part(0)) + dot_nt(d_keys, w_part(1)) + dot_nt(d_values, w_part(2)))
    r.gt[...] = d_tokens.astype(BF16).reshape(4, 2, 128, 256)
    copy_to("gt", r.gt.at[:, 1 - c], r.gtr, sibling).start()
    sends_end("gt", r.gtr)

    await_recv("r1", r.r1)
    await_recv("g1", r.wo1)
    await_recv("v1", r.vr1)

    def add_first(i, carry):
        total = r.rs[4 * a + i].astype(F32)
        small = r.gwo[4 * a + i].astype(F32)
        for k in range(3):
            total = total + r.r1[k, i].astype(F32)
            small = small + r.wo1[k, i].astype(F32)
        r.s2[i] = total.astype(BF16)
        r.wos[i] = small.astype(BF16)
        return carry

    lax.fori_loop(0, 4, add_first, 0)
    r.v1[...] = r.v0[...] + r.vr1[0] + r.vr1[1] + r.vr1[2]
    for k in (1, 2, 3):
        part, to = ring(b, k), b_peer(k)
        copy_to("r2", r.s2.at[part], r.r2.at[k - 1], to).start()
        copy_to("g2", r.wos.at[part], r.wo2.at[k - 1], to).start()
        copy_to("v2", r.v1, r.vr2.at[k - 1], to).start()
    sends_end("r2", r.r2)
    sends_end("g2", r.wo2)
    sends_end("v2", r.vr2)

    await_recv("gt", r.gtr)
    full = (
        r.dfirst[...]
        + r.gt[:, c].reshape(512, 256).astype(F32)
        + r.gtr[...].reshape(512, 256).astype(F32))
    r.gob[...] = full.astype(BF16).reshape(4, 128, 256)
    for k in (1, 2, 3):
        copy_to("go", r.gob.at[ring(z, k)], r.gor.at[z], z_peer(k)).start()
    sends_end("go", r.gob.at[pl.ds(0, 3)])

    await_recv("r2", r.r2)
    await_recv("g2", r.wo2)
    await_recv("v2", r.vr2)
    total = r.s2[b].astype(F32)
    small = r.wos[b].astype(F32)
    for k in range(3):
        total = total + r.r2[k].astype(F32)
        small = small + r.wo2[k].astype(F32)
    r.fin[0] = total[:, 0:128]
    r.fin[1] = total[:, 128:256]
    r.fwo[...] = small
    r.v2[...] = r.v1[...] + r.vr2[0] + r.vr2[1] + r.vr2[2]
    r.p3f[...] = jnp.zeros((8, 48, 128), F32)

    @pl.when(c == 0)
    def _():
        for i in range(8):
            for half in range(2):
                for row in range(2):
                    at = 16 * half + 8 * row
                    r.p3f[i, at : at + 8, :] = r.fin.at[half][
                        pl.ds(2 * i + row, 8, stride=16), :]

    @pl.when(c == 1)
    def _():
        for i in range(8):
            for half in range(2):
                r.p3f[i, 16 * half : 16 * half + 16, :] = r.fin[half, 16 * i : 16 * i + 16, :]

    for i in range(8):
        for row in range(2):
            at = 32 + 8 * row
            r.p3f[i, at : at + 2, :] = r.fwo[pl.ds(2 * i + row, 2, stride=16), :]
    r.p3[...] = r.p3f[...].astype(BF16)
    for k in range(1, 8):
        copy_to("p3", r.p3.at[ring(gy, k, 8)], r.r3.at[gy], gy_peer(k)).start()
        copy_to("v3", r.v2, r.vr3.at[gy], gy_peer(k)).start()
    sends_end("p3", r.p3.at[pl.ds(0, 7)])
    sends_end("v3", r.vr3.at[pl.ds(0, 7)])

    await_recv("q1", r.q1.at[pl.ds(0, 15)])
    total = r.gio[gx].astype(F32)
    for k in range(1, 16):
        total = total + r.q1[ring(gx, -k, 16)].astype(F32)
    r.fio[...] = total
    r.p4f[...] = jnp.zeros((8, 16, 128), F32)
    for i in range(8):
        for row in range(2):
            at = 8 * row
            r.p4f[i, at : at + 4, :] = r.fio[pl.ds(2 * i + row, 4, stride=16), :]
    r.p4[...] = r.p4f[...].astype(BF16)
    for k in range(1, 8):
        copy_to("p4", r.p4.at[ring(gy, k, 8)], r.r4.at[gy], gy_peer(k)).start()
    sends_end("p4", r.p4.at[pl.ds(0, 7)])

    own_copies += [
        pltpu.make_async_copy(r.gob.at[z], r.gor.at[z], r.own_s.at[1]),
        pltpu.make_async_copy(r.p3.at[gy], r.r3.at[gy], r.own_s.at[2]),
        pltpu.make_async_copy(r.p4.at[gy], r.r4.at[gy], r.own_s.at[3]),
        pltpu.make_async_copy(r.v2, r.vr3.at[gy], r.own_s.at[4]),
    ]
    for copy in own_copies[1:]:
        copy.start()
    await_recv("lo", r.lor.at[pl.ds(0, 3)])
    await_recv("go", r.gor.at[pl.ds(0, 3)])
    await_recv("p3", r.r3.at[pl.ds(0, 7)])
    await_recv("v3", r.vr3.at[pl.ds(0, 7)])
    await_recv("p4", r.r4.at[pl.ds(0, 7)])
    for copy in own_copies:
        copy.wait()
    for make in closing:
        make().wait_send()


def unpack(*refs):
    r = Refs()
    for name, ref in zip(tuple(PACKED) + OUTPUTS, refs):
        setattr(r, name, ref)
    gx, gy = lax.axis_index("gx"), lax.axis_index("gy")
    place = 2 * (8 * gx + gy)
    up_place = 128 * lax.rem(gx, 2) + 16 * gy
    r.layer_out[...] = r.lor[...]
    r.grad_tokens[...] = r.gor[...].astype(F32)
    core0 = jnp.zeros((48, 128), F32)
    core1 = jnp.zeros((48, 128), F32)
    into0 = jnp.zeros((16, 128), F32)
    into1 = jnp.zeros((16, 128), F32)
    total = jnp.zeros((16, 256), F32)
    for i in range(4):
        core0 = core0 + r.r3[2 * i].astype(F32)
        core1 = core1 + r.r3[2 * i + 1].astype(F32)
        into0 = into0 + r.r4[2 * i].astype(F32)
        into1 = into1 + r.r4[2 * i + 1].astype(F32)
        total = total + r.vr3[2 * i] + r.vr3[2 * i + 1]
    r.g_w_down[:, 0:128] = core1[0:16]
    r.g_w_down[:, 128:256] = core1[16:32]
    w_out = core0 + core1
    for row in range(2):
        out_row = slice(row, row + 1)
        for j in range(8):
            for half in range(2):
                at = 16 * half + 8 * row + j
                lanes = 256 * j + 128 * half
                r.g_w_up[out_row, lanes : lanes + 128] = core0[at : at + 1]
        for k in range(3):
            at = 8 * row + k
            r.g_w_in[out_row, 256 * k : 256 * k + 128] = into0[at : at + 1]
            r.g_w_in[out_row, 256 * k + 128 : 256 * k + 256] = into1[at : at + 1]
        at = 32 + 8 * row
        r.g_w_out[out_row, 0:128] = w_out[at : at + 1]
        r.g_w_out[out_row, 128:256] = w_out[at + 1 : at + 2]
    biases = into0 + into1
    for name, lane in (("b_q", 0), ("b_v", 64)):
        pair = jnp.concatenate(
            [biases[3:4, lane : lane + 1], biases[11:12, lane : lane + 1]], axis=1)
        getattr(r, "g_" + name)[...] = pair.reshape(2)
    moved = pltpu.roll(total, lax.rem(256 - place, 256), axis=1)
    for name in SMALL[2:]:
        row = ROW[name]
        getattr(r, "g_" + name)[...] = moved[row : row + 1, 0:2].reshape(2)
    up_total = column_sum(jnp.where(iota((8, 256), 0) == lax.div(gx, 2), total[8:16], 0.0))
    up_total = jnp.broadcast_to(up_total, (8, 256))
    up_total = pltpu.roll(up_total, lax.rem(256 - up_place, 256), axis=1)
    r.g_b_up[...] = up_total[0:1, 0:16].reshape(16)


def body(
    tokens, lengths, w_in, b_q, b_v, w_out, b_out, gain_first, shift_first, w_up, b_up,
    w_down, b_down, gain_second, shift_second, cotangent,
):
    column = np.arange(D)
    freq = np.power(10000.0, -(2.0 * (column // 2)) / D).astype(np.float32)[None, :]
    args = (
        tokens, cotangent, lengths, jnp.asarray(freq), w_in, w_out, w_up, w_down,
        b_q, b_v, b_out, gain_first, shift_first, b_down, gain_second, shift_second, b_up,
    )
    vmem = pl.BlockSpec(memory_space=pltpu.VMEM)
    anywhere = pl.BlockSpec(memory_space=pl.ANY)
    in_specs = [anywhere] * len(args)
    in_specs[2] = pl.BlockSpec(memory_space=pltpu.SMEM)
    shape = jax.ShapeDtypeStruct
    vector = shape((2,), F32)
    scratch = [pltpu.VMEM(args[INPUTS.index(name)].shape, args[INPUTS.index(name)].dtype)
               for name in LOADED]
    scratch += [pltpu.VMEM(dims, kind) for dims, kind in SCRATCH.values()]
    scratch += [pltpu.SemaphoreType.DMA((count,)) for count in SEMS.values()]
    packed = pl.pallas_call(
        kernel,
        out_shape=tuple(shape(dims, kind) for dims, kind in PACKED.values()),
        in_specs=in_specs,
        out_specs=tuple([anywhere] * len(PACKED)),
        scratch_shapes=scratch,
        compiler_params=pltpu.CompilerParams(
            collective_id=0, has_side_effects=True, vmem_limit_bytes=VMEM_LIMIT),
        name="encoder_layer",
    )(*args)
    out_shape = (
        shape((4, 128, 256), BF16), shape((4, 128, 256), F32), shape((2, 768), F32),
        vector, vector, shape((2, 256), F32), vector, vector, vector,
        shape((2, 2048), F32), shape((16,), F32), shape((16, 256), F32),
        vector, vector, vector,
    )
    return pl.pallas_call(
        unpack,
        out_shape=out_shape,
        in_specs=[vmem] * len(packed),
        out_specs=tuple([vmem] * len(out_shape)),
        name="unpack_results",
    )(*packed)


def solution(mesh):
    both = ("gx", "gy")
    rows, vector, whole = P(both, None), P(both), P("gx", "gy", None)
    return jax.shard_map(
        body,
        mesh=mesh,
        in_specs=(
            whole, P("gx"), rows, vector, vector, rows, vector, vector, vector, rows, vector,
            rows, vector, vector, vector, whole,
        ),
        out_specs=(
            whole, whole, rows, vector, vector, rows, vector, vector, vector, rows, vector,
            rows, vector, vector, vector,
        ),
        check_vma=False,
    )
```

time: 76.6 us -> 65 us (0.85)
  Pallas kernels: 75.7 us -> 63.9 us
    pallas_call x1, Pallas kernels: 73.6 us -> 61.8 us  [body(): pl.pallas_call(kernel, out_shape=tuple((shape(dims, kind) for dims, kind...]
where the time goes in v3:
time: 65 us; the launch traced here: 64.8 us
  Pallas kernels  63.9 us (98%)
  between operations  0.82 us (1%)
    pallas_call x1, Pallas kernels, body(): pl.pallas_call(kernel, out_shape=tuple((shape(dims, kind) for dims, kind...  61.8 us
    pallas_call x1, Pallas kernels, body(): pl.pallas_call(unpack, out_shape=out_shape, in_specs=[vmem] * len(packed)...  2.15 us

profile of v3, /device:TPU:1, one launch (start us, length us, event | category | flops | bytes accessed | tf_op | source)
XLA Modules:
  0.0 64.8 jit_solution(15170577859984051399)
XLA Ops:
  0.7 61.8 %encoder_layer.1 = (bf16[4,128,256]{2,1,0:T(8,128)(2,1)}, bf16[4,128,256]{2,1,0:T(8,128)(2,1)}, bf16[8,48,128]{2,1,0:T(8,128)(2,1)}, bf16[8,16,128]{2,1,0:T(8,128)(2,1)}, f32[8,16,256]{2,1,0:T(8,128)}) custom-call(bf16[4,128,256]{2,1,0:T(8,128)(2,1)} %refs_0_.1, bf16[4,128,256]{2,1,0:T(8,128)(2,1)} %refs_1_.1, s32[4]{0:T(128)} %refs_2_.1, ...), custom_call_target="tpu_custom_call" | custom-call | tf_op jit(solution)/shard_map/encoder_layer/pallas_call | solution.py:868
  62.5 2.2 %unpack_results.1 = (bf16[4,128,256]{2,1,0:T(8,128)(2,1)}, f32[4,128,256]{2,1,0:T(8,128)}, f32[2,768]{1,0:T(2,128)}, f32[2]{0:T(128)}, f32[2]{0:T(128)}, /*index...) custom-call(bf16[4,128,256]{2,1,0:T(8,128)(2,1)} %get-tuple-element., ...), custom_call_target="tpu_custom_call" | custom-call | tf_op jit(solution)/shard_map/unpack_results/pallas_call | solution.py:884

commit v4 on v3

--- a/solution.py
+++ b/solution.py
@@ -121,7 +121,6 @@
     vr1=((3, 16, 256), F32),
     v1=((16, 256), F32),
     vr2=((3, 16, 256), F32),
-    v2=((16, 256), F32),
     gt=((4, 2, 128, 256), BF16),
     gtr=((4, 128, 256), BF16),
     gob=((4, 128, 256), BF16),
@@ -132,10 +131,10 @@
 )
 
 GROUPS = (
-    "s1", "s2", "tk", "tf", "ct", "wi", "wa", "wb", "fa", "fb", "fc", "fw", "mx", "dm", "lo",
-    "gs", "r1", "r2", "g1", "g2", "v1", "v2", "v3", "q1", "gt", "go", "p3", "p4",
+    "s1", "s2", "tk", "tf", "ct", "ia", "ib", "wa", "wb", "fa", "fb", "fc", "fw", "mx", "dm", "lo",
+    "gs", "r1", "r2", "g1", "g2", "v1", "v2", "q1", "gt", "go", "p3", "p4",
 )
-SEMS = dict(in_s=16, own_s=5, tk_r=3)
+SEMS = dict(in_s=16, own_s=4, tk_r=3, fc_r=3)
 for group_name in GROUPS:
     SEMS.setdefault(group_name + "_s", 1)
     SEMS.setdefault(group_name + "_r", 1)
@@ -153,7 +152,6 @@
     gor=((4, 128, 256), BF16),
     r3=((8, 48, 128), BF16),
     r4=((8, 16, 128), BF16),
-    vr3=((8, 16, 256), F32),
 )
 LOADED = INPUTS[3:]
 SMALL = ("b_q", "b_v", "b_out", "gain1", "shift1", "b_down", "gain2", "shift2")
@@ -230,7 +228,8 @@
     loads.append(pltpu.make_async_copy(r.cot.at[z], r.cotb.at[z], r.in_s.at[15]))
 
     barrier = pltpu.get_barrier_semaphore()
-    peers = [gx_peer(k) for k in range(1, 16)] + [gy_peer(k) for k in range(1, 8)]
+    peers = [gy_peer(k) for k in (4, 5, 3, 2, 6, 1, 7)]
+    peers += [a_peer(k) for k in (2, 1, 3)] + [b_peer(k) for k in (2, 1, 3)]
     for peer in peers:
         pl.semaphore_signal(barrier, inc=1, device_id=peer, device_id_type=MESH)
     for load in loads:
@@ -279,7 +278,7 @@
     r.s1[gy, 80:96, :] = r.v_w_down[:, 128:256]
     r.s1[gy, 96:112, :] = r.pf[16:32, :].astype(BF16)
 
-    pl.semaphore_wait(barrier, 22)
+    pl.semaphore_wait(barrier, 13)
 
     def first_part(at):
         return r.s1.at[at, pl.ds(0, 16)]
@@ -290,13 +289,13 @@
     for k in range(1, 8):
         copy_to("s1", first_part(gy), first_part(gy), gy_peer(k)).start()
     sends_end("s1", r.s1.at[pl.ds(0, 7), pl.ds(0, 16)])
-    for k in (1, 2, 3):
-        copy_to("tk", r.tok.at[ring(z, k)], r.img.at[z, c], z_peer(k), r.tk_r.at[k - 1]).start()
-    sends_end("tk", r.cotb.at[pl.ds(0, 3)])
     for k in range(1, 8):
         part = second_part(gy, lax.rem(gy + k, 2))
         copy_to("s2", part, part, gy_peer(k)).start()
     sends_end("s2", r.s1.at[pl.ds(0, 7), pl.ds(0, 48)])
+    for k in (1, 2, 3):
+        copy_to("tk", r.tok.at[ring(z, k)], r.img.at[z, c], z_peer(k), r.tk_r.at[k - 1]).start()
+    sends_end("tk", r.cotb.at[pl.ds(0, 3)])
     copy_to("tf", r.img.at[z, c], r.img.at[z, c], sibling).start()
 
     freq = r.v_freq[...]
@@ -326,9 +325,10 @@
     def wi_view(at):
         return r.wio.at[at, pl.ds(0, 64)]
 
-    for k in range(1, 16):
-        copy_to("wi", wi_view(gx), wi_view(gx), gx_peer(k)).start()
-    sends_end("wi", r.wio.at[pl.ds(0, 15), pl.ds(0, 64)])
+    for k in (1, 2, 3):
+        copy_to("ia", wi_view(here), wi_view(here), a_peer(k)).start()
+    for k in (1, 2, 3):
+        copy_to("ib", wi_view(here), wi_view(here), b_peer(k)).start()
 
     await_recv("s2", r.s1.at[pl.ds(0, 7), pl.ds(0, 48)])
 
@@ -373,8 +373,6 @@
     r.wio[here, 64:112, :] = r.asmf[64:112, :].astype(BF16)
     for k in (1, 2, 3):
         copy_to("wa", wo_view(here), wo_view(here), a_peer(k)).start()
-    for k in (1, 2, 3):
-        copy_to("wb", wo_view(here), wo_view(here), b_peer(k)).start()
 
     for k in (1, 2, 3):
         at = ring(z, -k)
@@ -384,6 +382,13 @@
     for k in (1, 2, 3):
         copy_to("ct", r.cot.at[ring(z, k)], r.cotb.at[z], z_peer(k)).start()
     sends_end("ct", r.cotb.at[pl.ds(0, 3)])
+    await_recv("ia", r.wio.at[pl.ds(0, 3), pl.ds(0, 64)])
+    for i in (1, 2, 3):
+        at = group(ring(a, -i), b)
+        for k in (1, 2, 3):
+            copy_to("ib", wi_view(at), wi_view(at), b_peer(k)).start()
+    sends_end("ia", r.wio.at[pl.ds(0, 3), pl.ds(0, 64)])
+    sends_end("ib", r.wio.at[pl.ds(0, 12), pl.ds(0, 64)])
     await_recv("tf", r.img.at[:, 1 - c])
 
     for i in range(8):
@@ -394,14 +399,19 @@
             r.sh[32 * at : 32 * at + 32, :] = (rows[32 * k : 32 * k + 32] + pos).astype(BF16)
     image = r.img[...].reshape(1024, 256)
 
+    r.sht[...] = r.sh[...].T
+    r.imgt[...] = image.T
+
     await_recv("fa", r.ff.at[c, pl.ds(0, 3)])
     for i in (1, 2, 3):
         at = group(ring(a, -i), b)
         for k in (1, 2, 3):
-            copy_to("fc", ff_view(at), ff_view(at), b_peer(k)).start()
+            copy_to("fc", ff_view(at), ff_view(at), b_peer(k), r.fc_r.at[k - 1]).start()
     for i in range(4):
         at = group(ring(a, -i), b)
         copy_to("fw", ff_view(at), ff_view(at), sibling).start()
+    for k in (1, 2, 3):
+        copy_to("wb", wo_view(here), wo_view(here), b_peer(k)).start()
     await_recv("wa", r.wio.at[pl.ds(0, 3), pl.ds(64, 48)])
     for i in (1, 2, 3):
         at = group(ring(a, -i), b)
@@ -414,10 +424,7 @@
     sends_end("wa", r.wio.at[pl.ds(0, 3), pl.ds(64, 48)])
     sends_end("wb", r.wio.at[pl.ds(0, 12), pl.ds(64, 48)])
 
-    r.sht[...] = r.sh[...].T
-    r.imgt[...] = image.T
-
-    await_recv("wi", r.wio.at[pl.ds(0, 15), pl.ds(0, 64)])
+    await_recv("ib", r.wio.at[pl.ds(0, 12), pl.ds(0, 64)])
     biases = jnp.zeros((16, 128), F32)
     for i in range(16):
         biases = biases + r.wio[i, 48:64, :].astype(F32)
@@ -470,9 +477,9 @@
     copy_to("mx", r.mx.at[:, 1 - c], r.mr, sibling).start()
     sends_end("mx", r.mr)
 
-    await_recv("fc", r.ff.at[c, pl.ds(0, 9)])
-    for i in (1, 2, 3):
-        for k in (1, 2, 3):
+    for k in (1, 3, 2):
+        await_recv("fc", r.ff.at[c, pl.ds(0, 3)], k - 1)
+        for i in (1, 2, 3):
             at = group(ring(a, -i), ring(b, -k))
             copy_to("fw", ff_view(at), ff_view(at), sibling).start()
 
@@ -661,6 +668,31 @@
                 r.dk[k : k + 256, :] += d_key
                 r.dv[k : k + 256, :] += d_value
 
+    await_recv("r1", r.r1)
+    await_recv("g1", r.wo1)
+    await_recv("v1", r.vr1)
+
+    def add_first(i, carry):
+        total = r.rs[4 * a + i].astype(F32)
+        small = r.gwo[4 * a + i].astype(F32)
+        for k in range(3):
+            total = total + r.r1[k, i].astype(F32)
+            small = small + r.wo1[k, i].astype(F32)
+        r.s2[i] = total.astype(BF16)
+        r.wos[i] = small.astype(BF16)
+        return carry
+
+    lax.fori_loop(0, 4, add_first, 0)
+    r.v1[...] = r.v0[...] + r.vr1[0] + r.vr1[1] + r.vr1[2]
+    for k in (1, 2, 3):
+        part, to = ring(b, k), b_peer(k)
+        copy_to("r2", r.s2.at[part], r.r2.at[k - 1], to).start()
+        copy_to("g2", r.wos.at[part], r.wo2.at[k - 1], to).start()
+        copy_to("v2", r.v1, r.vr2.at[k - 1], to).start()
+    sends_end("r2", r.r2)
+    sends_end("g2", r.wo2)
+    sends_end("v2", r.vr2)
+
     d_queries = (r.dqt[...] * SCORE_SCALE).T.astype(BF16)
     d_keys = (r.dk[...] * SCORE_SCALE).astype(BF16)
     d_values = r.dv[...].astype(BF16)
@@ -684,31 +716,6 @@
     copy_to("gt", r.gt.at[:, 1 - c], r.gtr, sibling).start()
     sends_end("gt", r.gtr)
 
-    await_recv("r1", r.r1)
-    await_recv("g1", r.wo1)
-    await_recv("v1", r.vr1)
-
-    def add_first(i, carry):
-        total = r.rs[4 * a + i].astype(F32)
-        small = r.gwo[4 * a + i].astype(F32)
-        for k in range(3):
-            total = total + r.r1[k, i].astype(F32)
-            small = small + r.wo1[k, i].astype(F32)
-        r.s2[i] = total.astype(BF16)
-        r.wos[i] = small.astype(BF16)
-        return carry
-
-    lax.fori_loop(0, 4, add_first, 0)
-    r.v1[...] = r.v0[...] + r.vr1[0] + r.vr1[1] + r.vr1[2]
-    for k in (1, 2, 3):
-        part, to = ring(b, k), b_peer(k)
-        copy_to("r2", r.s2.at[part], r.r2.at[k - 1], to).start()
-        copy_to("g2", r.wos.at[part], r.wo2.at[k - 1], to).start()
-        copy_to("v2", r.v1, r.vr2.at[k - 1], to).start()
-    sends_end("r2", r.r2)
-    sends_end("g2", r.wo2)
-    sends_end("v2", r.vr2)
-
     await_recv("gt", r.gtr)
     full = (
         r.dfirst[...]
@@ -730,7 +737,6 @@
     r.fin[0] = total[:, 0:128]
     r.fin[1] = total[:, 128:256]
     r.fwo[...] = small
-    r.v2[...] = r.v1[...] + r.vr2[0] + r.vr2[1] + r.vr2[2]
     r.p3f[...] = jnp.zeros((8, 48, 128), F32)
 
     @pl.when(c == 0)
@@ -752,12 +758,18 @@
         for row in range(2):
             at = 32 + 8 * row
             r.p3f[i, at : at + 2, :] = r.fwo[pl.ds(2 * i + row, 2, stride=16), :]
+    sums = r.v1[...] + r.vr2[0] + r.vr2[1] + r.vr2[2]
+    own_lanes = pltpu.roll(sums[0:8], lax.rem(256 - 16 * gx, 256), axis=1)[:, 0:128]
+    up_sums = column_sum(jnp.where(iota((8, 256), 0) == lax.div(gx, 2), sums[8:16], 0.0))
+    right = lax.rem(gx, 2).astype(F32)
+    up_sums = up_sums[:, 0:128] * (1.0 - right) + up_sums[:, 128:256] * right
+    for i in range(8):
+        r.p3f[i, 34:40, :] = own_lanes[2:8]
+        r.p3f[i, 42:43, :] = up_sums
     r.p3[...] = r.p3f[...].astype(BF16)
     for k in range(1, 8):
         copy_to("p3", r.p3.at[ring(gy, k, 8)], r.r3.at[gy], gy_peer(k)).start()
-        copy_to("v3", r.v2, r.vr3.at[gy], gy_peer(k)).start()
     sends_end("p3", r.p3.at[pl.ds(0, 7)])
-    sends_end("v3", r.vr3.at[pl.ds(0, 7)])
 
     await_recv("q1", r.q1.at[pl.ds(0, 15)])
     total = r.gio[gx].astype(F32)
@@ -778,14 +790,12 @@
         pltpu.make_async_copy(r.gob.at[z], r.gor.at[z], r.own_s.at[1]),
         pltpu.make_async_copy(r.p3.at[gy], r.r3.at[gy], r.own_s.at[2]),
         pltpu.make_async_copy(r.p4.at[gy], r.r4.at[gy], r.own_s.at[3]),
-        pltpu.make_async_copy(r.v2, r.vr3.at[gy], r.own_s.at[4]),
     ]
     for copy in own_copies[1:]:
         copy.start()
     await_recv("lo", r.lor.at[pl.ds(0, 3)])
     await_recv("go", r.gor.at[pl.ds(0, 3)])
     await_recv("p3", r.r3.at[pl.ds(0, 7)])
-    await_recv("v3", r.vr3.at[pl.ds(0, 7)])
     await_recv("p4", r.r4.at[pl.ds(0, 7)])
     for copy in own_copies:
         copy.wait()
@@ -797,22 +807,18 @@
     r = Refs()
     for name, ref in zip(tuple(PACKED) + OUTPUTS, refs):
         setattr(r, name, ref)
-    gx, gy = lax.axis_index("gx"), lax.axis_index("gy")
-    place = 2 * (8 * gx + gy)
-    up_place = 128 * lax.rem(gx, 2) + 16 * gy
+    gy = lax.axis_index("gy")
     r.layer_out[...] = r.lor[...]
     r.grad_tokens[...] = r.gor[...].astype(F32)
     core0 = jnp.zeros((48, 128), F32)
     core1 = jnp.zeros((48, 128), F32)
     into0 = jnp.zeros((16, 128), F32)
     into1 = jnp.zeros((16, 128), F32)
-    total = jnp.zeros((16, 256), F32)
     for i in range(4):
         core0 = core0 + r.r3[2 * i].astype(F32)
         core1 = core1 + r.r3[2 * i + 1].astype(F32)
         into0 = into0 + r.r4[2 * i].astype(F32)
         into1 = into1 + r.r4[2 * i + 1].astype(F32)
-        total = total + r.vr3[2 * i] + r.vr3[2 * i + 1]
     r.g_w_down[:, 0:128] = core1[0:16]
     r.g_w_down[:, 128:256] = core1[16:32]
     w_out = core0 + core1
@@ -835,14 +841,12 @@
         pair = jnp.concatenate(
             [biases[3:4, lane : lane + 1], biases[11:12, lane : lane + 1]], axis=1)
         getattr(r, "g_" + name)[...] = pair.reshape(2)
-    moved = pltpu.roll(total, lax.rem(256 - place, 256), axis=1)
+    moved = pltpu.roll(w_out[32:48], lax.rem(128 - 2 * gy, 128), axis=1)
     for name in SMALL[2:]:
         row = ROW[name]
         getattr(r, "g_" + name)[...] = moved[row : row + 1, 0:2].reshape(2)
-    up_total = column_sum(jnp.where(iota((8, 256), 0) == lax.div(gx, 2), total[8:16], 0.0))
-    up_total = jnp.broadcast_to(up_total, (8, 256))
-    up_total = pltpu.roll(up_total, lax.rem(256 - up_place, 256), axis=1)
-    r.g_b_up[...] = up_total[0:1, 0:16].reshape(16)
+    moved = pltpu.roll(w_out[40:48], lax.rem(128 - 16 * gy, 128), axis=1)
+    r.g_b_up[...] = moved[2:3, 0:16].reshape(16)
 
 
 def body(

time: 65 us -> 61.9 us (0.952)
  Pallas kernels: 63.9 us -> 60.9 us
    pallas_call x1, Pallas kernels: 61.8 us -> 58.9 us  [body(): pl.pallas_call(kernel, out_shape=tuple((shape(dims, kind) for dims, kind...]
where the time goes in v4:
time: 61.9 us; the launch traced here: 61.7 us
  Pallas kernels  60.9 us (98%)
  between operations  0.82 us (1%)
    pallas_call x1, Pallas kernels, body(): pl.pallas_call(kernel, out_shape=tuple((shape(dims, kind) for dims, kind...  58.9 us
    pallas_call x1, Pallas kernels, body(): pl.pallas_call(unpack, out_shape=out_shape, in_specs=[vmem] * len(packed)...  2.03 us

profile of v4, /device:TPU:1, one launch (start us, length us, event | category | flops | bytes accessed | tf_op | source)
XLA Modules:
  0.0 61.7 jit_solution(12504687833933859796)
XLA Ops:
  0.7 58.9 %encoder_layer.1 = (bf16[4,128,256]{2,1,0:T(8,128)(2,1)}, bf16[4,128,256]{2,1,0:T(8,128)(2,1)}, bf16[8,48,128]{2,1,0:T(8,128)(2,1)}, bf16[8,16,128]{2,1,0:T(8,128)(2,1)}) custom-call(bf16[4,128,256]{2,1,0:T(8,128)(2,1)} %refs_0_.1, bf16[4,128,256]{2,1,0:T(8,128)(2,1)} %refs_1_.1, s32[4]{0:T(128)} %refs_2_.1, f32[1,256]{1,0:T(1,128)} %constant.2.clone.refs_3_, ...), custom_call_target="tpu_custom_call" | custom-call | tf_op jit(solution)/shard_map/encoder_layer/pallas_call | solution.py:872
  59.5 2.0 %unpack_results.1 = (bf16[4,128,256]{2,1,0:T(8,128)(2,1)}, f32[4,128,256]{2,1,0:T(8,128)}, f32[2,768]{1,0:T(2,128)}, f32[2]{0:T(128)}, f32[2]{0:T(128)}, /*index...) custom-call(bf16[4,128,256]{2,1,0:T(8,128)(2,1)} %get-tuple-element., ...), custom_call_target="tpu_custom_call" | custom-call | tf_op jit(solution)/shard_map/unpack_results/pallas_call | solution.py:888

commit v5 on v4

--- a/solution.py
+++ b/solution.py
@@ -134,7 +134,7 @@
     "s1", "s2", "tk", "tf", "ct", "ia", "ib", "wa", "wb", "fa", "fb", "fc", "fw", "mx", "dm", "lo",
     "gs", "r1", "r2", "g1", "g2", "v1", "v2", "q1", "gt", "go", "p3", "p4",
 )
-SEMS = dict(in_s=16, own_s=4, tk_r=3, fc_r=3)
+SEMS = dict(in_s=16, own_s=4, tk_r=3, fc_r=3, gs_r=2)
 for group_name in GROUPS:
     SEMS.setdefault(group_name + "_s", 1)
     SEMS.setdefault(group_name + "_r", 1)
@@ -360,8 +360,6 @@
 
     for k in (1, 2, 3):
         copy_to("fa", ff_view(here), ff_view(here), a_peer(k)).start()
-    for k in (1, 2, 3):
-        copy_to("fb", ff_view(here), ff_view(here), b_peer(k)).start()
 
     r.asmf[96:112, :] = jnp.zeros((16, 128), F32)
     shared_at = pl.multiple_of(16 + 80 * c, 16)
@@ -387,6 +385,8 @@
         at = group(ring(a, -i), b)
         for k in (1, 2, 3):
             copy_to("ib", wi_view(at), wi_view(at), b_peer(k)).start()
+    for k in (1, 2, 3):
+        copy_to("fb", ff_view(here), ff_view(here), b_peer(k)).start()
     sends_end("ia", r.wio.at[pl.ds(0, 3), pl.ds(0, 64)])
     sends_end("ib", r.wio.at[pl.ds(0, 12), pl.ds(0, 64)])
     await_recv("tf", r.img.at[:, 1 - c])
@@ -568,6 +568,38 @@
     r.gv[ROW["b_down"] : ROW["b_down"] + 1, :] = column_sum(d_ffn.astype(F32))
     r.acc[...] = d_second
 
+    def first_sums(half):
+        await_recv("gs", r.gs.at[pl.ds(0, 8)], half)
+
+        @pl.when(c == 0)
+        def _():
+            rows = pl.ds(64 * half, 64)
+
+            def add(g, carry):
+                r.rs[g, rows] = (
+                    r.gp[0, g, rows].astype(F32) + r.gs[g, rows].astype(F32)).astype(BF16)
+                return carry
+
+            lax.fori_loop(0, 16, add, 0)
+            for k in (2, 1, 3):
+                copy_to(
+                    "r1", r.rs.at[pl.ds(4 * ring(a, k), 4), rows], r.r1.at[k - 1, :, rows],
+                    a_peer(k)).start()
+
+        @pl.when(c == 1)
+        def _():
+            def add(i, carry):
+                at, to = 8 * half + i, 4 * lax.rem(i, 4) + 2 * half + lax.div(i, 4)
+                r.rs[to] = (r.gp[1, at].astype(F32) + r.gs[at].astype(F32)).astype(BF16)
+                return carry
+
+            lax.fori_loop(0, 8, add, 0)
+            part = pl.ds(2 * half, 2)
+            for k in (2, 1, 3):
+                copy_to(
+                    "r1", r.rs.at[pl.ds(4 * ring(a, k) + 2 * half, 2)], r.r1.at[k - 1, part],
+                    a_peer(k)).start()
+
     for j in range(4):
         d_active = dot_nt(r.dffn[...], down_block(j))
         d_up = (d_active * r.dgl[j].astype(F32)).astype(BF16)
@@ -584,14 +616,15 @@
         @pl.when(c == 0)
         def _():
             part = pl.ds(4 * j, 4)
-            copy_to("gs", r.gp.at[1, part], r.gs.at[part], sibling).start()
+            copy_to("gs", r.gp.at[1, part], r.gs.at[part], sibling, r.gs_r.at[j // 2]).start()
 
         @pl.when(c == 1)
         def _():
             part = pl.ds(32 * j, 32)
-            copy_to("gs", r.gp.at[0, :, part], r.gs.at[:, part], sibling).start()
+            copy_to("gs", r.gp.at[0, :, part], r.gs.at[:, part], sibling, r.gs_r.at[j // 2]).start()
 
     sends_end("gs", r.gs)
+    first_sums(0)
 
     d_hidden = r.acc[...]
     unit = r.unit1[...]
@@ -618,18 +651,9 @@
     r.gv[0:2, :] = jnp.zeros((2, 256), F32)
     r.v0[...] = r.gv[...]
 
-    await_recv("gs", r.gs)
-
-    def add_cores(i, carry):
-        at = group(lax.div(i, 4), lax.rem(i, 4))
-        r.rs[i] = (r.gp[c, at].astype(F32) + r.gs[at].astype(F32)).astype(BF16)
-        return carry
-
-    lax.fori_loop(0, 16, add_cores, 0)
-
-    for k in (1, 2, 3):
+    first_sums(1)
+    for k in (2, 1, 3):
         part, to = pl.ds(4 * ring(a, k), 4), a_peer(k)
-        copy_to("r1", r.rs.at[part], r.r1.at[k - 1], to).start()
         copy_to("g1", r.gwo.at[part], r.wo1.at[k - 1], to).start()
         copy_to("v1", r.v0, r.vr1.at[k - 1], to).start()
     sends_end("r1", r.r1)
@@ -657,6 +681,32 @@
         r.ds[head % 2] = d_scores
         rows = slice(head * HD, head * HD + HD)
         r.dqt[rows, :] = dot(r.kt[rows, :], d_scores)
+        if head == 3:
+            await_recv("r1", r.r1)
+            await_recv("g1", r.wo1)
+            await_recv("v1", r.vr1)
+
+            def add_first(i, carry):
+                total = r.rs[4 * a + i].astype(F32)
+                small = r.gwo[4 * a + i].astype(F32)
+                for k in range(3):
+                    total = total + r.r1[k, i].astype(F32)
+                    small = small + r.wo1[k, i].astype(F32)
+                r.s2[i] = total.astype(BF16)
+                r.wos[i] = small.astype(BF16)
+                return carry
+
+            lax.fori_loop(0, 4, add_first, 0)
+            r.v1[...] = r.v0[...] + r.vr1[0] + r.vr1[1] + r.vr1[2]
+            for k in (1, 2, 3):
+                part, to = ring(b, k), b_peer(k)
+                copy_to("r2", r.s2.at[part], r.r2.at[k - 1], to).start()
+                copy_to("g2", r.wos.at[part], r.wo2.at[k - 1], to).start()
+                copy_to("v2", r.v1, r.vr2.at[k - 1], to).start()
+            sends_end("r2", r.r2)
+            sends_end("g2", r.wo2)
+            sends_end("v2", r.vr2)
+
         do_masked = jnp.where(head_of_lane == head, r.doo[...], zero)
         for k in range(0, 1024, 256):
             d_key = dot(r.ds[head % 2, k : k + 256, :], r.qm[head])
@@ -667,31 +717,6 @@
             else:
                 r.dk[k : k + 256, :] += d_key
                 r.dv[k : k + 256, :] += d_value
-
-    await_recv("r1", r.r1)
-    await_recv("g1", r.wo1)
-    await_recv("v1", r.vr1)
-
-    def add_first(i, carry):
-        total = r.rs[4 * a + i].astype(F32)
-        small = r.gwo[4 * a + i].astype(F32)
-        for k in range(3):
-            total = total + r.r1[k, i].astype(F32)
-            small = small + r.wo1[k, i].astype(F32)
-        r.s2[i] = total.astype(BF16)
-        r.wos[i] = small.astype(BF16)
-        return carry
-
-    lax.fori_loop(0, 4, add_first, 0)
-    r.v1[...] = r.v0[...] + r.vr1[0] + r.vr1[1] + r.vr1[2]
-    for k in (1, 2, 3):
-        part, to = ring(b, k), b_peer(k)
-        copy_to("r2", r.s2.at[part], r.r2.at[k - 1], to).start()
-        copy_to("g2", r.wos.at[part], r.wo2.at[k - 1], to).start()
-        copy_to("v2", r.v1, r.vr2.at[k - 1], to).start()
-    sends_end("r2", r.r2)
-    sends_end("g2", r.wo2)
-    sends_end("v2", r.vr2)
 
     d_queries = (r.dqt[...] * SCORE_SCALE).T.astype(BF16)
     d_keys = (r.dk[...] * SCORE_SCALE).astype(BF16)

time: 61.9 us -> 60.1 us (0.971)
  Pallas kernels: 60.9 us -> 59.1 us
    pallas_call x1, Pallas kernels: 58.9 us -> 57.1 us  [body(): pl.pallas_call(kernel, out_shape=tuple((shape(dims, kind) for dims, kind...]
where the time goes in v5:
time: 60.1 us; the launch traced here: 59.9 us
  Pallas kernels  59.1 us (98%)
  between operations  0.82 us (1%)
    pallas_call x1, Pallas kernels, body(): pl.pallas_call(kernel, out_shape=tuple((shape(dims, kind) for dims, kind...  57.1 us
    pallas_call x1, Pallas kernels, body(): pl.pallas_call(unpack, out_shape=out_shape, in_specs=[vmem] * len(packed)...  2.03 us

profile of v5, /device:TPU:1, one launch (start us, length us, event | category | flops | bytes accessed | tf_op | source)
XLA Modules:
  0.0 59.9 jit_solution(9949268719223615415)
XLA Ops:
  0.7 57.1 %encoder_layer.1 = (bf16[4,128,256]{2,1,0:T(8,128)(2,1)}, bf16[4,128,256]{2,1,0:T(8,128)(2,1)}, bf16[8,48,128]{2,1,0:T(8,128)(2,1)}, bf16[8,16,128]{2,1,0:T(8,128)(2,1)}) custom-call(bf16[4,128,256]{2,1,0:T(8,128)(2,1)} %refs_0_.1, bf16[4,128,256]{2,1,0:T(8,128)(2,1)} %refs_1_.1, s32[4]{0:T(128)} %refs_2_.1, f32[1,256]{1,0:T(1,128)} %constant.2.clone.refs_3_, ...), custom_call_target="tpu_custom_call" | custom-call | tf_op jit(solution)/shard_map/encoder_layer/pallas_call | solution.py:897
  57.7 2.0 %unpack_results.1 = (bf16[4,128,256]{2,1,0:T(8,128)(2,1)}, f32[4,128,256]{2,1,0:T(8,128)}, f32[2,768]{1,0:T(2,128)}, f32[2]{0:T(128)}, f32[2]{0:T(128)}, /*index...) custom-call(bf16[4,128,256]{2,1,0:T(8,128)(2,1)} %get-tuple-element., ...), custom_call_target="tpu_custom_call" | custom-call | tf_op jit(solution)/shard_map/unpack_results/pallas_call | solution.py:913

commit v6 on v5

--- a/solution.py
+++ b/solution.py
@@ -134,7 +134,7 @@
     "s1", "s2", "tk", "tf", "ct", "ia", "ib", "wa", "wb", "fa", "fb", "fc", "fw", "mx", "dm", "lo",
     "gs", "r1", "r2", "g1", "g2", "v1", "v2", "q1", "gt", "go", "p3", "p4",
 )
-SEMS = dict(in_s=16, own_s=4, tk_r=3, fc_r=3, gs_r=2)
+SEMS = dict(in_s=16, own_s=4, tk_r=3, fc_r=3, gs_r=2, fa_r=3, ia_r=3)
 for group_name in GROUPS:
     SEMS.setdefault(group_name + "_s", 1)
     SEMS.setdefault(group_name + "_r", 1)
@@ -286,14 +286,14 @@
     def second_part(at, core):
         return r.s1.at[at, pl.ds(pl.multiple_of(16 + 48 * core, 16), 48)]
 
-    for k in range(1, 8):
+    for k in (4, 5, 3, 2, 6, 1, 7):
         copy_to("s1", first_part(gy), first_part(gy), gy_peer(k)).start()
     sends_end("s1", r.s1.at[pl.ds(0, 7), pl.ds(0, 16)])
-    for k in range(1, 8):
+    for k in (4, 5, 3, 2, 6, 1, 7):
         part = second_part(gy, lax.rem(gy + k, 2))
         copy_to("s2", part, part, gy_peer(k)).start()
     sends_end("s2", r.s1.at[pl.ds(0, 7), pl.ds(0, 48)])
-    for k in (1, 2, 3):
+    for k in (2, 1, 3):
         copy_to("tk", r.tok.at[ring(z, k)], r.img.at[z, c], z_peer(k), r.tk_r.at[k - 1]).start()
     sends_end("tk", r.cotb.at[pl.ds(0, 3)])
     copy_to("tf", r.img.at[z, c], r.img.at[z, c], sibling).start()
@@ -325,9 +325,9 @@
     def wi_view(at):
         return r.wio.at[at, pl.ds(0, 64)]
 
-    for k in (1, 2, 3):
-        copy_to("ia", wi_view(here), wi_view(here), a_peer(k)).start()
-    for k in (1, 2, 3):
+    for k in (2, 1, 3):
+        copy_to("ia", wi_view(here), wi_view(here), a_peer(k), r.ia_r.at[k - 1]).start()
+    for k in (2, 1, 3):
         copy_to("ib", wi_view(here), wi_view(here), b_peer(k)).start()
 
     await_recv("s2", r.s1.at[pl.ds(0, 7), pl.ds(0, 48)])
@@ -358,8 +358,8 @@
                 r.ff[1, here, 16 * i : 16 * i + 16, 128 * half : 128 * half + 128] = (
                     r.s1[i, 64 + 16 * half : 80 + 16 * half, :])
 
-    for k in (1, 2, 3):
-        copy_to("fa", ff_view(here), ff_view(here), a_peer(k)).start()
+    for k in (2, 1, 3):
+        copy_to("fa", ff_view(here), ff_view(here), a_peer(k), r.fa_r.at[k - 1]).start()
 
     r.asmf[96:112, :] = jnp.zeros((16, 128), F32)
     shared_at = pl.multiple_of(16 + 80 * c, 16)
@@ -369,23 +369,23 @@
             r.asmf[pl.ds(64 + 2 * i + row, 2, stride=16), :] = piece[2 * row : 2 * row + 2]
         r.asmf[96 + i : 97 + i, :] = piece[4:5]
     r.wio[here, 64:112, :] = r.asmf[64:112, :].astype(BF16)
-    for k in (1, 2, 3):
+    for k in (2, 1, 3):
         copy_to("wa", wo_view(here), wo_view(here), a_peer(k)).start()
 
-    for k in (1, 2, 3):
+    for k in (2, 1, 3):
         at = ring(z, -k)
         await_recv("tk", r.img.at[at, c], k - 1)
         copy_to("tf", r.img.at[at, c], r.img.at[at, c], sibling).start()
     sends_end("tf", r.img.at[:, 0])
-    for k in (1, 2, 3):
+    for k in (2, 1, 3):
         copy_to("ct", r.cot.at[ring(z, k)], r.cotb.at[z], z_peer(k)).start()
     sends_end("ct", r.cotb.at[pl.ds(0, 3)])
-    await_recv("ia", r.wio.at[pl.ds(0, 3), pl.ds(0, 64)])
-    for i in (1, 2, 3):
+    for i in (1, 3, 2):
         at = group(ring(a, -i), b)
-        for k in (1, 2, 3):
+        await_recv("ia", wi_view(at), i - 1)
+        for k in (2, 1, 3):
             copy_to("ib", wi_view(at), wi_view(at), b_peer(k)).start()
-    for k in (1, 2, 3):
+    for k in (2, 1, 3):
         copy_to("fb", ff_view(here), ff_view(here), b_peer(k)).start()
     sends_end("ia", r.wio.at[pl.ds(0, 3), pl.ds(0, 64)])
     sends_end("ib", r.wio.at[pl.ds(0, 12), pl.ds(0, 64)])
@@ -402,20 +402,20 @@
     r.sht[...] = r.sh[...].T
     r.imgt[...] = image.T
 
-    await_recv("fa", r.ff.at[c, pl.ds(0, 3)])
-    for i in (1, 2, 3):
+    for i in (1, 3, 2):
         at = group(ring(a, -i), b)
-        for k in (1, 2, 3):
+        await_recv("fa", ff_view(at), i - 1)
+        for k in (2, 1, 3):
             copy_to("fc", ff_view(at), ff_view(at), b_peer(k), r.fc_r.at[k - 1]).start()
     for i in range(4):
         at = group(ring(a, -i), b)
         copy_to("fw", ff_view(at), ff_view(at), sibling).start()
-    for k in (1, 2, 3):
+    for k in (2, 1, 3):
         copy_to("wb", wo_view(here), wo_view(here), b_peer(k)).start()
     await_recv("wa", r.wio.at[pl.ds(0, 3), pl.ds(64, 48)])
     for i in (1, 2, 3):
         at = group(ring(a, -i), b)
-        for k in (1, 2, 3):
+        for k in (2, 1, 3):
             copy_to("wb", wo_view(at), wo_view(at), b_peer(k)).start()
     sends_end("fa", r.ff.at[c, pl.ds(0, 3)])
     sends_end("fb", r.ff.at[c, pl.ds(0, 3)])
@@ -469,7 +469,7 @@
         r.ri[head : head + 1, :] = inverse
         if head == 2:
             await_recv("fb", r.ff.at[c, pl.ds(0, 3)])
-            for k in (1, 2, 3):
+            for k in (2, 1, 3):
                 at = group(a, ring(b, -k))
                 copy_to("fw", ff_view(at), ff_view(at), sibling).start()
 
@@ -552,7 +552,7 @@
 
     out, unit, inverse = norm_forward(r.acc[...], vec("gain2"), vec("shift2"))
     r.lob[...] = out.astype(BF16).reshape(4, 128, 256)
-    for k in (1, 2, 3):
+    for k in (2, 1, 3):
         copy_to("lo", r.lob.at[ring(z, k)], r.lor.at[z], z_peer(k)).start()
     sends_end("lo", r.lob.at[pl.ds(0, 3)])
     own_copies = [pltpu.make_async_copy(r.lob.at[z], r.lor.at[z], r.own_s.at[0])]
@@ -698,7 +698,7 @@
 
             lax.fori_loop(0, 4, add_first, 0)
             r.v1[...] = r.v0[...] + r.vr1[0] + r.vr1[1] + r.vr1[2]
-            for k in (1, 2, 3):
+            for k in (2, 1, 3):
                 part, to = ring(b, k), b_peer(k)
                 copy_to("r2", r.s2.at[part], r.r2.at[k - 1], to).start()
                 copy_to("g2", r.wos.at[part], r.wo2.at[k - 1], to).start()
@@ -731,7 +731,7 @@
     for i in range(8):
         r.gio[8 * c + i, 48:64, :] = sums[16 * i : 16 * i + 16, :]
         r.gio[8 * (1 - c) + i, 48:64, :] = jnp.zeros((16, 128), BF16)
-    for k in range(1, 16):
+    for k in (10, 6, 14, 9, 11, 2, 8, 5, 7, 13, 15, 1, 3, 4, 12):
         copy_to("q1", r.gio.at[ring(gx, k, 16)], r.q1.at[gx], gx_peer(k)).start()
     sends_end("q1", r.q1.at[pl.ds(0, 15)])
 
@@ -747,7 +747,7 @@
         + r.gt[:, c].reshape(512, 256).astype(F32)
         + r.gtr[...].reshape(512, 256).astype(F32))
     r.gob[...] = full.astype(BF16).reshape(4, 128, 256)
-    for k in (1, 2, 3):
+    for k in (2, 1, 3):
         copy_to("go", r.gob.at[ring(z, k)], r.gor.at[z], z_peer(k)).start()
     sends_end("go", r.gob.at[pl.ds(0, 3)])
 
@@ -792,7 +792,7 @@
         r.p3f[i, 34:40, :] = own_lanes[2:8]
         r.p3f[i, 42:43, :] = up_sums
     r.p3[...] = r.p3f[...].astype(BF16)
-    for k in range(1, 8):
+    for k in (4, 5, 3, 2, 6, 1, 7):
         copy_to("p3", r.p3.at[ring(gy, k, 8)], r.r3.at[gy], gy_peer(k)).start()
     sends_end("p3", r.p3.at[pl.ds(0, 7)])
 
@@ -807,7 +807,7 @@
             at = 8 * row
             r.p4f[i, at : at + 4, :] = r.fio[pl.ds(2 * i + row, 4, stride=16), :]
     r.p4[...] = r.p4f[...].astype(BF16)
-    for k in range(1, 8):
+    for k in (4, 5, 3, 2, 6, 1, 7):
         copy_to("p4", r.p4.at[ring(gy, k, 8)], r.r4.at[gy], gy_peer(k)).start()
     sends_end("p4", r.p4.at[pl.ds(0, 7)])
 

time: 60.1 us -> 59.5 us (0.990)
  no operation moved by 1% of the time
where the time goes in v6:
time: 59.5 us; the launch traced here: 59.3 us
  Pallas kernels  58.5 us (98%)
  between operations  0.82 us (1%)
    pallas_call x1, Pallas kernels, body(): pl.pallas_call(kernel, out_shape=tuple((shape(dims, kind) for dims, kind...  56.5 us
    pallas_call x1, Pallas kernels, body(): pl.pallas_call(unpack, out_shape=out_shape, in_specs=[vmem] * len(packed)...  2.03 us

profile of v6, /device:TPU:1, one launch (start us, length us, event | category | flops | bytes accessed | tf_op | source)
XLA Modules:
  0.0 59.3 jit_solution(16738847367896084536)
XLA Ops:
  0.7 56.5 %encoder_layer.1 = (bf16[4,128,256]{2,1,0:T(8,128)(2,1)}, bf16[4,128,256]{2,1,0:T(8,128)(2,1)}, bf16[8,48,128]{2,1,0:T(8,128)(2,1)}, bf16[8,16,128]{2,1,0:T(8,128)(2,1)}) custom-call(bf16[4,128,256]{2,1,0:T(8,128)(2,1)} %refs_0_.1, bf16[4,128,256]{2,1,0:T(8,128)(2,1)} %refs_1_.1, s32[4]{0:T(128)} %refs_2_.1, f32[1,256]{1,0:T(1,128)} %constant.2.clone.refs_3_, ...), custom_call_target="tpu_custom_call" | custom-call | tf_op jit(solution)/shard_map/encoder_layer/pallas_call | solution.py:897
  57.2 2.0 %unpack_results.1 = (bf16[4,128,256]{2,1,0:T(8,128)(2,1)}, f32[4,128,256]{2,1,0:T(8,128)}, f32[2,768]{1,0:T(2,128)}, f32[2]{0:T(128)}, f32[2]{0:T(128)}, /*index...) custom-call(bf16[4,128,256]{2,1,0:T(8,128)(2,1)} %get-tuple-element., ...), custom_call_target="tpu_custom_call" | custom-call | tf_op jit(solution)/shard_map/unpack_results/pallas_call | solution.py:913

commit v7 on v6

--- a/solution.py
+++ b/solution.py
@@ -60,7 +60,7 @@
 SCRATCH = dict(
     pf=((112, 128), F32),
     s1=((8, 112, 128), BF16),
-    asmf=((384, 128), F32),
+    asmf=((400, 128), F32),
     img=((4, 2, 128, 256), BF16),
     cotb=((4, 128, 256), BF16),
     wio=((16, 112, 128), BF16),
@@ -98,7 +98,7 @@
     r1=((3, 4, 128, 256), BF16),
     s2=((4, 128, 256), BF16),
     r2=((3, 128, 256), BF16),
-    fin=((2, 128, 128), F32),
+    fin=((2, 144, 128), F32),
     gv=((16, 256), F32),
     dfirst=((512, 256), F32),
     dms=((4, 128, 128), BF16),
@@ -113,10 +113,10 @@
     wo1=((3, 4, 32, 128), BF16),
     wos=((4, 32, 128), BF16),
     wo2=((3, 32, 128), BF16),
-    fwo=((32, 128), F32),
+    fwo=((144, 128), F32),
     gio=((16, 64, 128), BF16),
     q1=((16, 64, 128), BF16),
-    fio=((64, 128), F32),
+    fio=((144, 128), F32),
     v0=((16, 256), F32),
     vr1=((3, 16, 256), F32),
     v1=((16, 256), F32),
@@ -759,9 +759,9 @@
     for k in range(3):
         total = total + r.r2[k].astype(F32)
         small = small + r.wo2[k].astype(F32)
-    r.fin[0] = total[:, 0:128]
-    r.fin[1] = total[:, 128:256]
-    r.fwo[...] = small
+    r.fin[0, 0:128, :] = total[:, 0:128]
+    r.fin[1, 0:128, :] = total[:, 128:256]
+    r.fwo[0:32, :] = small
     r.p3f[...] = jnp.zeros((8, 48, 128), F32)
 
     @pl.when(c == 0)
@@ -800,7 +800,7 @@
     total = r.gio[gx].astype(F32)
     for k in range(1, 16):
         total = total + r.q1[ring(gx, -k, 16)].astype(F32)
-    r.fio[...] = total
+    r.fio[0:64, :] = total
     r.p4f[...] = jnp.zeros((8, 16, 128), F32)
     for i in range(8):
         for row in range(2):

time: 59.5 us -> 59.5 us (level)
  no operation moved by 1% of the time
where the time goes in v7:
time: 59.5 us; the launch traced here: 59.4 us
  Pallas kernels  58.5 us (98%)
  between operations  0.82 us (1%)
    pallas_call x1, Pallas kernels, body(): pl.pallas_call(kernel, out_shape=tuple((shape(dims, kind) for dims, kind...  56.5 us
    pallas_call x1, Pallas kernels, body(): pl.pallas_call(unpack, out_shape=out_shape, in_specs=[vmem] * len(packed)...  2.03 us

profile of v7, /device:TPU:1, one launch (start us, length us, event | category | flops | bytes accessed | tf_op | source)
XLA Modules:
  0.0 59.4 jit_solution(8912770302480729779)
XLA Ops:
  0.7 56.5 %encoder_layer.1 = (bf16[4,128,256]{2,1,0:T(8,128)(2,1)}, bf16[4,128,256]{2,1,0:T(8,128)(2,1)}, bf16[8,48,128]{2,1,0:T(8,128)(2,1)}, bf16[8,16,128]{2,1,0:T(8,128)(2,1)}) custom-call(bf16[4,128,256]{2,1,0:T(8,128)(2,1)} %refs_0_.1, bf16[4,128,256]{2,1,0:T(8,128)(2,1)} %refs_1_.1, s32[4]{0:T(128)} %refs_2_.1, f32[1,256]{1,0:T(1,128)} %constant.2.clone.refs_3_, ...), custom_call_target="tpu_custom_call" | custom-call | tf_op jit(solution)/shard_map/encoder_layer/pallas_call | solution.py:897
  57.2 2.0 %unpack_results.1 = (bf16[4,128,256]{2,1,0:T(8,128)(2,1)}, f32[4,128,256]{2,1,0:T(8,128)}, f32[2,768]{1,0:T(2,128)}, f32[2]{0:T(128)}, f32[2]{0:T(128)}, /*index...) custom-call(bf16[4,128,256]{2,1,0:T(8,128)(2,1)} %get-tuple-element., ...), custom_call_target="tpu_custom_call" | custom-call | tf_op jit(solution)/shard_map/unpack_results/pallas_call | solution.py:913
